TPU v7x, 32 devices: a whole 2x2x4 slice. The times are simulated.
32 devices in a mesh: head: 4 (over z), ctx: 8 (over y, x, core).
Axes of the slice: x: 2, y: 2, z: 4, core: 2. Of those that a mesh axis runs over, the one named last changes fastest.
Arguments:
- inputs: bfloat16 [2048, 4096], P('ctx'), may hold values from -8 to 8
- out_grad: bfloat16 [2048, 4096], P('ctx', 'head'), may hold values from -6 to 6
- w_query: bfloat16 [4096, 4096], P(None, 'head'), may hold values from -4 to 4
- w_key: bfloat16 [4096, 1024], P(None, 'head'), may hold values from -4 to 4
- value_projection: bfloat16 [4096, 1024], P(None, 'head'), may hold values from -0.09375 to 0.09375
- w_out: bfloat16 [4096, 4096], P('head'), may hold values from -0.09375 to 0.09375
- doc_lengths: int32 [8], replicated, may hold values from 1 to 1024, 2048 in all
- span_order: int32 [16], replicated, may hold values from 0 to 15, as said below
Outputs:
- input_grad: bfloat16 [2048, 4096], P('ctx', 'head')
Inputs may be any that keep to these rules, and one draw needn't show every extreme that they name: `span_order`: A permutation of 0 to 15; entries 2 d and 2 d + 1 are c and 15 - c for some c, in either order.
All inputs are finite; a program needn't handle non-finite values.
Results may differ from a plain program's by a relative error of at most 0.012.
The roundings to bfloat16 on the way count: a program that leaves them out, or rounds other values in their place, can miss the bound.
Values may be sent and summed in bfloat16 or wider, within the bound.
No kernel may reach another device: no remote copies, remote signals or barrier semaphores. Data moves between devices by JAX's collectives and lax.ppermute only.
A program may use at most 64 MiB of HBM per device.

v0:
```python
import functools
import math

import jax
import jax.numpy as jnp
from jax import lax
from jax.experimental import pallas as pl
from jax.experimental.pallas import tpu as pltpu
from jax.sharding import PartitionSpec as P

ASKER_NUM = 32
SHARED_KV_NUM = 8
CHANNEL_DIM = 128

masked_score = -1e30
MIB = 1 << 20
COST = 0
AT_ONCE = 4
VMEM = pltpu.VMEM
HBM = pltpu.HBM


def mm(a, b):
    return lax.dot_general(a, b, (((1,), (0,)), ((), ())), preferred_element_type=jnp.float32)


def mm_nt(a, b):
    return lax.dot_general(a, b, (((1,), (1,)), ((), ())), preferred_element_type=jnp.float32)


def mm_tn(a, b):
    return lax.dot_general(a, b, (((0,), (0,)), ((), ())), preferred_element_type=jnp.float32)


def params():
    return pltpu.CompilerParams(vmem_limit_bytes=24 * MIB)


def cost(micros):
    return pl.CostEstimate(flops=int(micros * COST), bytes_accessed=1, transcendentals=0)


def upper_half(order):
    first = order[2 * lax.axis_index("ctx")]
    return jnp.where(2 * first >= order.shape[0], 0, 1)


def in_hbm(x):
    return pltpu.with_memory_space_constraint(x, HBM)


def fetch(src, dst, sem):
    copy = pltpu.make_async_copy(src, dst, sem)
    copy.start()
    return copy


def kv_body(parts, x_ref, wk_ref, wv_ref, out_ref, x, wk, wv, acc, sems):
    width = wk.shape[1]
    depth = wk.shape[0] // parts
    copies = []
    for i in range(parts):
        rows = slice(i * depth, (i + 1) * depth)
        copies.append(
            [
                fetch(x_ref.at[:, rows], x.at[:, rows], sems.at[i, 0]),
                fetch(wk_ref.at[rows], wk.at[rows], sems.at[i, 1]),
                fetch(wv_ref.at[rows], wv.at[rows], sems.at[i, 2]),
            ]
        )
    for i in range(parts):
        rows = slice(i * depth, (i + 1) * depth)
        for copy in copies[i]:
            copy.wait()
        left = x[:, rows]
        terms = mm(left, wk[rows, :]), mm(left, wv[rows, :])
        for j, term in enumerate(terms):
            columns = slice(j * width, (j + 1) * width)
            total = term if i == 0 else acc[:, columns] + term
            if i < parts - 1:
                acc[:, columns] = total
            else:
                out_ref[:, columns] = total.astype(out_ref.dtype)


def project_kv(x, wk, wv):
    tokens, depth = x.shape
    width = wk.shape[1]
    parts = 4
    return pl.pallas_call(
        functools.partial(kv_body, parts),
        in_specs=[pl.BlockSpec(memory_space=HBM)] * 3,
        out_specs=pl.BlockSpec(memory_space=VMEM),
        out_shape=jax.ShapeDtypeStruct((tokens, 2 * width), jnp.bfloat16),
        scratch_shapes=[
            VMEM(x.shape, x.dtype),
            VMEM(wk.shape, wk.dtype),
            VMEM(wv.shape, wv.dtype),
            VMEM((tokens, 2 * width), jnp.float32),
            pltpu.SemaphoreType.DMA((parts, 3)),
        ],
        compiler_params=params(),
        cost_estimate=cost(3.4),
        name="project_kv",
    )(in_hbm(x), in_hbm(wk), in_hbm(wv))


def project_body(parts, x_ref, w_ref, out_ref, x, w, acc, sems):
    depth = w.shape[0] // parts
    copies = []
    for i in range(parts):
        rows = slice(i * depth, (i + 1) * depth)
        copies.append(
            [
                fetch(x_ref.at[:, rows], x.at[:, rows], sems.at[i, 0]),
                fetch(w_ref.at[rows], w.at[rows], sems.at[i, 1]),
            ]
        )
    for i in range(parts):
        rows = slice(i * depth, (i + 1) * depth)
        for copy in copies[i]:
            copy.wait()
        total = mm(x[:, rows], w[rows, :])
        if i:
            total = acc[...] + total
        if i < parts - 1:
            acc[...] = total
        else:
            out_ref[...] = total.astype(out_ref.dtype)


def project(x, w):
    tokens, depth = x.shape
    width = w.shape[1]
    parts = 4
    return pl.pallas_call(
        functools.partial(project_body, parts),
        in_specs=[pl.BlockSpec(memory_space=HBM)] * 2,
        out_specs=pl.BlockSpec(memory_space=VMEM),
        out_shape=jax.ShapeDtypeStruct((tokens, width), jnp.bfloat16),
        scratch_shapes=[
            VMEM(x.shape, x.dtype),
            VMEM(w.shape, w.dtype),
            VMEM((tokens, width), jnp.float32),
            pltpu.SemaphoreType.DMA((parts, 2)),
        ],
        compiler_params=params(),
        cost_estimate=cost(4.9),
        name="project",
    )(in_hbm(x), in_hbm(w))


def back_body(places, given, rows, *refs):
    refs = list(refs)
    sems, w = refs.pop(), refs.pop()
    out_ref, w_ref = refs.pop(), refs.pop()
    me = lax.axis_index("head")
    depth = w.shape[2]
    copies = [
        fetch(w_ref.at[:, pl.ds(pl.multiple_of((me ^ k) * depth, depth), depth)], w.at[i], sems.at[i])
        for i, k in enumerate(places)
    ]
    total = refs.pop(0)[...] if given else None
    for i, copy in enumerate(copies):
        x = refs.pop(0)[...]
        if x.shape[0] < rows:
            x = jnp.concatenate([x, refs.pop(0)[...]], axis=0)
        copy.wait()
        term = mm_nt(x, w[i])
        total = term if total is None else total + term
    out_ref[...] = total.astype(out_ref.dtype)


def back_project(blocks, places, w, total, dtype):
    rows, depth = blocks[0][0].shape[0] * len(blocks[0]), blocks[0][0].shape[1]
    given = [] if total is None else [total]
    flat = [x for block in blocks for x in block]
    return pl.pallas_call(
        functools.partial(back_body, places, len(given), rows),
        in_specs=[pl.BlockSpec(memory_space=VMEM)] * (len(given) + len(flat))
        + [pl.BlockSpec(memory_space=HBM)],
        out_specs=pl.BlockSpec(memory_space=VMEM),
        out_shape=jax.ShapeDtypeStruct((rows, w.shape[0]), dtype),
        scratch_shapes=[
            VMEM((len(places), w.shape[0], depth), w.dtype),
            pltpu.SemaphoreType.DMA((len(places),)),
        ],
        compiler_params=params(),
        cost_estimate=cost(3.4),
        name="context_grad",
    )(*given, *flat, in_hbm(w))


def query_terms_body(places, upper_ref, lower_ref, w_ref, upper_out, lower_out, w, sems):
    me = lax.axis_index("head")
    share = w.shape[1]
    copies = [
        fetch(w_ref.at[pl.ds(pl.multiple_of((me ^ k) * share, share), share)], w.at[i], sems.at[i])
        for i, k in enumerate(places)
    ]
    half = upper_ref.shape[0]
    x = jnp.concatenate([upper_ref[...], lower_ref[...]], axis=0)
    for i, copy in enumerate(copies):
        copy.wait()
        total = mm_nt(x, w[i])
        upper_out[i] = total[:half]
        lower_out[i] = total[half:]


def query_terms(upper, lower, w, heads, places):
    rows, depth = upper.shape
    share = w.shape[0] // heads
    size = len(places)
    return pl.pallas_call(
        functools.partial(query_terms_body, places),
        in_specs=[pl.BlockSpec(memory_space=VMEM)] * 2 + [pl.BlockSpec(memory_space=HBM)],
        out_specs=[pl.BlockSpec(memory_space=VMEM)] * 2,
        out_shape=[jax.ShapeDtypeStruct((size, rows, share), jnp.float32)] * 2,
        scratch_shapes=[
            VMEM((size, share, depth), w.dtype),
            pltpu.SemaphoreType.DMA((size,)),
        ],
        compiler_params=params(),
        cost_estimate=cost(4.6),
        name="query_terms",
    )(upper, lower, in_hbm(w))


def all_terms_body(places, count, first_ref, *refs):
    terms, (wk_ref, wv_ref), refs = refs[:count], refs[count : count + 2], refs[count + 2 :]
    outs, (wk, wv, sems) = refs[:-3], refs[-3:]
    me = lax.axis_index("head")
    size, share, width = wk.shape
    copies = {}
    for i, k in enumerate(places):
        rows = pl.ds(pl.multiple_of((me ^ k) * share, share), share)
        copies[i] = [
            fetch(wk_ref.at[rows], wk.at[i], sems.at[i, 0]),
            fetch(wv_ref.at[rows], wv.at[i], sems.at[i, 1]),
        ]
    grads = terms[0][...].astype(jnp.float32)
    for term in terms[1:]:
        grads = grads + term[...].astype(jnp.float32)
    grads = grads.astype(jnp.bfloat16)
    for i, pair in copies.items():
        for copy in pair:
            copy.wait()
        total = first_ref[i] + mm_nt(grads[:, :width], wk[i])
        total = total + mm_nt(grads[:, width:], wv[i])
        if len(outs) == 1:
            outs[0][i] = total.astype(outs[0].dtype)
        else:
            outs[i][...] = total.astype(outs[i].dtype)


def all_terms(first, terms, wk, wv, places, stacked):
    size, rows, share = first.shape
    width = wk.shape[1]
    return pl.pallas_call(
        functools.partial(all_terms_body, places, len(terms)),
        in_specs=[pl.BlockSpec(memory_space=VMEM)] * (1 + len(terms))
        + [pl.BlockSpec(memory_space=HBM)] * 2,
        out_specs=[pl.BlockSpec(memory_space=VMEM)] * (1 if stacked else size),
        out_shape=[jax.ShapeDtypeStruct((size, rows, share), jnp.bfloat16)]
        if stacked
        else [jax.ShapeDtypeStruct((rows, share), jnp.bfloat16)] * size,
        scratch_shapes=[
            VMEM((size, share, width), wk.dtype),
            VMEM((size, share, width), wv.dtype),
            pltpu.SemaphoreType.DMA((size, 2)),
        ],
        compiler_params=params(),
        cost_estimate=cost(3.2),
        name="all_terms",
    )(first, *terms, in_hbm(wk), in_hbm(wv))


def part_of(ref, at):
    return (ref[...] if at is None else ref[at]).astype(jnp.float32)


def add_body(at, a_ref, b_ref, out_ref):
    out_ref[...] = (a_ref[...].astype(jnp.float32) + part_of(b_ref, at)).astype(out_ref.dtype)


def add(a, b, at):
    return pl.pallas_call(
        functools.partial(add_body, at),
        in_specs=[pl.BlockSpec(memory_space=VMEM)] * 2,
        out_specs=pl.BlockSpec(memory_space=VMEM),
        out_shape=jax.ShapeDtypeStruct(a.shape, a.dtype),
        compiler_params=params(),
        cost_estimate=cost(0.5),
        name="add",
    )(a, b)


def join_body(ats, order, *refs):
    refs, out_ref = list(refs[:-1]), refs[-1]
    half = out_ref.shape[0] // 2
    at = upper_half(order) * half
    for j, place in enumerate((at, half - at)):
        total = None
        for i in ats[j]:
            term = part_of(refs.pop(0), i)
            total = term if total is None else total + term
        out_ref[pl.ds(pl.multiple_of(place, half), half), :] = total.astype(out_ref.dtype)


def join_rows(upper, lower, span_order):
    rows, width = upper[0][0].shape
    ats = [[at for _, at in terms] for terms in (upper, lower)]
    blocks = [block for block, _ in upper + lower]
    return pl.pallas_call(
        functools.partial(join_body, ats),
        in_specs=[pl.BlockSpec(memory_space=pltpu.SMEM)]
        + [pl.BlockSpec(memory_space=VMEM)] * len(blocks),
        out_specs=pl.BlockSpec(memory_space=VMEM),
        out_shape=jax.ShapeDtypeStruct((2 * rows, width), jnp.bfloat16),
        compiler_params=params(),
        cost_estimate=cost(1.5),
        name="join_rows",
    )(span_order, *blocks)


def find_places(order, places, me, spans):
    for i in range(spans):
        k = (i // 2) ^ me
        places[order[i]] = (k % 2) * (spans // 2) + (k // 2) * 2 + (i % 2)


def own_span(order, lengths, docs, me, j, half):
    span = order[2 * me + j]
    position = span * half + lax.broadcasted_iota(jnp.int32, (1, half), 1)
    first, end = 0, 0
    start = jnp.zeros((1, half), jnp.int32)
    for k in range(docs):
        end = end + lengths[k]
        start = jnp.where(position >= end, end, start)
        first = jnp.where(span * half >= end, end, first)
    return span, position, start, first // half


def stack_heads(ref, rows, group, share, dim):
    base = group * share
    return jnp.concatenate(
        [ref[rows, (base + h) * dim : (base + h + 1) * dim] for h in range(share)], axis=0
    )


def load_blocks(refs, held):
    rows = refs[0].shape[0]
    for k, ref in enumerate(refs):
        held[k * rows : (k + 1) * rows, :] = ref[...]


def span_group(i, span, held, places, half):
    numbers = [span - AT_ONCE * i - j for j in range(AT_ONCE - 1, -1, -1)]
    known = [jnp.maximum(p, 0) for p in numbers]
    at = [pl.multiple_of(places[p] * half, half) for p in known]
    block = jnp.concatenate([held[pl.ds(place, half), :] for place in at], axis=0)
    key = numbers[0] * half + lax.broadcasted_iota(jnp.int32, (AT_ONCE * half, 1), 0)
    return known, block, key


def keep(allowed, x, other):
    width = allowed.shape[1]
    return jnp.concatenate(
        [
            jnp.where(allowed, x[:, i : i + width], other)
            for i in range(0, x.shape[1], width)
        ],
        axis=1,
    )


def stats_body(sizes, upper, order, lengths, q_ref, *refs):
    peers, half, groups, share, dim, docs = sizes
    blocks = refs[:peers]
    level_ref, mixed_ref, held, kept, places = refs[peers:]
    me = lax.axis_index("ctx")
    width = groups * dim
    factor = math.log2(math.e) / math.sqrt(dim)
    find_places(order, places, me, 2 * peers)
    load_blocks(blocks, held)
    columns = share * half
    at = upper_half(order)
    j = at if upper else 1 - at
    span, position, start, lowest = own_span(order, lengths, docs, me, j, half)
    rows = pl.ds(pl.multiple_of(j * half, half), half)
    queries = [stack_heads(q_ref, rows, g, share, dim) for g in range(groups)]

    deep = AT_ONCE * half
    steps = (span - lowest) // AT_ONCE + 1

    def score(i, carry):
        known, block, key = span_group(i, span, held, places, half)
        allowed = (key <= position) & (key >= start)
        fresh = []
        for g in range(groups):
            logits = keep(allowed, mm_nt(block[:, g * dim : (g + 1) * dim], queries[g]), masked_score)
            kept[g, pl.ds(pl.multiple_of(i * deep, deep), deep), :] = logits
            high = jnp.max(logits.reshape(deep // 8, 8, columns), axis=0)
            fresh.append(jnp.maximum(carry[g], high))
        return tuple(fresh)

    empty = jnp.full((8, columns), masked_score, jnp.float32)
    tops = lax.fori_loop(0, steps, score, (empty,) * groups)
    tops = [jnp.max(top, axis=0, keepdims=True) for top in tops]

    def mix(i, carry):
        known, block, key = span_group(i, span, held, places, half)
        fresh = []
        for g in range(groups):
            total, mixed = carry[g]
            values = block[:, width + g * dim : width + (g + 1) * dim]
            logits = kept[g, pl.ds(pl.multiple_of(i * deep, deep), deep), :]
            weights = jnp.exp2((logits - tops[g]) * factor)
            total = total + jnp.sum(weights.reshape(deep // 8, 8, columns), axis=0)
            mixed = mixed + mm_tn(values, weights.astype(jnp.bfloat16))
            fresh.append((total, mixed))
        return tuple(fresh)

    empty = (jnp.zeros((8, columns), jnp.float32), jnp.zeros((dim, columns), jnp.float32))
    done = lax.fori_loop(0, steps, mix, (empty,) * groups)
    for g in range(groups):
        top, (total, mixed) = tops[g], done[g]
        total = jnp.sum(total, axis=0, keepdims=True)
        level_ref[g] = top * factor + jnp.log2(total)
        mixed_ref[g] = mixed / total


def stats(upper, q, *args):
    *blocks, span_order, doc_lengths, sizes = args
    peers, half, groups, share, dim, docs = sizes
    columns = share * half
    return pl.pallas_call(
        functools.partial(stats_body, sizes, upper),
        in_specs=[pl.BlockSpec(memory_space=pltpu.SMEM)] * 2
        + [pl.BlockSpec(memory_space=VMEM)] * (1 + peers),
        out_specs=[pl.BlockSpec(memory_space=VMEM)] * 2,
        out_shape=[
            jax.ShapeDtypeStruct((groups, 1, columns), jnp.float32),
            jax.ShapeDtypeStruct((groups, dim, columns), jnp.float32),
        ],
        scratch_shapes=[
            VMEM((2 * peers * half, 2 * groups * dim), jnp.bfloat16),
            VMEM((groups, (2 * peers + AT_ONCE) * half, columns), jnp.float32),
            pltpu.SMEM((2 * peers,), jnp.int32),
        ],
        compiler_params=params(),
        cost_estimate=cost(2.4),
        name="upper_stats" if upper else "lower_stats",
    )(span_order, doc_lengths, q, *blocks)


def grads_body(sizes, upper, order, lengths, q_ref, g_ref, level_ref, mixed_ref, *refs):
    peers, half, groups, share, dim, docs = sizes
    spans = 2 * peers
    if upper:
        blocks = refs[:peers]
        dq_ref, even_ref, *odd_refs, rest_ref, held, sums, places = refs[peers:]
    else:
        rest_ref, blocks = refs[0], refs[1 : 1 + peers]
        dq_ref, even_ref, *odd_refs, held, sums, places = refs[1 + peers :]
    me = lax.axis_index("ctx")
    width = groups * dim
    scale = 1.0 / math.sqrt(dim)
    factor = math.log2(math.e) * scale
    find_places(order, places, me, spans)
    load_blocks(blocks, held)
    columns = share * half
    at = upper_half(order)
    j = at if upper else 1 - at
    span, position, start, lowest = own_span(order, lengths, docs, me, j, half)
    if upper:
        sums[...] = jnp.zeros_like(sums)
    else:
        sums[...] = rest_ref[...]
    rows = pl.ds(pl.multiple_of(j * half, half), half)
    queries = [stack_heads(q_ref, rows, g, share, dim) for g in range(groups)]
    outs = [stack_heads(g_ref, rows, g, share, dim) for g in range(groups)]
    levels = [level_ref[g] for g in range(groups)]
    deltas = []
    for g in range(groups):
        turned = jnp.concatenate(
            [outs[g][h * half : (h + 1) * half].astype(jnp.float32).T for h in range(share)],
            axis=1,
        )
        deltas.append(jnp.sum(turned * mixed_ref[g], axis=0, keepdims=True))

    def visit(i, carry):
        known, block, key = span_group(i, span, held, places, half)
        allowed = (key <= position) & (key >= start)
        targets = [pl.ds(pl.multiple_of(p * half, half), half) for p in known]
        fresh = []
        for g in range(groups):
            keys = block[:, g * dim : (g + 1) * dim]
            values = block[:, width + g * dim : width + (g + 1) * dim]
            logits = mm_nt(keys, queries[g]) * factor
            chance = keep(allowed, jnp.exp2(logits - levels[g]), 0.0)
            slopes = mm_nt(values, outs[g])
            score = (chance * (slopes - deltas[g])).astype(jnp.bfloat16)
            key_term = mm(score, queries[g])
            value_term = mm(chance.astype(jnp.bfloat16), outs[g])
            for j, target in enumerate(targets):
                part = slice(j * half, (j + 1) * half)
                sums[target, g * dim : (g + 1) * dim] += key_term[part]
                sums[target, width + g * dim : width + (g + 1) * dim] += value_term[part]
            fresh.append(carry[g] + mm_tn(keys, score))
        return tuple(fresh)

    empty = jnp.zeros((dim, columns), jnp.float32)
    done = lax.fori_loop(0, (span - lowest) // AT_ONCE + 1, visit, (empty,) * groups)
    for g in range(groups):
        for h in range(share):
            head = g * share + h
            dq_ref[:, head * dim : (head + 1) * dim] = (
                (done[g][:, h * half : (h + 1) * half].T * scale).astype(dq_ref.dtype)
            )
    for k in range(peers):
        out, slot = even_ref, k // 2
        if k % 2:
            out, slot = odd_refs[slot // odd_refs[0].shape[0]], slot % odd_refs[0].shape[0]
        first = order[2 * (me ^ k)]
        other = spans - 1 - first
        pick = jnp.maximum(first, other) if upper else jnp.minimum(first, other)
        part = pl.ds(pl.multiple_of(pick * half, half), half)
        out[slot, :, :width] = (sums[part, :width] * scale).astype(out.dtype)
        out[slot, :, width:] = sums[part, width:].astype(out.dtype)
    if upper:
        rest_ref[...] = sums[: peers * half, :]


def grads(upper, q, g, level, mixed, *args):
    *blocks, span_order, doc_lengths, sizes = args
    peers, half, groups, share, dim, docs = sizes
    tokens, width = 2 * half, groups * dim
    columns = share * half
    terms = jax.ShapeDtypeStruct((peers // 2, half, 2 * width), jnp.bfloat16)
    odds = jax.ShapeDtypeStruct((peers // 4, half, 2 * width), jnp.bfloat16)
    rests = jax.ShapeDtypeStruct((peers * half, 2 * width), jnp.float32)
    outs = [jax.ShapeDtypeStruct((half, g.shape[1]), jnp.bfloat16), terms, odds, odds] + [rests] * upper
    return pl.pallas_call(
        functools.partial(grads_body, sizes, upper),
        in_specs=[pl.BlockSpec(memory_space=pltpu.SMEM)] * 2
        + [pl.BlockSpec(memory_space=VMEM)] * (4 + len(blocks)),
        out_specs=[pl.BlockSpec(memory_space=VMEM)] * len(outs),
        out_shape=outs,
        scratch_shapes=[
            VMEM((peers * tokens, 2 * width), jnp.bfloat16),
            VMEM(((2 if upper else 1) * peers * half, 2 * width), jnp.float32),
            pltpu.SMEM((2 * peers,), jnp.int32),
        ],
        compiler_params=params(),
        cost_estimate=cost(3.0),
        name="upper_grads" if upper else "lower_grads",
    )(span_order, doc_lengths, q, g, level, mixed, *blocks)


def swap(x, k, axis):
    return lax.ppermute(x, axis, [(i, i ^ k) for i in range(lax.axis_size(axis))])


def gather_even(x, axis, held):
    size = lax.axis_size(axis)
    got, bit = {0: x}, 2
    while bit < size:
        passed = {k: block for k, block in got.items() if k}
        passed, held = lax.optimization_barrier((passed, held))
        got |= {bit: swap(x, bit, axis)}
        got |= {k ^ bit: swap(block, bit, axis) for k, block in passed.items()}
        bit *= 2
    return [got[k] for k in sorted(got)], held


def pair_body(even_ref, *refs):
    count = even_ref.shape[0]
    odd_refs, outs = refs[:-count], refs[-count:]
    part = odd_refs[0].shape[0]
    for k, out in enumerate(outs):
        total = even_ref[k].astype(jnp.float32) + odd_refs[k // part][k % part].astype(jnp.float32)
        out[...] = total.astype(out.dtype)


def pair_sums(even, *got):
    count, rows, width = even.shape
    return pl.pallas_call(
        pair_body,
        in_specs=[pl.BlockSpec(memory_space=VMEM)] * (1 + len(got)),
        out_specs=[pl.BlockSpec(memory_space=VMEM)] * count,
        out_shape=[jax.ShapeDtypeStruct((rows, width), jnp.bfloat16)] * count,
        compiler_params=params(),
        cost_estimate=cost(0.7),
        name="pair_sums",
    )(even, *got)


def scatter_ctx(pairs):
    return [part if k == 0 else swap(part, 2 * k, "ctx") for k, part in enumerate(pairs)]


def shards(inputs, out_grad, w_query, w_key, value_projection, w_out, doc_lengths, span_order):
    tokens = inputs.shape[0]
    share = ASKER_NUM // SHARED_KV_NUM
    half = tokens // 2
    sizes = (
        lax.axis_size("ctx"),
        tokens // 2,
        w_key.shape[1] // CHANNEL_DIM,
        share,
        CHANNEL_DIM,
        doc_lengths.shape[0],
    )
    heads = lax.axis_size("head")
    last = [span_order]

    def turn(call, *args):
        held, *args = lax.optimization_barrier((last[0], *args))
        out = call(*args)
        last[0] = out if hasattr(out, "shape") else out[0]
        return out

    def attend(upper, call, *args):
        return turn(lambda *a: call(upper, *a, span_order, doc_lengths, sizes), *args)

    def context(blocks, places, total, dtype):
        shape = jax.tree.structure((blocks, total))

        def call(*flat):
            parts, given = jax.tree.unflatten(shape, flat)
            return back_project(parts, places, w_out, given, dtype)

        return turn(call, *jax.tree.leaves((blocks, total)))

    def send_first(parts, stack):
        places = range(heads - 1, 0, -2)
        if stack is None:
            return {k ^ 1: (swap(parts[k], 1, "head"), None) for k in places}
        got = swap(stack, 1, "head")
        return {k ^ 1: (got, i) for i, k in enumerate(places)}

    def send_rest(parts, got):
        ends, bit = [(parts[0], None), got[0]], 2
        parts = {
            k: turn(lambda a, b, at=got[k][1]: add(a, b, at), parts[k], got[k][0])
            for k in range(2, heads, 2)
        }
        while bit < heads:
            moved = {k ^ bit: swap(parts[k], bit, "head") for k in parts if k & bit}
            ends.append((moved.pop(0), None))
            parts = {k: turn(lambda a, b: add(a, b, None), parts[k], moved[k]) for k in moved}
            bit *= 2
        return ends

    far = [{0: out_grad[:half]}, {0: out_grad[half:]}]
    bit = heads // 2
    while bit > 1:
        far = [got | {k ^ bit: swap(x, bit, "head") for k, x in got.items()} for got in far]
        bit //= 2
    near = swap(out_grad, 1, "head")
    own = turn(project_kv, inputs, w_key, value_projection)
    near_blocks, far[0] = gather_even(own, "ctx", far[0])
    query = turn(project, inputs, w_query)
    query, near_blocks = lax.optimization_barrier((query, near_blocks))
    blocks = (*near_blocks, *[swap(block, 1, "ctx") for block in near_blocks])
    query, far[1], near = lax.optimization_barrier((query, far[1], near))
    upper_stats = attend(True, stats, query, *blocks)
    lower_stats = attend(False, stats, query, *blocks)
    passed = [{k ^ 1: swap(x, 1, "head") for k, x in got.items() if k} for got in far]
    firsts = {0: (out_grad,), 1: (near,)}
    firsts |= {k: (far[0][k], far[1][k]) for k in range(2, heads, 2)}
    lasts = {k: (passed[0][k], passed[1][k]) for k in range(3, heads, 2)}
    total = context(list(firsts.values()), list(firsts), None, jnp.float32)
    context_grad = context(list(lasts.values()), list(lasts), total, jnp.bfloat16)
    upper_dq, even, *odd, rest = attend(True, grads, query, context_grad, *upper_stats, *blocks)
    upper = scatter_ctx(turn(pair_sums, even, *[swap(x, 1, "ctx") for x in odd]))
    lower_dq, even, *odd = attend(
        False, grads, query, context_grad, *lower_stats, rest, *blocks
    )
    sides = [list(range(heads - 1, 0, -2)), list(range(heads - 2, -1, -2))]

    def firsts_of(places):
        return turn(lambda a, b: query_terms(a, b, w_query, heads, places), upper_dq, lower_dq)

    def terms_of(first, terms, places, stacked=False):
        outs = turn(
            lambda a, *b: all_terms(a, b, w_key, value_projection, places, stacked), first, *terms
        )
        return outs[0] if stacked else dict(zip(places, outs))

    first = [firsts_of(sides[0])]
    lower_odd = [swap(x, 1, "ctx") for x in odd]
    upper_got = send_first(None, terms_of(first[0][0], upper, sides[0], True))
    lower = scatter_ctx(turn(pair_sums, even, *lower_odd))
    first.append(firsts_of(sides[1]))
    upper = send_rest(terms_of(first[1][0], upper, sides[1]), upper_got)
    lower_got = send_first(terms_of(first[0][1], lower, sides[0]), None)
    lower = send_rest(terms_of(first[1][1], lower, sides[1]), lower_got)
    return join_rows(upper, lower, span_order)


def solution(mesh):
    in_specs = (
        P("ctx", None),
        P("ctx", "head"),
        P(None, "head"),
        P(None, "head"),
        P(None, "head"),
        P("head", None),
        P(),
        P(),
    )
    out_specs = P("ctx", "head")
    return jax.shard_map(shards, mesh=mesh, in_specs=in_specs, out_specs=out_specs, check_vma=False)
```

profile of v0, /device:TPU:0, one launch (start us, length us, event | category | flops | bytes accessed | tf_op | source)
XLA Modules:
  0.0 113.0 jit_solution(18015758837443955759)
XLA Ops:
  0.0 1.1 fusion
  1.1 4.1 %collective-permute-start.1 = (bf16[128,1024]{1,0:T(8,128)(2,1)S(1)}, bf16[128,1024]{1,0:T(8,128)(2,1)S(1)}, u32[]{:S(2)}, u32[]{:S(2)}) collective-permute-start(bf16[128,1024]{1,0:T(8,128)(2,1)S(1)} %get-tuple-element.268), channel_id=1, source_target_pairs={{0,16},{8,24},{16,0},{24,8},{1,17},{9,25},{17,1},{25,9},{2,18},{10... | collective-permute-start | bytes 786440 | tf_op jit(solution)/shard_map/ppermute | solution.py:562
  5.2 3.3 %project_kv.1.refs_0_.refs_1_ = bf16[256,512]{1,0:T(8,128)(2,1)S(1)} custom-call(bf16[256,4096]{1,0:T(8,128)(2,1)} %x_ref.1, bf16[4096,256]{1,0:T(8,128)(2,1)} %refs_4_.9, bf16[4096,256]{1,0:T(8,128)(2,1)} %refs_5_.7), custom_call_target="tpu_custom_call" | custom-call | bytes 1 | tf_op jit(solution)/shard_map/project_kv/pallas_call | solution.py:90
  8.5 1.6 %collective-permute-start = (bf16[256,512]{1,0:T(8,128)(2,1)S(1)}, bf16[256,512]{1,0:T(8,128)(2,1)S(1)}, u32[]{:S(2)}, u32[]{:S(2)}) collective-permute-start(bf16[256,512]{1,0:T(8,128)(2,1)S(1)} %project_kv.1.refs_0_.refs_1_), channel_id=1, source_target_pairs={{0,2},{1,3},{2,0},{3,1},{4,6},{5,7},{6,4},{7,5},{8,10},{9,11},{10,... | collective-permute-start | bytes 786440 | tf_op jit(solution)/shard_map/ppermute | solution.py:562
  10.1 1.5 %collective-permute-start.3 = (bf16[256,512]{1,0:T(8,128)(2,1)S(1)}, bf16[256,512]{1,0:T(8,128)(2,1)S(1)}, u32[]{:S(2)}, u32[]{:S(2)}) collective-permute-start(bf16[256,512]{1,0:T(8,128)(2,1)S(1)} %project_kv.1.refs_0_.refs_1_), channel_id=1, source_target_pairs={{0,4},{1,5},{2,6},{3,7},{4,0},{5,1},{6,2},{7,3},{8,12},{9,13},{10,... | collective-permute-start | bytes 786440 | tf_op jit(solution)/shard_map/ppermute | solution.py:562
  11.6 1.6 %collective-permute-start.6 = (bf16[256,1024]{1,0:T(8,128)(2,1)S(1)}, bf16[256,1024]{1,0:T(8,128)(2,1)S(1)}, u32[]{:S(2)}, u32[]{:S(2)}) collective-permute-start(bf16[256,1024]{1,0:T(8,128)(2,1)S(1)} %copy-done), channel_id=1, source_target_pairs={{0,8},{8,0},{16,24},{24,16},{1,9},{9,1},{17,25},{25,17},{2,10},{10... | collective-permute-start | bytes 1572872 | tf_op jit(solution)/shard_map/ppermute | solution.py:562
  13.2 4.0 %collective-permute-done.1.refs_2_ = bf16[128,1024]{1,0:T(8,128)(2,1)S(1)} collective-permute-done((bf16[128,1024]{1,0:T(8,128)(2,1)S(1)}, bf16[128,1024]{1,0:T(8,128)(2,1)S(1)}, u32[]{:S(2)}, u32[]{:S(2)}) %collective-permute-start.1) | collective-permute-done | bytes 262176 | tf_op jit(solution)/shard_map/ppermute | solution.py:562
  17.2 1.6 %collective-permute-start.4 = (bf16[256,512]{1,0:T(8,128)(2,1)S(1)}, bf16[256,512]{1,0:T(8,128)(2,1)S(1)}, u32[]{:S(2)}, u32[]{:S(2)}) collective-permute-start(bf16[256,512]{1,0:T(8,128)(2,1)S(1)} %collective-permute-done.refs_1_.refs_2_), channel_id=1, source_target_pairs={{0,4},{1,5},{2,6},{3,7},{4,0},{5,1},{6,2},{7,3},{8,12},{9,13},{10,... | collective-permute-start | bytes 786440 | tf_op jit(solution)/shard_map/ppermute | solution.py:562
  18.8 4.9 %project.1.q_ref = bf16[256,1024]{1,0:T(8,128)(2,1)S(1)} custom-call(bf16[256,4096]{1,0:T(8,128)(2,1)} %x_ref.1, bf16[4096,1024]{1,0:T(8,128)(2,1)} %w_ref.4), custom_call_target="tpu_custom_call" | custom-call | bytes 1 | tf_op jit(solution)/shard_map/project/pallas_call | solution.py:136
  23.7 0.9 collective-permute-done.4.refs_3_.refs_4_
  24.6 0.5 collective-permute-start.9
  25.2 7.2 %collective-permute-done.5.refs_3_ = bf16[128,1024]{1,0:T(8,128)(2,1)S(1)} collective-permute-done((bf16[128,1024]{1,0:T(8,128)(2,1)S(1)}, bf16[128,1024]{1,0:T(8,128)(2,1)S(1)}, u32[]{:S(2)}, u32[]{:S(2)}) %collective-permute-start.5) | collective-permute-done | bytes 262176 | tf_op jit(solution)/shard_map/ppermute | solution.py:562
  32.3 1.6 %collective-permute-done.6.refs_1_ = bf16[256,1024]{1,0:T(8,128)(2,1)S(1)} collective-permute-done((bf16[256,1024]{1,0:T(8,128)(2,1)S(1)}, bf16[256,1024]{1,0:T(8,128)(2,1)S(1)}, u32[]{:S(2)}, u32[]{:S(2)}) %collective-permute-start.6) | collective-permute-done | bytes 524320 | tf_op jit(solution)/shard_map/ppermute | solution.py:562
  34.0 2.0 %collective-permute-start.7 = (bf16[128,1024]{1,0:T(8,128)(2,1)S(1)}, bf16[128,1024]{1,0:T(8,128)(2,1)S(1)}, u32[]{:S(2)}, u32[]{:S(2)}) collective-permute-start(bf16[128,1024]{1,0:T(8,128)(2,1)S(1)} %collective-permute-done.5.refs_3_), channel_id=1, source_target_pairs={{0,8},{8,0},{16,24},{24,16},{1,9},{9,1},{17,25},{25,17},{2,10},{10... | collective-permute-start | bytes 786440 | tf_op jit(solution)/shard_map/ppermute | solution.py:562
  36.0 2.9 %upper_stats.1 = (f32[2,1,512]{2,1,0:T(1,128)S(1)}, f32[2,128,512]{2,1,0:T(8,128)S(1)}) custom-call(s32[16]{0:T(128)S(1)} %copy-done.1, s32[8]{0:T(128)S(1)} %copy-done.2, bf16[256,1024]{1,0:T(8,128)(2,1)S(1)} %project.1.q_ref, bf16[256,512]{1,0:T(8,128)(2,1)S(1)} %project_kv.1.refs_0_.refs_1_, bf16[256,512]{1,0:T(8,128)(2,1)S(1)} %collective-permute-done.refs_1_.refs_2_, ...), custom_call_target="tpu_custom_call" | custom-call | bytes 1 | tf_op jit(solution)/shard_map/upper_stats/pallas_call | solution.py:437
  38.9 1.9 %lower_stats.1 = (f32[2,1,512]{2,1,0:T(1,128)S(1)}, f32[2,128,512]{2,1,0:T(8,128)S(1)}) custom-call(s32[16]{0:T(128)S(1)} %copy-done.1, s32[8]{0:T(128)S(1)} %copy-done.2, bf16[256,1024]{1,0:T(8,128)(2,1)S(1)} %project.1.q_ref, bf16[256,512]{1,0:T(8,128)(2,1)S(1)} %project_kv.1.refs_0_.refs_1_, bf16[256,512]{1,0:T(8,128)(2,1)S(1)} %collective-permute-done.refs_1_.refs_2_, ...), custom_call_target="tpu_custom_call" | custom-call | bytes 1 | tf_op jit(solution)/shard_map/lower_stats/pallas_call | solution.py:437
  40.8 4.2 %context_grad.2.refs_0_ = f32[256,1024]{1,0:T(8,128)S(1)} custom-call(bf16[256,1024]{1,0:T(8,128)(2,1)S(1)} %copy-done, bf16[256,1024]{1,0:T(8,128)(2,1)S(1)} %collective-permute-done.6.refs_1_, bf16[128,1024]{1,0:T(8,128)(2,1)S(1)} %collective-permute-done.1.refs_2_, bf16[128,1024]{1,0:T(8,128)(2,1)S(1)} %collective-permute-done.5.refs_3_, ...), custom_call_target="tpu_custom_call" | custom-call | bytes 1 | tf_op jit(solution)/shard_map/context_grad/pallas_call | solution.py:178
  45.1 2.7 %collective-permute-done.7.refs_2_ = bf16[128,1024]{1,0:T(8,128)(2,1)S(1)} collective-permute-done((bf16[128,1024]{1,0:T(8,128)(2,1)S(1)}, bf16[128,1024]{1,0:T(8,128)(2,1)S(1)}, u32[]{:S(2)}, u32[]{:S(2)}) %collective-permute-start.7) | collective-permute-done | bytes 262176 | tf_op jit(solution)/shard_map/ppermute | solution.py:562
  47.8 2.4 %context_grad.3.g_ref = bf16[256,1024]{1,0:T(8,128)(2,1)S(1)} custom-call(f32[256,1024]{1,0:T(8,128)S(1)} %context_grad.2.refs_0_, bf16[128,1024]{1,0:T(8,128)(2,1)S(1)} %collective-permute-done.2.refs_1_, bf16[128,1024]{1,0:T(8,128)(2,1)S(1)} %collective-permute-done.7.refs_2_, bf16[1024,4096]{1,0:T(8,128)(2,1)} %refs_3_.1), custom_call_target="tpu_custom_call" | custom-call | bytes 1 | tf_op jit(solution)/shard_map/context_grad/pallas_call | solution.py:178
  50.2 4.6 %upper_grads.1 = (bf16[128,1024]{1,0:T(8,128)(2,1)S(1)}, bf16[4,128,512]{2,1,0:T(8,128)(2,1)S(1)}, bf16[2,128,512]{2,1,0:T(8,128)(2,1)S(1)}, bf16[2,128,512]{2,1,0:T(8,128)(2,1)S(1)}, f32[1024,512]{1,0:T(8,128)S(1)}) custom-call(s32[16]{0:T(128)S(1)} %copy-done.1, s32[8]{0:T(128)S(1)} %copy-done.2, bf16[256,1024]{1,0:T(8,128)(2,1)S(1)} %project.1.q_ref, ...), custom_call_target="tpu_custom_call" | custom-call | bytes 1 | tf_op jit(solution)/shard_map/upper_grads/pallas_call | solution.py:544
  54.9 0.5 collective-permute-start.13
  55.4 1.0 collective-permute-done.12.refs_0_
  56.4 0.4 collective-permute-done.13.refs_1_
  57.0 0.8 collective-permute-start.15
  57.8 2.6 %collective-permute-start.16 = (bf16[128,512]{1,0:T(8,128)(2,1)S(1)}, bf16[128,512]{1,0:T(8,128)(2,1)S(1)}, u32[]{:S(2)}, u32[]{:S(2)}) collective-permute-start(bf16[128,512]{1,0:T(8,128)(2,1)S(1)} %get-tuple-element.221), channel_id=1, source_target_pairs={{0,6},{1,7},{2,4},{3,5},{4,2},{5,3},{6,0},{7,1},{8,14},{9,15},{10,... | collective-permute-start | bytes 393224 | tf_op jit(solution)/shard_map/ppermute | solution.py:562
  60.5 3.0 %lower_grads.1 = (bf16[128,1024]{1,0:T(8,128)(2,1)S(1)}, bf16[4,128,512]{2,1,0:T(8,128)(2,1)S(1)}, bf16[2,128,512]{2,1,0:T(8,128)(2,1)S(1)}, bf16[2,128,512]{2,1,0:T(8,128)(2,1)S(1)}) custom-call(s32[16]{0:T(128)S(1)} %copy-done.1, s32[8]{0:T(128)S(1)} %copy-done.2, bf16[256,1024]{1,0:T(8,128)(2,1)S(1)} %project.1.q_ref, ...), custom_call_target="tpu_custom_call" | custom-call | bytes 1 | tf_op jit(solution)/shard_map/lower_grads/pallas_call | solution.py:544
  63.4 3.1 %query_terms.2 = (f32[2,128,1024]{2,1,0:T(8,128)S(1)}, f32[2,128,1024]{2,1,0:T(8,128)S(1)}) custom-call(bf16[128,1024]{1,0:T(8,128)(2,1)S(1)} %get-tuple-element.234.upper_ref, bf16[128,1024]{1,0:T(8,128)(2,1)S(1)} %get-tuple-element.235.lower_ref, bf16[4096,1024]{1,0:T(8,128)(2,1)} %w_ref.4), custom_call_target="tpu_custom_call" | custom-call | bytes 1 | tf_op jit(solution)/shard_map/query_terms/pallas_call | solution.py:214
  66.6 2.2 %all_terms.4 = bf16[2,128,1024]{2,1,0:T(8,128)(2,1)S(1)} custom-call(f32[2,128,1024]{2,1,0:T(8,128)S(1)} %get-tuple-element.222.first_ref, bf16[128,512]{1,0:T(8,128)(2,1)S(1)} %get-tuple-element.238.refs_0_, bf16[128,512]{1,0:T(8,128)(2,1)S(1)} %collective-permute-done.14.refs_1_, bf16[128,512]{1,0:T(8,128)(2,1)S(1)} %collective-permute-done.15.refs_2_, ...), custom_call_target="tpu_custom_call" | custom-call | bytes 1 | tf_op jit(solution)/shard_map/all_terms/pallas_call | solution.py:259
  68.8 0.5 collective-permute-start.19
  69.3 0.5 collective-permute-start.18
  69.8 1.0 collective-permute-done.17.refs_0_
  70.9 0.4 collective-permute-done.18.refs_1_
  71.3 1.3 %collective-permute-start.21 = (bf16[128,512]{1,0:T(8,128)(2,1)S(1)}, bf16[128,512]{1,0:T(8,128)(2,1)S(1)}, u32[]{:S(2)}, u32[]{:S(2)}) collective-permute-start(bf16[128,512]{1,0:T(8,128)(2,1)S(1)} %get-tuple-element.247), channel_id=1, source_target_pairs={{0,2},{1,3},{2,0},{3,1},{4,6},{5,7},{6,4},{7,5},{8,10},{9,11},{10,... | collective-permute-start | bytes 393224 | tf_op jit(solution)/shard_map/ppermute | solution.py:562
  72.6 1.6 %collective-permute-start.22 = (bf16[128,512]{1,0:T(8,128)(2,1)S(1)}, bf16[128,512]{1,0:T(8,128)(2,1)S(1)}, u32[]{:S(2)}, u32[]{:S(2)}) collective-permute-start(bf16[128,512]{1,0:T(8,128)(2,1)S(1)} %get-tuple-element.248), channel_id=1, source_target_pairs={{0,4},{1,5},{2,6},{3,7},{4,0},{5,1},{6,2},{7,3},{8,12},{9,13},{10,... | collective-permute-start | bytes 393224 | tf_op jit(solution)/shard_map/ppermute | solution.py:562
  74.2 0.7 collective-permute-start.23
  74.9 3.1 %query_terms.3 = (f32[2,128,1024]{2,1,0:T(8,128)S(1)}, f32[2,128,1024]{2,1,0:T(8,128)S(1)}) custom-call(bf16[128,1024]{1,0:T(8,128)(2,1)S(1)} %get-tuple-element.234.upper_ref, bf16[128,1024]{1,0:T(8,128)(2,1)S(1)} %get-tuple-element.235.lower_ref, bf16[4096,1024]{1,0:T(8,128)(2,1)} %w_ref.4), custom_call_target="tpu_custom_call" | custom-call | bytes 1 | tf_op jit(solution)/shard_map/query_terms/pallas_call | solution.py:214
  78.0 2.2 %all_terms.5 = (bf16[128,1024]{1,0:T(8,128)(2,1)S(1)}, bf16[128,1024]{1,0:T(8,128)(2,1)S(1)}) custom-call(f32[2,128,1024]{2,1,0:T(8,128)S(1)} %get-tuple-element.237.first_ref, bf16[128,512]{1,0:T(8,128)(2,1)S(1)} %get-tuple-element.238.refs_0_, bf16[128,512]{1,0:T(8,128)(2,1)S(1)} %collective-permute-done.14.refs_1_, ...), custom_call_target="tpu_custom_call" | custom-call | bytes 1 | tf_op jit(solution)/shard_map/all_terms/pallas_call | solution.py:259
  80.2 1.8 %collective-permute-done.19.b_ref.refs_1_ = bf16[2,128,1024]{2,1,0:T(8,128)(2,1)S(1)} collective-permute-done((bf16[2,128,1024]{2,1,0:T(8,128)(2,1)S(1)}, bf16[2,128,1024]{2,1,0:T(8,128)(2,1)S(1)}, u32[]{:S(2)}, u32[]{:S(2)}) %collective-permute-start.19) | collective-permute-done | bytes 524320 | tf_op jit(solution)/shard_map/ppermute | solution.py:562
  82.1 2.2 %all_terms.6 = (bf16[128,1024]{1,0:T(8,128)(2,1)S(1)}, bf16[128,1024]{1,0:T(8,128)(2,1)S(1)}) custom-call(f32[2,128,1024]{2,1,0:T(8,128)S(1)} %get-tuple-element.250.first_ref, bf16[128,512]{1,0:T(8,128)(2,1)S(1)} %get-tuple-element.258.refs_0_, bf16[128,512]{1,0:T(8,128)(2,1)S(1)} %collective-permute-done.21.refs_1_, ...), custom_call_target="tpu_custom_call" | custom-call | bytes 1 | tf_op jit(solution)/shard_map/all_terms/pallas_call | solution.py:259
  84.3 0.5 collective-permute-start.25
  84.8 3.4 %collective-permute-start.20 = (bf16[128,1024]{1,0:T(8,128)(2,1)S(1)}, bf16[128,1024]{1,0:T(8,128)(2,1)S(1)}, u32[]{:S(2)}, u32[]{:S(2)}) collective-permute-start(bf16[128,1024]{1,0:T(8,128)(2,1)S(1)} %add.2), channel_id=1, source_target_pairs={{0,16},{8,24},{16,0},{24,8},{1,17},{9,25},{17,1},{25,9},{2,18},{10... | collective-permute-start | bytes 786440 | tf_op jit(solution)/shard_map/ppermute | solution.py:562
  88.2 0.3 collective-permute-start.24
  88.5 2.2 %all_terms.7 = (bf16[128,1024]{1,0:T(8,128)(2,1)S(1)}, bf16[128,1024]{1,0:T(8,128)(2,1)S(1)}) custom-call(f32[2,128,1024]{2,1,0:T(8,128)S(1)} %get-tuple-element.257.first_ref, bf16[128,512]{1,0:T(8,128)(2,1)S(1)} %get-tuple-element.258.refs_0_, bf16[128,512]{1,0:T(8,128)(2,1)S(1)} %collective-permute-done.21.refs_1_, ...), custom_call_target="tpu_custom_call" | custom-call | bytes 1 | tf_op jit(solution)/shard_map/all_terms/pallas_call | solution.py:259
  90.7 8.2 %collective-permute-done.25.b_ref = bf16[128,1024]{1,0:T(8,128)(2,1)S(1)} collective-permute-done((bf16[128,1024]{1,0:T(8,128)(2,1)S(1)}, bf16[128,1024]{1,0:T(8,128)(2,1)S(1)}, u32[]{:S(2)}, u32[]{:S(2)}) %collective-permute-start.25) | collective-permute-done | bytes 262176 | tf_op jit(solution)/shard_map/ppermute | solution.py:562
  99.0 0.5 collective-permute-start.26
  99.5 6.9 %collective-permute-done.24.refs_4_ = bf16[128,1024]{1,0:T(8,128)(2,1)S(1)} collective-permute-done((bf16[128,1024]{1,0:T(8,128)(2,1)S(1)}, bf16[128,1024]{1,0:T(8,128)(2,1)S(1)}, u32[]{:S(2)}, u32[]{:S(2)}) %collective-permute-start.24) | collective-permute-done | bytes 262176 | tf_op jit(solution)/shard_map/ppermute | solution.py:562
  106.5 5.0 %collective-permute-done.26.refs_5_ = bf16[128,1024]{1,0:T(8,128)(2,1)S(1)} collective-permute-done((bf16[128,1024]{1,0:T(8,128)(2,1)S(1)}, bf16[128,1024]{1,0:T(8,128)(2,1)S(1)}, u32[]{:S(2)}, u32[]{:S(2)}) %collective-permute-start.26) | collective-permute-done | bytes 262176 | tf_op jit(solution)/shard_map/ppermute | solution.py:562
  111.5 1.5 %join_rows.1 = bf16[256,1024]{1,0:T(8,128)(2,1)} custom-call(s32[16]{0:T(128)S(1)} %copy-done.1, bf16[128,1024]{1,0:T(8,128)(2,1)S(1)} %get-tuple-element.242.refs_0_, bf16[2,128,1024]{2,1,0:T(8,128)(2,1)S(1)} %collective-permute-done.19.b_ref.refs_1_, bf16[128,1024]{1,0:T(8,128)(2,1)S(1)} %collective-permute-done.20.refs_2_, ...), custom_call_target="tpu_custom_call" | custom-call | bytes 1 | tf_op jit(solution)/shard_map/join_rows/pallas_call | solution.py:314
  (32 shorter events, 0.6 us)
Async XLA Ops:
  1.1 10.5 %copy-start = (bf16[256,1024]{1,0:T(8,128)(2,1)S(1)}, bf16[256,1024]{1,0:T(8,128)(2,1)}, u32[]{:S(2)}) copy-start(bf16[256,1024]{1,0:T(8,128)(2,1)} %refs_0_) | copy-start | bytes 1572868
  1.1 16.1 %collective-permute-start.1 = (bf16[128,1024]{1,0:T(8,128)(2,1)S(1)}, bf16[128,1024]{1,0:T(8,128)(2,1)S(1)}, u32[]{:S(2)}, u32[]{:S(2)}) collective-permute-start(bf16[128,1024]{1,0:T(8,128)(2,1)S(1)} %get-tuple-element.268), channel_id=1, source_target_pairs={{0,16},{8,24},{16,0},{24,8},{1,17},{9,25},{17,1},{25,9},{2,18},{10... | collective-permute-start | bytes 786440 | tf_op jit(solution)/shard_map/ppermute | solution.py:562
  8.5 8.7 %collective-permute-start = (bf16[256,512]{1,0:T(8,128)(2,1)S(1)}, bf16[256,512]{1,0:T(8,128)(2,1)S(1)}, u32[]{:S(2)}, u32[]{:S(2)}) collective-permute-start(bf16[256,512]{1,0:T(8,128)(2,1)S(1)} %project_kv.1.refs_0_.refs_1_), channel_id=1, source_target_pairs={{0,2},{1,3},{2,0},{3,1},{4,6},{5,7},{6,4},{7,5},{8,10},{9,11},{10,... | collective-permute-start | bytes 786440 | tf_op jit(solution)/shard_map/ppermute | solution.py:562
  10.1 13.6 %collective-permute-start.3 = (bf16[256,512]{1,0:T(8,128)(2,1)S(1)}, bf16[256,512]{1,0:T(8,128)(2,1)S(1)}, u32[]{:S(2)}, u32[]{:S(2)}) collective-permute-start(bf16[256,512]{1,0:T(8,128)(2,1)S(1)} %project_kv.1.refs_0_.refs_1_), channel_id=1, source_target_pairs={{0,4},{1,5},{2,6},{3,7},{4,0},{5,1},{6,2},{7,3},{8,12},{9,13},{10,... | collective-permute-start | bytes 786440 | tf_op jit(solution)/shard_map/ppermute | solution.py:562
  11.6 22.4 %collective-permute-start.6 = (bf16[256,1024]{1,0:T(8,128)(2,1)S(1)}, bf16[256,1024]{1,0:T(8,128)(2,1)S(1)}, u32[]{:S(2)}, u32[]{:S(2)}) collective-permute-start(bf16[256,1024]{1,0:T(8,128)(2,1)S(1)} %copy-done), channel_id=1, source_target_pairs={{0,8},{8,0},{16,24},{24,16},{1,9},{9,1},{17,25},{25,17},{2,10},{10... | collective-permute-start | bytes 1572872 | tf_op jit(solution)/shard_map/ppermute | solution.py:562
  17.2 7.4 %collective-permute-start.4 = (bf16[256,512]{1,0:T(8,128)(2,1)S(1)}, bf16[256,512]{1,0:T(8,128)(2,1)S(1)}, u32[]{:S(2)}, u32[]{:S(2)}) collective-permute-start(bf16[256,512]{1,0:T(8,128)(2,1)S(1)} %collective-permute-done.refs_1_.refs_2_), channel_id=1, source_target_pairs={{0,4},{1,5},{2,6},{3,7},{4,0},{5,1},{6,2},{7,3},{8,12},{9,13},{10,... | collective-permute-start | bytes 786440 | tf_op jit(solution)/shard_map/ppermute | solution.py:562
  18.8 17.2 %copy-start.1 = (s32[16]{0:T(128)S(1)}, s32[16]{0:T(128)}, u32[]{:S(2)}) copy-start(s32[16]{0:T(128)} %order.9) | copy-start | bytes 196
  18.8 17.2 %copy-start.2 = (s32[8]{0:T(128)S(1)}, s32[8]{0:T(128)}, u32[]{:S(2)}) copy-start(s32[8]{0:T(128)} %lengths.7) | copy-start | bytes 100
  18.8 13.5 %collective-permute-start.5 = (bf16[128,1024]{1,0:T(8,128)(2,1)S(1)}, bf16[128,1024]{1,0:T(8,128)(2,1)S(1)}, u32[]{:S(2)}, u32[]{:S(2)}) collective-permute-start(bf16[128,1024]{1,0:T(8,128)(2,1)S(1)} %get-tuple-element.267), channel_id=1, source_target_pairs={{0,16},{8,24},{16,0},{24,8},{1,17},{9,25},{17,1},{25,9},{2,18},{10... | collective-permute-start | bytes 786440 | tf_op jit(solution)/shard_map/ppermute | solution.py:562
  24.6 9.3 %collective-permute-start.8 = (bf16[256,512]{1,0:T(8,128)(2,1)S(1)}, bf16[256,512]{1,0:T(8,128)(2,1)S(1)}, u32[]{:S(2)}, u32[]{:S(2)}) collective-permute-start(bf16[256,512]{1,0:T(8,128)(2,1)S(1)} %project_kv.1.refs_0_.refs_1_), channel_id=1, source_target_pairs={{0,1},{1,0},{2,3},{3,2},{4,5},{5,4},{6,7},{7,6},{8,9},{9,8},{10,11... | collective-permute-start | bytes 786440 | tf_op jit(solution)/shard_map/ppermute | solution.py:562
  24.6 11.3 %collective-permute-start.9 = (bf16[256,512]{1,0:T(8,128)(2,1)S(1)}, bf16[256,512]{1,0:T(8,128)(2,1)S(1)}, u32[]{:S(2)}, u32[]{:S(2)}) collective-permute-start(bf16[256,512]{1,0:T(8,128)(2,1)S(1)} %collective-permute-done.refs_1_.refs_2_), channel_id=1, source_target_pairs={{0,1},{1,0},{2,3},{3,2},{4,5},{5,4},{6,7},{7,6},{8,9},{9,8},{10,11... | collective-permute-start | bytes 786440 | tf_op jit(solution)/shard_map/ppermute | solution.py:562
  25.2 10.8 %collective-permute-start.10 = (bf16[256,512]{1,0:T(8,128)(2,1)S(1)}, bf16[256,512]{1,0:T(8,128)(2,1)S(1)}, u32[]{:S(2)}, u32[]{:S(2)}) collective-permute-start(bf16[256,512]{1,0:T(8,128)(2,1)S(1)} %collective-permute-done.3.refs_2_.refs_3_), channel_id=1, source_target_pairs={{0,1},{1,0},{2,3},{3,2},{4,5},{5,4},{6,7},{7,6},{8,9},{9,8},{10,11... | collective-permute-start | bytes 786440 | tf_op jit(solution)/shard_map/ppermute | solution.py:562
  32.3 3.7 %collective-permute-start.11 = (bf16[256,512]{1,0:T(8,128)(2,1)S(1)}, bf16[256,512]{1,0:T(8,128)(2,1)S(1)}, u32[]{:S(2)}, u32[]{:S(2)}) collective-permute-start(bf16[256,512]{1,0:T(8,128)(2,1)S(1)} %collective-permute-done.4.refs_3_.refs_4_), channel_id=1, source_target_pairs={{0,1},{1,0},{2,3},{3,2},{4,5},{5,4},{6,7},{7,6},{8,9},{9,8},{10,11... | collective-permute-start | bytes 786440 | tf_op jit(solution)/shard_map/ppermute | solution.py:562
  34.0 11.1 %collective-permute-start.2 = (bf16[128,1024]{1,0:T(8,128)(2,1)S(1)}, bf16[128,1024]{1,0:T(8,128)(2,1)S(1)}, u32[]{:S(2)}, u32[]{:S(2)}) collective-permute-start(bf16[128,1024]{1,0:T(8,128)(2,1)S(1)} %collective-permute-done.1.refs_2_), channel_id=1, source_target_pairs={{0,8},{8,0},{16,24},{24,16},{1,9},{9,1},{17,25},{25,17},{2,10},{10... | collective-permute-start | bytes 786440 | tf_op jit(solution)/shard_map/ppermute | solution.py:562
  34.0 13.8 %collective-permute-start.7 = (bf16[128,1024]{1,0:T(8,128)(2,1)S(1)}, bf16[128,1024]{1,0:T(8,128)(2,1)S(1)}, u32[]{:S(2)}, u32[]{:S(2)}) collective-permute-start(bf16[128,1024]{1,0:T(8,128)(2,1)S(1)} %collective-permute-done.5.refs_3_), channel_id=1, source_target_pairs={{0,8},{8,0},{16,24},{24,16},{1,9},{9,1},{17,25},{25,17},{2,10},{10... | collective-permute-start | bytes 786440 | tf_op jit(solution)/shard_map/ppermute | solution.py:562
  54.8 1.6 %collective-permute-start.12 = (bf16[2,128,512]{2,1,0:T(8,128)(2,1)S(1)}, bf16[2,128,512]{2,1,0:T(8,128)(2,1)S(1)}, u32[]{:S(2)}, u32[]{:S(2)}) collective-permute-start(bf16[2,128,512]{2,1,0:T(8,128)(2,1)S(1)} %get-tuple-element.194), channel_id=1, source_target_pairs={{0,1},{1,0},{2,3},{3,2},{4,5},{5,4},{6,7},{7,6},{8,9},{9,8},{10,11... | collective-permute-start | bytes 786440 | tf_op jit(solution)/shard_map/ppermute | solution.py:562
  54.9 1.9 %collective-permute-start.13 = (bf16[2,128,512]{2,1,0:T(8,128)(2,1)S(1)}, bf16[2,128,512]{2,1,0:T(8,128)(2,1)S(1)}, u32[]{:S(2)}, u32[]{:S(2)}) collective-permute-start(bf16[2,128,512]{2,1,0:T(8,128)(2,1)S(1)} %get-tuple-element.195), channel_id=1, source_target_pairs={{0,1},{1,0},{2,3},{3,2},{4,5},{5,4},{6,7},{7,6},{8,9},{9,8},{10,11... | collective-permute-start | bytes 786440 | tf_op jit(solution)/shard_map/ppermute | solution.py:562
  56.9 9.7 %collective-permute-start.14 = (bf16[128,512]{1,0:T(8,128)(2,1)S(1)}, bf16[128,512]{1,0:T(8,128)(2,1)S(1)}, u32[]{:S(2)}, u32[]{:S(2)}) collective-permute-start(bf16[128,512]{1,0:T(8,128)(2,1)S(1)} %get-tuple-element.219), channel_id=1, source_target_pairs={{0,2},{1,3},{2,0},{3,1},{4,6},{5,7},{6,4},{7,5},{8,10},{9,11},{10,... | collective-permute-start | bytes 393224 | tf_op jit(solution)/shard_map/ppermute | solution.py:562
  57.0 9.6 %collective-permute-start.15 = (bf16[128,512]{1,0:T(8,128)(2,1)S(1)}, bf16[128,512]{1,0:T(8,128)(2,1)S(1)}, u32[]{:S(2)}, u32[]{:S(2)}) collective-permute-start(bf16[128,512]{1,0:T(8,128)(2,1)S(1)} %get-tuple-element.220), channel_id=1, source_target_pairs={{0,4},{1,5},{2,6},{3,7},{4,0},{5,1},{6,2},{7,3},{8,12},{9,13},{10,... | collective-permute-start | bytes 393224 | tf_op jit(solution)/shard_map/ppermute | solution.py:562
  57.8 8.8 %collective-permute-start.16 = (bf16[128,512]{1,0:T(8,128)(2,1)S(1)}, bf16[128,512]{1,0:T(8,128)(2,1)S(1)}, u32[]{:S(2)}, u32[]{:S(2)}) collective-permute-start(bf16[128,512]{1,0:T(8,128)(2,1)S(1)} %get-tuple-element.221), channel_id=1, source_target_pairs={{0,6},{1,7},{2,4},{3,5},{4,2},{5,3},{6,0},{7,1},{8,14},{9,15},{10,... | collective-permute-start | bytes 393224 | tf_op jit(solution)/shard_map/ppermute | solution.py:562
  68.8 13.2 %collective-permute-start.19 = (bf16[2,128,1024]{2,1,0:T(8,128)(2,1)S(1)}, bf16[2,128,1024]{2,1,0:T(8,128)(2,1)S(1)}, u32[]{:S(2)}, u32[]{:S(2)}) collective-permute-start(bf16[2,128,1024]{2,1,0:T(8,128)(2,1)S(1)} %all_terms.4), channel_id=1, source_target_pairs={{0,8},{8,0},{16,24},{24,16},{1,9},{9,1},{17,25},{25,17},{2,10},{10... | collective-permute-start | bytes 1572872 | tf_op jit(solution)/shard_map/ppermute | solution.py:562
  69.3 1.5 %collective-permute-start.17 = (bf16[2,128,512]{2,1,0:T(8,128)(2,1)S(1)}, bf16[2,128,512]{2,1,0:T(8,128)(2,1)S(1)}, u32[]{:S(2)}, u32[]{:S(2)}) collective-permute-start(bf16[2,128,512]{2,1,0:T(8,128)(2,1)S(1)} %get-tuple-element.228), channel_id=1, source_target_pairs={{0,1},{1,0},{2,3},{3,2},{4,5},{5,4},{6,7},{7,6},{8,9},{9,8},{10,11... | collective-permute-start | bytes 786440 | tf_op jit(solution)/shard_map/ppermute | solution.py:562
  69.3 1.9 %collective-permute-start.18 = (bf16[2,128,512]{2,1,0:T(8,128)(2,1)S(1)}, bf16[2,128,512]{2,1,0:T(8,128)(2,1)S(1)}, u32[]{:S(2)}, u32[]{:S(2)}) collective-permute-start(bf16[2,128,512]{2,1,0:T(8,128)(2,1)S(1)} %get-tuple-element.229), channel_id=1, source_target_pairs={{0,1},{1,0},{2,3},{3,2},{4,5},{5,4},{6,7},{7,6},{8,9},{9,8},{10,11... | collective-permute-start | bytes 786440 | tf_op jit(solution)/shard_map/ppermute | solution.py:562
  71.3 10.7 %collective-permute-start.21 = (bf16[128,512]{1,0:T(8,128)(2,1)S(1)}, bf16[128,512]{1,0:T(8,128)(2,1)S(1)}, u32[]{:S(2)}, u32[]{:S(2)}) collective-permute-start(bf16[128,512]{1,0:T(8,128)(2,1)S(1)} %get-tuple-element.247), channel_id=1, source_target_pairs={{0,2},{1,3},{2,0},{3,1},{4,6},{5,7},{6,4},{7,5},{8,10},{9,11},{10,... | collective-permute-start | bytes 393224 | tf_op jit(solution)/shard_map/ppermute | solution.py:562
  72.6 9.5 %collective-permute-start.22 = (bf16[128,512]{1,0:T(8,128)(2,1)S(1)}, bf16[128,512]{1,0:T(8,128)(2,1)S(1)}, u32[]{:S(2)}, u32[]{:S(2)}) collective-permute-start(bf16[128,512]{1,0:T(8,128)(2,1)S(1)} %get-tuple-element.248), channel_id=1, source_target_pairs={{0,4},{1,5},{2,6},{3,7},{4,0},{5,1},{6,2},{7,3},{8,12},{9,13},{10,... | collective-permute-start | bytes 393224 | tf_op jit(solution)/shard_map/ppermute | solution.py:562
  74.2 7.9 %collective-permute-start.23 = (bf16[128,512]{1,0:T(8,128)(2,1)S(1)}, bf16[128,512]{1,0:T(8,128)(2,1)S(1)}, u32[]{:S(2)}, u32[]{:S(2)}) collective-permute-start(bf16[128,512]{1,0:T(8,128)(2,1)S(1)} %get-tuple-element.249), channel_id=1, source_target_pairs={{0,6},{1,7},{2,4},{3,5},{4,2},{5,3},{6,0},{7,1},{8,14},{9,15},{10,... | collective-permute-start | bytes 393224 | tf_op jit(solution)/shard_map/ppermute | solution.py:562
  84.3 14.6 %collective-permute-start.25 = (bf16[128,1024]{1,0:T(8,128)(2,1)S(1)}, bf16[128,1024]{1,0:T(8,128)(2,1)S(1)}, u32[]{:S(2)}, u32[]{:S(2)}) collective-permute-start(bf16[128,1024]{1,0:T(8,128)(2,1)S(1)} %get-tuple-element.255), channel_id=1, source_target_pairs={{0,8},{8,0},{16,24},{24,16},{1,9},{9,1},{17,25},{25,17},{2,10},{10... | collective-permute-start | bytes 786440 | tf_op jit(solution)/shard_map/ppermute | solution.py:562
  84.8 21.7 %collective-permute-start.20 = (bf16[128,1024]{1,0:T(8,128)(2,1)S(1)}, bf16[128,1024]{1,0:T(8,128)(2,1)S(1)}, u32[]{:S(2)}, u32[]{:S(2)}) collective-permute-start(bf16[128,1024]{1,0:T(8,128)(2,1)S(1)} %add.2), channel_id=1, source_target_pairs={{0,16},{8,24},{16,0},{24,8},{1,17},{9,25},{17,1},{25,9},{2,18},{10... | collective-permute-start | bytes 786440 | tf_op jit(solution)/shard_map/ppermute | solution.py:562
  88.2 18.2 %collective-permute-start.24 = (bf16[128,1024]{1,0:T(8,128)(2,1)S(1)}, bf16[128,1024]{1,0:T(8,128)(2,1)S(1)}, u32[]{:S(2)}, u32[]{:S(2)}) collective-permute-start(bf16[128,1024]{1,0:T(8,128)(2,1)S(1)} %get-tuple-element.263), channel_id=1, source_target_pairs={{0,8},{8,0},{16,24},{24,16},{1,9},{9,1},{17,25},{25,17},{2,10},{10... | collective-permute-start | bytes 786440 | tf_op jit(solution)/shard_map/ppermute | solution.py:562
  99.0 12.5 %collective-permute-start.26 = (bf16[128,1024]{1,0:T(8,128)(2,1)S(1)}, bf16[128,1024]{1,0:T(8,128)(2,1)S(1)}, u32[]{:S(2)}, u32[]{:S(2)}) collective-permute-start(bf16[128,1024]{1,0:T(8,128)(2,1)S(1)} %add.3), channel_id=1, source_target_pairs={{0,16},{8,24},{16,0},{24,8},{1,17},{9,25},{17,1},{25,9},{2,18},{10... | collective-permute-start | bytes 786440 | tf_op jit(solution)/shard_map/ppermute | solution.py:562
where the time goes:
time: 114 us; the launch traced here: 113 us
  Pallas kernels  44.1 us (39%)
  waiting for transfers between devices  41.2 us (36%)
  starting transfers between devices  26.3 us (23%)
    ppermute x27, waiting for transfers between devices, swap(): lax.ppermute(x, axis, [(i, i ^ k) for i in range(lax.axis_size(axis))])  41.2 us
    ppermute x27, starting transfers between devices, swap(): lax.ppermute(x, axis, [(i, i ^ k) for i in range(lax.axis_size(axis))])  26.3 us
    pallas_call x4, Pallas kernels, all_terms(): pl.pallas_call(functools.partial(all_terms_body, places, len(terms)), in_...  8.81 us
    pallas_call x2, Pallas kernels, grads(): pl.pallas_call(functools.partial(grads_body, sizes, upper), in_specs=[pl....  7.58 us
    pallas_call x2, Pallas kernels, back_project(): pl.pallas_call(functools.partial(back_body, places, len(given), rows), in...  6.57 us
    pallas_call x2, Pallas kernels, query_terms(): pl.pallas_call(functools.partial(query_terms_body, places), in_specs=[pl....  6.21 us
    pallas_call x1, Pallas kernels, project(): pl.pallas_call(functools.partial(project_body, parts), in_specs=[pl.Block...  4.89 us
    pallas_call x2, Pallas kernels, stats(): pl.pallas_call(functools.partial(stats_body, sizes, upper), in_specs=[pl....  4.81 us
  transfers between devices with their start and end apart: 27, of which 13 were waited for; matrix products, arithmetic and copies ran while one was open for 0% of the time, Pallas kernels for 27%

commit v1 on v0

--- a/solution.py
+++ b/solution.py
@@ -16,6 +16,7 @@
 MIB = 1 << 20
 COST = 0
 AT_ONCE = 4
+PARTS = 2
 VMEM = pltpu.VMEM
 HBM = pltpu.HBM
 
@@ -156,18 +157,23 @@
     out_ref, w_ref = refs.pop(), refs.pop()
     me = lax.axis_index("head")
     depth = w.shape[2]
-    copies = [
-        fetch(w_ref.at[:, pl.ds(pl.multiple_of((me ^ k) * depth, depth), depth)], w.at[i], sems.at[i])
-        for i, k in enumerate(places)
-    ]
+    step = depth // PARTS
+    copies = {}
+    for i, k in enumerate(places):
+        for j in range(PARTS):
+            columns = pl.ds(pl.multiple_of((me ^ k) * depth + j * step, step), step)
+            part = slice(j * step, (j + 1) * step)
+            copies[i, j] = fetch(w_ref.at[:, columns], w.at[i, :, part], sems.at[i, j])
     total = refs.pop(0)[...] if given else None
-    for i, copy in enumerate(copies):
+    for i in range(len(places)):
         x = refs.pop(0)[...]
         if x.shape[0] < rows:
             x = jnp.concatenate([x, refs.pop(0)[...]], axis=0)
-        copy.wait()
-        term = mm_nt(x, w[i])
-        total = term if total is None else total + term
+        for j in range(PARTS):
+            copies[i, j].wait()
+            part = slice(j * step, (j + 1) * step)
+            term = mm_nt(x[:, part], w[i, :, part])
+            total = term if total is None else total + term
     out_ref[...] = total.astype(out_ref.dtype)
 
 
@@ -183,7 +189,7 @@
         out_shape=jax.ShapeDtypeStruct((rows, w.shape[0]), dtype),
         scratch_shapes=[
             VMEM((len(places), w.shape[0], depth), w.dtype),
-            pltpu.SemaphoreType.DMA((len(places),)),
+            pltpu.SemaphoreType.DMA((len(places), PARTS)),
         ],
         compiler_params=params(),
         cost_estimate=cost(3.4),
@@ -194,15 +200,21 @@
 def query_terms_body(places, upper_ref, lower_ref, w_ref, upper_out, lower_out, w, sems):
     me = lax.axis_index("head")
     share = w.shape[1]
-    copies = [
-        fetch(w_ref.at[pl.ds(pl.multiple_of((me ^ k) * share, share), share)], w.at[i], sems.at[i])
-        for i, k in enumerate(places)
-    ]
+    step = w.shape[2] // PARTS
+    parts = [slice(j * step, (j + 1) * step) for j in range(PARTS)]
+    copies = {}
+    for i, k in enumerate(places):
+        rows = pl.ds(pl.multiple_of((me ^ k) * share, share), share)
+        for j, part in enumerate(parts):
+            copies[i, j] = fetch(w_ref.at[rows, part], w.at[i, :, part], sems.at[i, j])
     half = upper_ref.shape[0]
     x = jnp.concatenate([upper_ref[...], lower_ref[...]], axis=0)
-    for i, copy in enumerate(copies):
-        copy.wait()
-        total = mm_nt(x, w[i])
+    for i in range(len(places)):
+        total = None
+        for j, part in enumerate(parts):
+            copies[i, j].wait()
+            term = mm_nt(x[:, part], w[i, :, part])
+            total = term if total is None else total + term
         upper_out[i] = total[:half]
         lower_out[i] = total[half:]
 
@@ -218,7 +230,7 @@
         out_shape=[jax.ShapeDtypeStruct((size, rows, share), jnp.float32)] * 2,
         scratch_shapes=[
             VMEM((size, share, depth), w.dtype),
-            pltpu.SemaphoreType.DMA((size,)),
+            pltpu.SemaphoreType.DMA((size, PARTS)),
         ],
         compiler_params=params(),
         cost_estimate=cost(4.6),
@@ -376,13 +388,15 @@
 
 def stats_body(sizes, upper, order, lengths, q_ref, *refs):
     peers, half, groups, share, dim, docs = sizes
-    blocks = refs[:peers]
-    level_ref, mixed_ref, held, kept, places = refs[peers:]
+    if upper:
+        level_ref, mixed_ref, held, kept, places = refs[peers:]
+        load_blocks(refs[:peers], held)
+    else:
+        held, level_ref, mixed_ref, kept, places = refs
     me = lax.axis_index("ctx")
     width = groups * dim
     factor = math.log2(math.e) / math.sqrt(dim)
     find_places(order, places, me, 2 * peers)
-    load_blocks(blocks, held)
     columns = share * half
     at = upper_half(order)
     j = at if upper else 1 - at
@@ -437,14 +451,14 @@
     return pl.pallas_call(
         functools.partial(stats_body, sizes, upper),
         in_specs=[pl.BlockSpec(memory_space=pltpu.SMEM)] * 2
-        + [pl.BlockSpec(memory_space=VMEM)] * (1 + peers),
-        out_specs=[pl.BlockSpec(memory_space=VMEM)] * 2,
+        + [pl.BlockSpec(memory_space=VMEM)] * (1 + len(blocks)),
+        out_specs=[pl.BlockSpec(memory_space=VMEM)] * (3 if upper else 2),
         out_shape=[
             jax.ShapeDtypeStruct((groups, 1, columns), jnp.float32),
             jax.ShapeDtypeStruct((groups, dim, columns), jnp.float32),
-        ],
+        ]
+        + [jax.ShapeDtypeStruct((2 * peers * half, 2 * groups * dim), jnp.bfloat16)] * upper,
         scratch_shapes=[
-            VMEM((2 * peers * half, 2 * groups * dim), jnp.bfloat16),
             VMEM((groups, (2 * peers + AT_ONCE) * half, columns), jnp.float32),
             pltpu.SMEM((2 * peers,), jnp.int32),
         ],
@@ -458,17 +472,14 @@
     peers, half, groups, share, dim, docs = sizes
     spans = 2 * peers
     if upper:
-        blocks = refs[:peers]
-        dq_ref, even_ref, *odd_refs, rest_ref, held, sums, places = refs[peers:]
+        held, dq_ref, even_ref, *odd_refs, rest_ref, sums, places = refs
     else:
-        rest_ref, blocks = refs[0], refs[1 : 1 + peers]
-        dq_ref, even_ref, *odd_refs, held, sums, places = refs[1 + peers :]
+        rest_ref, held, dq_ref, even_ref, *odd_refs, sums, places = refs
     me = lax.axis_index("ctx")
     width = groups * dim
     scale = 1.0 / math.sqrt(dim)
     factor = math.log2(math.e) * scale
     find_places(order, places, me, spans)
-    load_blocks(blocks, held)
     columns = share * half
     at = upper_half(order)
     j = at if upper else 1 - at
@@ -548,7 +559,6 @@
         out_specs=[pl.BlockSpec(memory_space=VMEM)] * len(outs),
         out_shape=outs,
         scratch_shapes=[
-            VMEM((peers * tokens, 2 * width), jnp.bfloat16),
             VMEM(((2 if upper else 1) * peers * half, 2 * width), jnp.float32),
             pltpu.SMEM((2 * peers,), jnp.int32),
         ],
@@ -658,25 +668,25 @@
     while bit > 1:
         far = [got | {k ^ bit: swap(x, bit, "head") for k, x in got.items()} for got in far]
         bit //= 2
-    near = swap(out_grad, 1, "head")
+    near = [swap(out_grad[:half], 1, "head"), swap(out_grad[half:], 1, "head")]
     own = turn(project_kv, inputs, w_key, value_projection)
-    near_blocks, far[0] = gather_even(own, "ctx", far[0])
+    near_blocks, (far[0], near[0]) = gather_even(own, "ctx", (far[0], near[0]))
     query = turn(project, inputs, w_query)
     query, near_blocks = lax.optimization_barrier((query, near_blocks))
     blocks = (*near_blocks, *[swap(block, 1, "ctx") for block in near_blocks])
-    query, far[1], near = lax.optimization_barrier((query, far[1], near))
-    upper_stats = attend(True, stats, query, *blocks)
-    lower_stats = attend(False, stats, query, *blocks)
+    query, far[1], near[1] = lax.optimization_barrier((query, far[1], near[1]))
+    *upper_stats, held = attend(True, stats, query, *blocks)
+    lower_stats = attend(False, stats, query, held)
     passed = [{k ^ 1: swap(x, 1, "head") for k, x in got.items() if k} for got in far]
-    firsts = {0: (out_grad,), 1: (near,)}
+    firsts = {0: (out_grad,), 1: tuple(near)}
     firsts |= {k: (far[0][k], far[1][k]) for k in range(2, heads, 2)}
     lasts = {k: (passed[0][k], passed[1][k]) for k in range(3, heads, 2)}
     total = context(list(firsts.values()), list(firsts), None, jnp.float32)
     context_grad = context(list(lasts.values()), list(lasts), total, jnp.bfloat16)
-    upper_dq, even, *odd, rest = attend(True, grads, query, context_grad, *upper_stats, *blocks)
+    upper_dq, even, *odd, rest = attend(True, grads, query, context_grad, *upper_stats, held)
     upper = scatter_ctx(turn(pair_sums, even, *[swap(x, 1, "ctx") for x in odd]))
     lower_dq, even, *odd = attend(
-        False, grads, query, context_grad, *lower_stats, rest, *blocks
+        False, grads, query, context_grad, *lower_stats, rest, held
     )
     sides = [list(range(heads - 1, 0, -2)), list(range(heads - 2, -1, -2))]
 
@@ -694,8 +704,8 @@
     upper_got = send_first(None, terms_of(first[0][0], upper, sides[0], True))
     lower = scatter_ctx(turn(pair_sums, even, *lower_odd))
     first.append(firsts_of(sides[1]))
+    lower_got = send_first(terms_of(first[0][1], lower, sides[0]), None)
     upper = send_rest(terms_of(first[1][0], upper, sides[1]), upper_got)
-    lower_got = send_first(terms_of(first[0][1], lower, sides[0]), None)
     lower = send_rest(terms_of(first[1][1], lower, sides[1]), lower_got)
     return join_rows(upper, lower, span_order)
 

time: 114 us -> 108 us (0.947)
  waiting for transfers between devices: 41.2 us -> 34.9 us
  starting transfers between devices: 26.3 us -> 30.5 us
  Pallas kernels: 44.1 us -> 40.7 us
    ppermute x27 -> x28, waiting for transfers between devices: 41.2 us -> 34.9 us  [swap(): lax.ppermute(x, axis, [(i, i ^ k) for i in range(lax.axis_size(axis))])]
    ppermute x27 -> x28, starting transfers between devices: 26.3 us -> 30.5 us  [swap(): lax.ppermute(x, axis, [(i, i ^ k) for i in range(lax.axis_size(axis))])]
    pallas_call x2, Pallas kernels: 7.58 us -> 5.83 us  [grads(): pl.pallas_call(functools.partial(grads_body, sizes, upper), in_specs=[pl....]
  transfers between devices with their start and end apart: 27 -> 28, of which waited for: 13 -> 11; matrix products, arithmetic and copies ran while one was open for 0% -> 0% of each run, Pallas kernels for 27% -> 32%
where the time goes in v1:
time: 108 us; the launch traced here: 107 us
  Pallas kernels  40.7 us (38%)
  waiting for transfers between devices  34.9 us (32%)
  starting transfers between devices  30.5 us (28%)
  local copies, waits for them, and re-layouts  1.08 us (1%)
    ppermute x28, waiting for transfers between devices, swap(): lax.ppermute(x, axis, [(i, i ^ k) for i in range(lax.axis_size(axis))])  34.9 us
    ppermute x28, starting transfers between devices, swap(): lax.ppermute(x, axis, [(i, i ^ k) for i in range(lax.axis_size(axis))])  30.5 us
    pallas_call x4, Pallas kernels, all_terms(): pl.pallas_call(functools.partial(all_terms_body, places, len(terms)), in_...  8.79 us
    pallas_call x2, Pallas kernels, query_terms(): pl.pallas_call(functools.partial(query_terms_body, places), in_specs=[pl....  6.3 us
    pallas_call x2, Pallas kernels, back_project(): pl.pallas_call(functools.partial(back_body, places, len(given), rows), in...  5.93 us
    pallas_call x2, Pallas kernels, grads(): pl.pallas_call(functools.partial(grads_body, sizes, upper), in_specs=[pl....  5.83 us
    pallas_call x1, Pallas kernels, project(): pl.pallas_call(functools.partial(project_body, parts), in_specs=[pl.Block...  4.87 us
    pallas_call x2, Pallas kernels, stats(): pl.pallas_call(functools.partial(stats_body, sizes, upper), in_specs=[pl....  3.74 us
  transfers between devices with their start and end apart: 28, of which 11 were waited for; matrix products, arithmetic and copies ran while one was open for 0% of the time, Pallas kernels for 32%

profile of v1, /device:TPU:0, one launch (start us, length us, event | category | flops | bytes accessed | tf_op | source)
XLA Modules:
  0.0 107.5 jit_solution(7496556586453835801)
XLA Ops:
  0.0 1.1 fusion
  1.1 3.1 %collective-permute-start.2 = (bf16[128,1024]{1,0:T(8,128)(2,1)S(1)}, bf16[128,1024]{1,0:T(8,128)(2,1)S(1)}, u32[]{:S(2)}, u32[]{:S(2)}) collective-permute-start(bf16[128,1024]{1,0:T(8,128)(2,1)S(1)} %get-tuple-element.234), channel_id=1, source_target_pairs={{0,8},{8,0},{16,24},{24,16},{1,9},{9,1},{17,25},{25,17},{2,10},{10... | collective-permute-start | bytes 786440 | tf_op jit(solution)/shard_map/ppermute | solution.py:572
  4.2 2.6 %collective-permute-start.1 = (bf16[128,1024]{1,0:T(8,128)(2,1)S(1)}, bf16[128,1024]{1,0:T(8,128)(2,1)S(1)}, u32[]{:S(2)}, u32[]{:S(2)}) collective-permute-start(bf16[128,1024]{1,0:T(8,128)(2,1)S(1)} %get-tuple-element.234), channel_id=1, source_target_pairs={{0,16},{8,24},{16,0},{24,8},{1,17},{9,25},{17,1},{25,9},{2,18},{10... | collective-permute-start | bytes 786440 | tf_op jit(solution)/shard_map/ppermute | solution.py:572
  6.7 3.3 %project_kv.1.refs_0_ = bf16[256,512]{1,0:T(8,128)(2,1)S(1)} custom-call(bf16[256,4096]{1,0:T(8,128)(2,1)} %x_ref.1, bf16[4096,256]{1,0:T(8,128)(2,1)} %refs_4_.7, bf16[4096,256]{1,0:T(8,128)(2,1)} %refs_5_.9), custom_call_target="tpu_custom_call" | custom-call | bytes 1 | tf_op jit(solution)/shard_map/project_kv/pallas_call | solution.py:91
  10.1 1.6 %collective-permute-start = (bf16[256,512]{1,0:T(8,128)(2,1)S(1)}, bf16[256,512]{1,0:T(8,128)(2,1)S(1)}, u32[]{:S(2)}, u32[]{:S(2)}) collective-permute-start(bf16[256,512]{1,0:T(8,128)(2,1)S(1)} %project_kv.1.refs_0_), channel_id=1, source_target_pairs={{0,2},{1,3},{2,0},{3,1},{4,6},{5,7},{6,4},{7,5},{8,10},{9,11},{10,... | collective-permute-start | bytes 786440 | tf_op jit(solution)/shard_map/ppermute | solution.py:572
  11.6 1.5 %collective-permute-start.4 = (bf16[256,512]{1,0:T(8,128)(2,1)S(1)}, bf16[256,512]{1,0:T(8,128)(2,1)S(1)}, u32[]{:S(2)}, u32[]{:S(2)}) collective-permute-start(bf16[256,512]{1,0:T(8,128)(2,1)S(1)} %project_kv.1.refs_0_), channel_id=1, source_target_pairs={{0,4},{1,5},{2,6},{3,7},{4,0},{5,1},{6,2},{7,3},{8,12},{9,13},{10,... | collective-permute-start | bytes 786440 | tf_op jit(solution)/shard_map/ppermute | solution.py:572
  13.2 2.8 %collective-permute-done.2.refs_1_ = bf16[128,1024]{1,0:T(8,128)(2,1)S(1)} collective-permute-done((bf16[128,1024]{1,0:T(8,128)(2,1)S(1)}, bf16[128,1024]{1,0:T(8,128)(2,1)S(1)}, u32[]{:S(2)}, u32[]{:S(2)}) %collective-permute-start.2) | collective-permute-done | bytes 262176 | tf_op jit(solution)/shard_map/ppermute | solution.py:572
  16.0 2.5 %collective-permute-done.1.refs_3_ = bf16[128,1024]{1,0:T(8,128)(2,1)S(1)} collective-permute-done((bf16[128,1024]{1,0:T(8,128)(2,1)S(1)}, bf16[128,1024]{1,0:T(8,128)(2,1)S(1)}, u32[]{:S(2)}, u32[]{:S(2)}) %collective-permute-start.1) | collective-permute-done | bytes 262176 | tf_op jit(solution)/shard_map/ppermute | solution.py:572
  18.5 1.5 %collective-permute-start.5 = (bf16[256,512]{1,0:T(8,128)(2,1)S(1)}, bf16[256,512]{1,0:T(8,128)(2,1)S(1)}, u32[]{:S(2)}, u32[]{:S(2)}) collective-permute-start(bf16[256,512]{1,0:T(8,128)(2,1)S(1)} %collective-permute-done.refs_1_), channel_id=1, source_target_pairs={{0,4},{1,5},{2,6},{3,7},{4,0},{5,1},{6,2},{7,3},{8,12},{9,13},{10,... | collective-permute-start | bytes 786440 | tf_op jit(solution)/shard_map/ppermute | solution.py:572
  20.0 0.4 collective-permute-start.7
  20.5 2.6 %collective-permute-start.6 = (bf16[128,1024]{1,0:T(8,128)(2,1)S(1)}, bf16[128,1024]{1,0:T(8,128)(2,1)S(1)}, u32[]{:S(2)}, u32[]{:S(2)}) collective-permute-start(bf16[128,1024]{1,0:T(8,128)(2,1)S(1)} %get-tuple-element.233), channel_id=1, source_target_pairs={{0,16},{8,24},{16,0},{24,8},{1,17},{9,25},{17,1},{25,9},{2,18},{10... | collective-permute-start | bytes 786440 | tf_op jit(solution)/shard_map/ppermute | solution.py:572
  23.1 4.9 %project.1.q_ref = bf16[256,1024]{1,0:T(8,128)(2,1)S(1)} custom-call(bf16[256,4096]{1,0:T(8,128)(2,1)} %x_ref.1, bf16[4096,1024]{1,0:T(8,128)(2,1)} %w_ref.4), custom_call_target="tpu_custom_call" | custom-call | bytes 1 | tf_op jit(solution)/shard_map/project/pallas_call | solution.py:137
  28.1 0.5 collective-permute-start.10
  28.7 1.2 %collective-permute-done.7.refs_2_ = bf16[128,1024]{1,0:T(8,128)(2,1)S(1)} collective-permute-done((bf16[128,1024]{1,0:T(8,128)(2,1)S(1)}, bf16[128,1024]{1,0:T(8,128)(2,1)S(1)}, u32[]{:S(2)}, u32[]{:S(2)}) %collective-permute-start.7) | collective-permute-done | bytes 262176 | tf_op jit(solution)/shard_map/ppermute | solution.py:572
  29.8 3.8 %collective-permute-done.6.refs_4_ = bf16[128,1024]{1,0:T(8,128)(2,1)S(1)} collective-permute-done((bf16[128,1024]{1,0:T(8,128)(2,1)S(1)}, bf16[128,1024]{1,0:T(8,128)(2,1)S(1)}, u32[]{:S(2)}, u32[]{:S(2)}) %collective-permute-start.6) | collective-permute-done | bytes 262176 | tf_op jit(solution)/shard_map/ppermute | solution.py:572
  33.7 2.0 %collective-permute-start.8 = (bf16[128,1024]{1,0:T(8,128)(2,1)S(1)}, bf16[128,1024]{1,0:T(8,128)(2,1)S(1)}, u32[]{:S(2)}, u32[]{:S(2)}) collective-permute-start(bf16[128,1024]{1,0:T(8,128)(2,1)S(1)} %collective-permute-done.6.refs_4_), channel_id=1, source_target_pairs={{0,8},{8,0},{16,24},{24,16},{1,9},{9,1},{17,25},{25,17},{2,10},{10... | collective-permute-start | bytes 786440 | tf_op jit(solution)/shard_map/ppermute | solution.py:572
  35.7 1.9 %upper_stats.1 = (f32[2,1,512]{2,1,0:T(1,128)S(1)}, f32[2,128,512]{2,1,0:T(8,128)S(1)}, bf16[2048,512]{1,0:T(8,128)(2,1)S(1)}) custom-call(s32[16]{0:T(128)S(1)} %copy-done.1, s32[8]{0:T(128)S(1)} %copy-done.2, bf16[256,1024]{1,0:T(8,128)(2,1)S(1)} %project.1.q_ref, bf16[256,512]{1,0:T(8,128)(2,1)S(1)} %project_kv.1.refs_0_, ...), custom_call_target="tpu_custom_call" | custom-call | bytes 1 | tf_op jit(solution)/shard_map/upper_stats/pallas_call | solution.py:451
  37.6 1.8 %lower_stats.1 = (f32[2,1,512]{2,1,0:T(1,128)S(1)}, f32[2,128,512]{2,1,0:T(8,128)S(1)}) custom-call(s32[16]{0:T(128)S(1)} %copy-done.1, s32[8]{0:T(128)S(1)} %copy-done.2, bf16[256,1024]{1,0:T(8,128)(2,1)S(1)} %project.1.q_ref, bf16[2048,512]{1,0:T(8,128)(2,1)S(1)} %get-tuple-element.180.refs_0_.refs_1_), custom_call_target="tpu_custom_call" | custom-call | bytes 1 | tf_op jit(solution)/shard_map/lower_stats/pallas_call | solution.py:451
  39.5 3.8 %context_grad.2.refs_0_ = f32[256,1024]{1,0:T(8,128)S(1)} custom-call(bf16[256,1024]{1,0:T(8,128)(2,1)S(1)} %copy-done, bf16[128,1024]{1,0:T(8,128)(2,1)S(1)} %collective-permute-done.2.refs_1_, bf16[128,1024]{1,0:T(8,128)(2,1)S(1)} %collective-permute-done.7.refs_2_, bf16[128,1024]{1,0:T(8,128)(2,1)S(1)} %collective-permute-done.1.refs_3_, ...), custom_call_target="tpu_custom_call" | custom-call | bytes 1 | tf_op jit(solution)/shard_map/context_grad/pallas_call | solution.py:184
  43.3 1.5 %collective-permute-done.8.refs_2_ = bf16[128,1024]{1,0:T(8,128)(2,1)S(1)} collective-permute-done((bf16[128,1024]{1,0:T(8,128)(2,1)S(1)}, bf16[128,1024]{1,0:T(8,128)(2,1)S(1)}, u32[]{:S(2)}, u32[]{:S(2)}) %collective-permute-start.8) | collective-permute-done | bytes 262176 | tf_op jit(solution)/shard_map/ppermute | solution.py:572
  44.8 2.1 %context_grad.3.g_ref = bf16[256,1024]{1,0:T(8,128)(2,1)S(1)} custom-call(f32[256,1024]{1,0:T(8,128)S(1)} %context_grad.2.refs_0_, bf16[128,1024]{1,0:T(8,128)(2,1)S(1)} %collective-permute-done.3.refs_1_, bf16[128,1024]{1,0:T(8,128)(2,1)S(1)} %collective-permute-done.8.refs_2_, bf16[1024,4096]{1,0:T(8,128)(2,1)} %refs_3_.1), custom_call_target="tpu_custom_call" | custom-call | bytes 1 | tf_op jit(solution)/shard_map/context_grad/pallas_call | solution.py:184
  46.9 3.0 %upper_grads.1 = (bf16[128,1024]{1,0:T(8,128)(2,1)S(1)}, bf16[4,128,512]{2,1,0:T(8,128)(2,1)S(1)}, bf16[2,128,512]{2,1,0:T(8,128)(2,1)S(1)}, bf16[2,128,512]{2,1,0:T(8,128)(2,1)S(1)}, f32[1024,512]{1,0:T(8,128)S(1)}) custom-call(s32[16]{0:T(128)S(1)} %copy-done.1, s32[8]{0:T(128)S(1)} %copy-done.2, bf16[256,1024]{1,0:T(8,128)(2,1)S(1)} %project.1.q_ref, ...), custom_call_target="tpu_custom_call" | custom-call | bytes 1 | tf_op jit(solution)/shard_map/upper_grads/pallas_call | solution.py:555
  50.0 0.5 collective-permute-start.14
  50.5 1.0 collective-permute-done.13.refs_0_
  51.5 0.4 collective-permute-done.14.refs_1_
  51.9 0.1 pair_sums.2
  52.0 1.6 %collective-permute-start.15 = (bf16[128,512]{1,0:T(8,128)(2,1)S(1)}, bf16[128,512]{1,0:T(8,128)(2,1)S(1)}, u32[]{:S(2)}, u32[]{:S(2)}) collective-permute-start(bf16[128,512]{1,0:T(8,128)(2,1)S(1)} %get-tuple-element.185), channel_id=1, source_target_pairs={{0,2},{1,3},{2,0},{3,1},{4,6},{5,7},{6,4},{7,5},{8,10},{9,11},{10,... | collective-permute-start | bytes 393224 | tf_op jit(solution)/shard_map/ppermute | solution.py:572
  53.6 0.9 collective-permute-start.16
  54.5 1.1 %collective-permute-start.17 = (bf16[128,512]{1,0:T(8,128)(2,1)S(1)}, bf16[128,512]{1,0:T(8,128)(2,1)S(1)}, u32[]{:S(2)}, u32[]{:S(2)}) collective-permute-start(bf16[128,512]{1,0:T(8,128)(2,1)S(1)} %get-tuple-element.187), channel_id=1, source_target_pairs={{0,6},{1,7},{2,4},{3,5},{4,2},{5,3},{6,0},{7,1},{8,14},{9,15},{10,... | collective-permute-start | bytes 393224 | tf_op jit(solution)/shard_map/ppermute | solution.py:572
  55.6 2.9 %lower_grads.1 = (bf16[128,1024]{1,0:T(8,128)(2,1)S(1)}, bf16[4,128,512]{2,1,0:T(8,128)(2,1)S(1)}, bf16[2,128,512]{2,1,0:T(8,128)(2,1)S(1)}, bf16[2,128,512]{2,1,0:T(8,128)(2,1)S(1)}) custom-call(s32[16]{0:T(128)S(1)} %copy-done.1, s32[8]{0:T(128)S(1)} %copy-done.2, bf16[256,1024]{1,0:T(8,128)(2,1)S(1)} %project.1.q_ref, ...), custom_call_target="tpu_custom_call" | custom-call | bytes 1 | tf_op jit(solution)/shard_map/lower_grads/pallas_call | solution.py:555
  58.4 0.9 collective-permute-start.18
  59.4 3.2 %query_terms.2 = (f32[2,128,1024]{2,1,0:T(8,128)S(1)}, f32[2,128,1024]{2,1,0:T(8,128)S(1)}) custom-call(bf16[128,1024]{1,0:T(8,128)(2,1)S(1)} %get-tuple-element.200.upper_ref, bf16[128,1024]{1,0:T(8,128)(2,1)S(1)} %get-tuple-element.201.lower_ref, bf16[4096,1024]{1,0:T(8,128)(2,1)} %w_ref.4), custom_call_target="tpu_custom_call" | custom-call | bytes 1 | tf_op jit(solution)/shard_map/query_terms/pallas_call | solution.py:226
  62.6 2.2 %all_terms.4 = bf16[2,128,1024]{2,1,0:T(8,128)(2,1)S(1)} custom-call(f32[2,128,1024]{2,1,0:T(8,128)S(1)} %get-tuple-element.188.first_ref, bf16[128,512]{1,0:T(8,128)(2,1)S(1)} %get-tuple-element.214.refs_0_, bf16[128,512]{1,0:T(8,128)(2,1)S(1)} %collective-permute-done.15.refs_1_, bf16[128,512]{1,0:T(8,128)(2,1)S(1)} %collective-permute-done.16.refs_2_, ...), custom_call_target="tpu_custom_call" | custom-call | bytes 1 | tf_op jit(solution)/shard_map/all_terms/pallas_call | solution.py:271
  64.9 0.1 pair_sums.3
  65.0 1.2 %collective-permute-start.20 = (bf16[128,512]{1,0:T(8,128)(2,1)S(1)}, bf16[128,512]{1,0:T(8,128)(2,1)S(1)}, u32[]{:S(2)}, u32[]{:S(2)}) collective-permute-start(bf16[128,512]{1,0:T(8,128)(2,1)S(1)} %get-tuple-element.204), channel_id=1, source_target_pairs={{0,2},{1,3},{2,0},{3,1},{4,6},{5,7},{6,4},{7,5},{8,10},{9,11},{10,... | collective-permute-start | bytes 393224 | tf_op jit(solution)/shard_map/ppermute | solution.py:572
  66.2 2.8 %collective-permute-start.21 = (bf16[128,512]{1,0:T(8,128)(2,1)S(1)}, bf16[128,512]{1,0:T(8,128)(2,1)S(1)}, u32[]{:S(2)}, u32[]{:S(2)}) collective-permute-start(bf16[128,512]{1,0:T(8,128)(2,1)S(1)} %get-tuple-element.205), channel_id=1, source_target_pairs={{0,4},{1,5},{2,6},{3,7},{4,0},{5,1},{6,2},{7,3},{8,12},{9,13},{10,... | collective-permute-start | bytes 393224 | tf_op jit(solution)/shard_map/ppermute | solution.py:572
  68.9 3.1 %query_terms.3 = (f32[2,128,1024]{2,1,0:T(8,128)S(1)}, f32[2,128,1024]{2,1,0:T(8,128)S(1)}) custom-call(bf16[128,1024]{1,0:T(8,128)(2,1)S(1)} %get-tuple-element.200.upper_ref, bf16[128,1024]{1,0:T(8,128)(2,1)S(1)} %get-tuple-element.201.lower_ref, bf16[4096,1024]{1,0:T(8,128)(2,1)} %w_ref.4), custom_call_target="tpu_custom_call" | custom-call | bytes 1 | tf_op jit(solution)/shard_map/query_terms/pallas_call | solution.py:226
  72.1 2.8 %collective-permute-done.21.refs_2_ = bf16[128,512]{1,0:T(8,128)(2,1)S(1)} collective-permute-done((bf16[128,512]{1,0:T(8,128)(2,1)S(1)}, bf16[128,512]{1,0:T(8,128)(2,1)S(1)}, u32[]{:S(2)}, u32[]{:S(2)}) %collective-permute-start.21) | collective-permute-done | bytes 131104 | tf_op jit(solution)/shard_map/ppermute | solution.py:572
  74.9 2.2 %all_terms.5 = (bf16[128,1024]{1,0:T(8,128)(2,1)S(1)}, bf16[128,1024]{1,0:T(8,128)(2,1)S(1)}) custom-call(f32[2,128,1024]{2,1,0:T(8,128)S(1)} %get-tuple-element.207.first_ref, bf16[128,512]{1,0:T(8,128)(2,1)S(1)} %get-tuple-element.224.refs_0_, bf16[128,512]{1,0:T(8,128)(2,1)S(1)} %collective-permute-done.20.refs_1_, ...), custom_call_target="tpu_custom_call" | custom-call | bytes 1 | tf_op jit(solution)/shard_map/all_terms/pallas_call | solution.py:271
  77.1 1.7 %collective-permute-start.26 = (bf16[128,1024]{1,0:T(8,128)(2,1)S(1)}, bf16[128,1024]{1,0:T(8,128)(2,1)S(1)}, u32[]{:S(2)}, u32[]{:S(2)}) collective-permute-start(bf16[128,1024]{1,0:T(8,128)(2,1)S(1)} %get-tuple-element.212), channel_id=1, source_target_pairs={{0,8},{8,0},{16,24},{24,16},{1,9},{9,1},{17,25},{25,17},{2,10},{10... | collective-permute-start | bytes 786440 | tf_op jit(solution)/shard_map/ppermute | solution.py:572
  78.9 0.4 collective-permute-start.25
  79.2 2.2 %all_terms.6 = (bf16[128,1024]{1,0:T(8,128)(2,1)S(1)}, bf16[128,1024]{1,0:T(8,128)(2,1)S(1)}) custom-call(f32[2,128,1024]{2,1,0:T(8,128)S(1)} %get-tuple-element.213.first_ref, bf16[128,512]{1,0:T(8,128)(2,1)S(1)} %get-tuple-element.214.refs_0_, bf16[128,512]{1,0:T(8,128)(2,1)S(1)} %collective-permute-done.15.refs_1_, ...), custom_call_target="tpu_custom_call" | custom-call | bytes 1 | tf_op jit(solution)/shard_map/all_terms/pallas_call | solution.py:271
  81.5 3.2 %collective-permute-start.24 = (bf16[128,1024]{1,0:T(8,128)(2,1)S(1)}, bf16[128,1024]{1,0:T(8,128)(2,1)S(1)}, u32[]{:S(2)}, u32[]{:S(2)}) collective-permute-start(bf16[128,1024]{1,0:T(8,128)(2,1)S(1)} %add.2), channel_id=1, source_target_pairs={{0,16},{8,24},{16,0},{24,8},{1,17},{9,25},{17,1},{25,9},{2,18},{10... | collective-permute-start | bytes 786440 | tf_op jit(solution)/shard_map/ppermute | solution.py:572
  84.7 2.2 %all_terms.7 = (bf16[128,1024]{1,0:T(8,128)(2,1)S(1)}, bf16[128,1024]{1,0:T(8,128)(2,1)S(1)}) custom-call(f32[2,128,1024]{2,1,0:T(8,128)S(1)} %get-tuple-element.223.first_ref, bf16[128,512]{1,0:T(8,128)(2,1)S(1)} %get-tuple-element.224.refs_0_, bf16[128,512]{1,0:T(8,128)(2,1)S(1)} %collective-permute-done.20.refs_1_, ...), custom_call_target="tpu_custom_call" | custom-call | bytes 1 | tf_op jit(solution)/shard_map/all_terms/pallas_call | solution.py:271
  86.9 7.9 %collective-permute-done.26.b_ref = bf16[128,1024]{1,0:T(8,128)(2,1)S(1)} collective-permute-done((bf16[128,1024]{1,0:T(8,128)(2,1)S(1)}, bf16[128,1024]{1,0:T(8,128)(2,1)S(1)}, u32[]{:S(2)}, u32[]{:S(2)}) %collective-permute-start.26) | collective-permute-done | bytes 262176 | tf_op jit(solution)/shard_map/ppermute | solution.py:572
  95.0 3.7 %collective-permute-done.25.refs_4_ = bf16[128,1024]{1,0:T(8,128)(2,1)S(1)} collective-permute-done((bf16[128,1024]{1,0:T(8,128)(2,1)S(1)}, bf16[128,1024]{1,0:T(8,128)(2,1)S(1)}, u32[]{:S(2)}, u32[]{:S(2)}) %collective-permute-start.25) | collective-permute-done | bytes 262176 | tf_op jit(solution)/shard_map/ppermute | solution.py:572
  98.8 7.2 %collective-permute-done.27.refs_5_ = bf16[128,1024]{1,0:T(8,128)(2,1)S(1)} collective-permute-done((bf16[128,1024]{1,0:T(8,128)(2,1)S(1)}, bf16[128,1024]{1,0:T(8,128)(2,1)S(1)}, u32[]{:S(2)}, u32[]{:S(2)}) %collective-permute-start.27) | collective-permute-done | bytes 262176 | tf_op jit(solution)/shard_map/ppermute | solution.py:572
  105.9 1.5 %join_rows.1 = bf16[256,1024]{1,0:T(8,128)(2,1)} custom-call(s32[16]{0:T(128)S(1)} %copy-done.1, bf16[128,1024]{1,0:T(8,128)(2,1)S(1)} %get-tuple-element.218.refs_0_, bf16[2,128,1024]{2,1,0:T(8,128)(2,1)S(1)} %collective-permute-done.23.b_ref.refs_1_, bf16[128,1024]{1,0:T(8,128)(2,1)S(1)} %collective-permute-done.24.refs_2_, ...), custom_call_target="tpu_custom_call" | custom-call | bytes 1 | tf_op jit(solution)/shard_map/join_rows/pallas_call | solution.py:326
  (34 shorter events, 0.6 us)
Async XLA Ops:
  1.1 14.9 %collective-permute-start.2 = (bf16[128,1024]{1,0:T(8,128)(2,1)S(1)}, bf16[128,1024]{1,0:T(8,128)(2,1)S(1)}, u32[]{:S(2)}, u32[]{:S(2)}) collective-permute-start(bf16[128,1024]{1,0:T(8,128)(2,1)S(1)} %get-tuple-element.234), channel_id=1, source_target_pairs={{0,8},{8,0},{16,24},{24,16},{1,9},{9,1},{17,25},{25,17},{2,10},{10... | collective-permute-start | bytes 786440 | tf_op jit(solution)/shard_map/ppermute | solution.py:572
  4.2 14.3 %collective-permute-start.1 = (bf16[128,1024]{1,0:T(8,128)(2,1)S(1)}, bf16[128,1024]{1,0:T(8,128)(2,1)S(1)}, u32[]{:S(2)}, u32[]{:S(2)}) collective-permute-start(bf16[128,1024]{1,0:T(8,128)(2,1)S(1)} %get-tuple-element.234), channel_id=1, source_target_pairs={{0,16},{8,24},{16,0},{24,8},{1,17},{9,25},{17,1},{25,9},{2,18},{10... | collective-permute-start | bytes 786440 | tf_op jit(solution)/shard_map/ppermute | solution.py:572
  10.1 8.4 %collective-permute-start = (bf16[256,512]{1,0:T(8,128)(2,1)S(1)}, bf16[256,512]{1,0:T(8,128)(2,1)S(1)}, u32[]{:S(2)}, u32[]{:S(2)}) collective-permute-start(bf16[256,512]{1,0:T(8,128)(2,1)S(1)} %project_kv.1.refs_0_), channel_id=1, source_target_pairs={{0,2},{1,3},{2,0},{3,1},{4,6},{5,7},{6,4},{7,5},{8,10},{9,11},{10,... | collective-permute-start | bytes 786440 | tf_op jit(solution)/shard_map/ppermute | solution.py:572
  11.6 16.4 %collective-permute-start.4 = (bf16[256,512]{1,0:T(8,128)(2,1)S(1)}, bf16[256,512]{1,0:T(8,128)(2,1)S(1)}, u32[]{:S(2)}, u32[]{:S(2)}) collective-permute-start(bf16[256,512]{1,0:T(8,128)(2,1)S(1)} %project_kv.1.refs_0_), channel_id=1, source_target_pairs={{0,4},{1,5},{2,6},{3,7},{4,0},{5,1},{6,2},{7,3},{8,12},{9,13},{10,... | collective-permute-start | bytes 786440 | tf_op jit(solution)/shard_map/ppermute | solution.py:572
  18.5 9.5 %collective-permute-start.5 = (bf16[256,512]{1,0:T(8,128)(2,1)S(1)}, bf16[256,512]{1,0:T(8,128)(2,1)S(1)}, u32[]{:S(2)}, u32[]{:S(2)}) collective-permute-start(bf16[256,512]{1,0:T(8,128)(2,1)S(1)} %collective-permute-done.refs_1_), channel_id=1, source_target_pairs={{0,4},{1,5},{2,6},{3,7},{4,0},{5,1},{6,2},{7,3},{8,12},{9,13},{10,... | collective-permute-start | bytes 786440 | tf_op jit(solution)/shard_map/ppermute | solution.py:572
  20.0 15.7 %copy-start.1 = (s32[16]{0:T(128)S(1)}, s32[16]{0:T(128)}, u32[]{:S(2)}) copy-start(s32[16]{0:T(128)} %order.9) | copy-start | bytes 196
  20.0 15.7 %copy-start.2 = (s32[8]{0:T(128)S(1)}, s32[8]{0:T(128)}, u32[]{:S(2)}) copy-start(s32[8]{0:T(128)} %lengths.7) | copy-start | bytes 100
  20.0 9.8 %collective-permute-start.7 = (bf16[128,1024]{1,0:T(8,128)(2,1)S(1)}, bf16[128,1024]{1,0:T(8,128)(2,1)S(1)}, u32[]{:S(2)}, u32[]{:S(2)}) collective-permute-start(bf16[128,1024]{1,0:T(8,128)(2,1)S(1)} %get-tuple-element.233), channel_id=1, source_target_pairs={{0,8},{8,0},{16,24},{24,16},{1,9},{9,1},{17,25},{25,17},{2,10},{10... | collective-permute-start | bytes 786440 | tf_op jit(solution)/shard_map/ppermute | solution.py:572
  20.5 13.2 %collective-permute-start.6 = (bf16[128,1024]{1,0:T(8,128)(2,1)S(1)}, bf16[128,1024]{1,0:T(8,128)(2,1)S(1)}, u32[]{:S(2)}, u32[]{:S(2)}) collective-permute-start(bf16[128,1024]{1,0:T(8,128)(2,1)S(1)} %get-tuple-element.233), channel_id=1, source_target_pairs={{0,16},{8,24},{16,0},{24,8},{1,17},{9,25},{17,1},{25,9},{2,18},{10... | collective-permute-start | bytes 786440 | tf_op jit(solution)/shard_map/ppermute | solution.py:572
  28.0 11.5 %copy-start = (bf16[256,1024]{1,0:T(8,128)(2,1)S(1)}, bf16[256,1024]{1,0:T(8,128)(2,1)}, u32[]{:S(2)}) copy-start(bf16[256,1024]{1,0:T(8,128)(2,1)} %refs_0_) | copy-start | bytes 1572868
  28.0 5.6 %collective-permute-start.9 = (bf16[256,512]{1,0:T(8,128)(2,1)S(1)}, bf16[256,512]{1,0:T(8,128)(2,1)S(1)}, u32[]{:S(2)}, u32[]{:S(2)}) collective-permute-start(bf16[256,512]{1,0:T(8,128)(2,1)S(1)} %project_kv.1.refs_0_), channel_id=1, source_target_pairs={{0,1},{1,0},{2,3},{3,2},{4,5},{5,4},{6,7},{7,6},{8,9},{9,8},{10,11... | collective-permute-start | bytes 786440 | tf_op jit(solution)/shard_map/ppermute | solution.py:572
  28.1 7.6 %collective-permute-start.10 = (bf16[256,512]{1,0:T(8,128)(2,1)S(1)}, bf16[256,512]{1,0:T(8,128)(2,1)S(1)}, u32[]{:S(2)}, u32[]{:S(2)}) collective-permute-start(bf16[256,512]{1,0:T(8,128)(2,1)S(1)} %collective-permute-done.refs_1_), channel_id=1, source_target_pairs={{0,1},{1,0},{2,3},{3,2},{4,5},{5,4},{6,7},{7,6},{8,9},{9,8},{10,11... | collective-permute-start | bytes 786440 | tf_op jit(solution)/shard_map/ppermute | solution.py:572
  28.6 7.1 %collective-permute-start.11 = (bf16[256,512]{1,0:T(8,128)(2,1)S(1)}, bf16[256,512]{1,0:T(8,128)(2,1)S(1)}, u32[]{:S(2)}, u32[]{:S(2)}) collective-permute-start(bf16[256,512]{1,0:T(8,128)(2,1)S(1)} %collective-permute-done.4.refs_2_), channel_id=1, source_target_pairs={{0,1},{1,0},{2,3},{3,2},{4,5},{5,4},{6,7},{7,6},{8,9},{9,8},{10,11... | collective-permute-start | bytes 786440 | tf_op jit(solution)/shard_map/ppermute | solution.py:572
  29.8 5.9 %collective-permute-start.12 = (bf16[256,512]{1,0:T(8,128)(2,1)S(1)}, bf16[256,512]{1,0:T(8,128)(2,1)S(1)}, u32[]{:S(2)}, u32[]{:S(2)}) collective-permute-start(bf16[256,512]{1,0:T(8,128)(2,1)S(1)} %collective-permute-done.5.refs_3_), channel_id=1, source_target_pairs={{0,1},{1,0},{2,3},{3,2},{4,5},{5,4},{6,7},{7,6},{8,9},{9,8},{10,11... | collective-permute-start | bytes 786440 | tf_op jit(solution)/shard_map/ppermute | solution.py:572
  33.7 9.7 %collective-permute-start.3 = (bf16[128,1024]{1,0:T(8,128)(2,1)S(1)}, bf16[128,1024]{1,0:T(8,128)(2,1)S(1)}, u32[]{:S(2)}, u32[]{:S(2)}) collective-permute-start(bf16[128,1024]{1,0:T(8,128)(2,1)S(1)} %collective-permute-done.1.refs_3_), channel_id=1, source_target_pairs={{0,8},{8,0},{16,24},{24,16},{1,9},{9,1},{17,25},{25,17},{2,10},{10... | collective-permute-start | bytes 786440 | tf_op jit(solution)/shard_map/ppermute | solution.py:572
  33.7 11.2 %collective-permute-start.8 = (bf16[128,1024]{1,0:T(8,128)(2,1)S(1)}, bf16[128,1024]{1,0:T(8,128)(2,1)S(1)}, u32[]{:S(2)}, u32[]{:S(2)}) collective-permute-start(bf16[128,1024]{1,0:T(8,128)(2,1)S(1)} %collective-permute-done.6.refs_4_), channel_id=1, source_target_pairs={{0,8},{8,0},{16,24},{24,16},{1,9},{9,1},{17,25},{25,17},{2,10},{10... | collective-permute-start | bytes 786440 | tf_op jit(solution)/shard_map/ppermute | solution.py:572
  49.9 1.6 %collective-permute-start.13 = (bf16[2,128,512]{2,1,0:T(8,128)(2,1)S(1)}, bf16[2,128,512]{2,1,0:T(8,128)(2,1)S(1)}, u32[]{:S(2)}, u32[]{:S(2)}) collective-permute-start(bf16[2,128,512]{2,1,0:T(8,128)(2,1)S(1)} %get-tuple-element.167), channel_id=1, source_target_pairs={{0,1},{1,0},{2,3},{3,2},{4,5},{5,4},{6,7},{7,6},{8,9},{9,8},{10,11... | collective-permute-start | bytes 786440 | tf_op jit(solution)/shard_map/ppermute | solution.py:572
  50.0 1.9 %collective-permute-start.14 = (bf16[2,128,512]{2,1,0:T(8,128)(2,1)S(1)}, bf16[2,128,512]{2,1,0:T(8,128)(2,1)S(1)}, u32[]{:S(2)}, u32[]{:S(2)}) collective-permute-start(bf16[2,128,512]{2,1,0:T(8,128)(2,1)S(1)} %get-tuple-element.168), channel_id=1, source_target_pairs={{0,1},{1,0},{2,3},{3,2},{4,5},{5,4},{6,7},{7,6},{8,9},{9,8},{10,11... | collective-permute-start | bytes 786440 | tf_op jit(solution)/shard_map/ppermute | solution.py:572
  52.0 10.5 %collective-permute-start.15 = (bf16[128,512]{1,0:T(8,128)(2,1)S(1)}, bf16[128,512]{1,0:T(8,128)(2,1)S(1)}, u32[]{:S(2)}, u32[]{:S(2)}) collective-permute-start(bf16[128,512]{1,0:T(8,128)(2,1)S(1)} %get-tuple-element.185), channel_id=1, source_target_pairs={{0,2},{1,3},{2,0},{3,1},{4,6},{5,7},{6,4},{7,5},{8,10},{9,11},{10,... | collective-permute-start | bytes 393224 | tf_op jit(solution)/shard_map/ppermute | solution.py:572
  53.6 9.0 %collective-permute-start.16 = (bf16[128,512]{1,0:T(8,128)(2,1)S(1)}, bf16[128,512]{1,0:T(8,128)(2,1)S(1)}, u32[]{:S(2)}, u32[]{:S(2)}) collective-permute-start(bf16[128,512]{1,0:T(8,128)(2,1)S(1)} %get-tuple-element.186), channel_id=1, source_target_pairs={{0,4},{1,5},{2,6},{3,7},{4,0},{5,1},{6,2},{7,3},{8,12},{9,13},{10,... | collective-permute-start | bytes 393224 | tf_op jit(solution)/shard_map/ppermute | solution.py:572
  54.5 8.1 %collective-permute-start.17 = (bf16[128,512]{1,0:T(8,128)(2,1)S(1)}, bf16[128,512]{1,0:T(8,128)(2,1)S(1)}, u32[]{:S(2)}, u32[]{:S(2)}) collective-permute-start(bf16[128,512]{1,0:T(8,128)(2,1)S(1)} %get-tuple-element.187), channel_id=1, source_target_pairs={{0,6},{1,7},{2,4},{3,5},{4,2},{5,3},{6,0},{7,1},{8,14},{9,15},{10,... | collective-permute-start | bytes 393224 | tf_op jit(solution)/shard_map/ppermute | solution.py:572
  58.4 6.4 %collective-permute-start.18 = (bf16[2,128,512]{2,1,0:T(8,128)(2,1)S(1)}, bf16[2,128,512]{2,1,0:T(8,128)(2,1)S(1)}, u32[]{:S(2)}, u32[]{:S(2)}) collective-permute-start(bf16[2,128,512]{2,1,0:T(8,128)(2,1)S(1)} %get-tuple-element.194), channel_id=1, source_target_pairs={{0,1},{1,0},{2,3},{3,2},{4,5},{5,4},{6,7},{7,6},{8,9},{9,8},{10,11... | collective-permute-start | bytes 786440 | tf_op jit(solution)/shard_map/ppermute | solution.py:572
  59.3 5.6 %collective-permute-start.19 = (bf16[2,128,512]{2,1,0:T(8,128)(2,1)S(1)}, bf16[2,128,512]{2,1,0:T(8,128)(2,1)S(1)}, u32[]{:S(2)}, u32[]{:S(2)}) collective-permute-start(bf16[2,128,512]{2,1,0:T(8,128)(2,1)S(1)} %get-tuple-element.195), channel_id=1, source_target_pairs={{0,1},{1,0},{2,3},{3,2},{4,5},{5,4},{6,7},{7,6},{8,9},{9,8},{10,11... | collective-permute-start | bytes 786440 | tf_op jit(solution)/shard_map/ppermute | solution.py:572
  64.8 16.7 %collective-permute-start.23 = (bf16[2,128,1024]{2,1,0:T(8,128)(2,1)S(1)}, bf16[2,128,1024]{2,1,0:T(8,128)(2,1)S(1)}, u32[]{:S(2)}, u32[]{:S(2)}) collective-permute-start(bf16[2,128,1024]{2,1,0:T(8,128)(2,1)S(1)} %all_terms.4), channel_id=1, source_target_pairs={{0,8},{8,0},{16,24},{24,16},{1,9},{9,1},{17,25},{25,17},{2,10},{10... | collective-permute-start | bytes 1572872 | tf_op jit(solution)/shard_map/ppermute | solution.py:572
  65.0 7.1 %collective-permute-start.20 = (bf16[128,512]{1,0:T(8,128)(2,1)S(1)}, bf16[128,512]{1,0:T(8,128)(2,1)S(1)}, u32[]{:S(2)}, u32[]{:S(2)}) collective-permute-start(bf16[128,512]{1,0:T(8,128)(2,1)S(1)} %get-tuple-element.204), channel_id=1, source_target_pairs={{0,2},{1,3},{2,0},{3,1},{4,6},{5,7},{6,4},{7,5},{8,10},{9,11},{10,... | collective-permute-start | bytes 393224 | tf_op jit(solution)/shard_map/ppermute | solution.py:572
  66.2 8.7 %collective-permute-start.21 = (bf16[128,512]{1,0:T(8,128)(2,1)S(1)}, bf16[128,512]{1,0:T(8,128)(2,1)S(1)}, u32[]{:S(2)}, u32[]{:S(2)}) collective-permute-start(bf16[128,512]{1,0:T(8,128)(2,1)S(1)} %get-tuple-element.205), channel_id=1, source_target_pairs={{0,4},{1,5},{2,6},{3,7},{4,0},{5,1},{6,2},{7,3},{8,12},{9,13},{10,... | collective-permute-start | bytes 393224 | tf_op jit(solution)/shard_map/ppermute | solution.py:572
  68.9 6.0 %collective-permute-start.22 = (bf16[128,512]{1,0:T(8,128)(2,1)S(1)}, bf16[128,512]{1,0:T(8,128)(2,1)S(1)}, u32[]{:S(2)}, u32[]{:S(2)}) collective-permute-start(bf16[128,512]{1,0:T(8,128)(2,1)S(1)} %get-tuple-element.206), channel_id=1, source_target_pairs={{0,6},{1,7},{2,4},{3,5},{4,2},{5,3},{6,0},{7,1},{8,14},{9,15},{10,... | collective-permute-start | bytes 393224 | tf_op jit(solution)/shard_map/ppermute | solution.py:572
  77.1 17.7 %collective-permute-start.26 = (bf16[128,1024]{1,0:T(8,128)(2,1)S(1)}, bf16[128,1024]{1,0:T(8,128)(2,1)S(1)}, u32[]{:S(2)}, u32[]{:S(2)}) collective-permute-start(bf16[128,1024]{1,0:T(8,128)(2,1)S(1)} %get-tuple-element.212), channel_id=1, source_target_pairs={{0,8},{8,0},{16,24},{24,16},{1,9},{9,1},{17,25},{25,17},{2,10},{10... | collective-permute-start | bytes 786440 | tf_op jit(solution)/shard_map/ppermute | solution.py:572
  78.9 19.9 %collective-permute-start.25 = (bf16[128,1024]{1,0:T(8,128)(2,1)S(1)}, bf16[128,1024]{1,0:T(8,128)(2,1)S(1)}, u32[]{:S(2)}, u32[]{:S(2)}) collective-permute-start(bf16[128,1024]{1,0:T(8,128)(2,1)S(1)} %get-tuple-element.229), channel_id=1, source_target_pairs={{0,8},{8,0},{16,24},{24,16},{1,9},{9,1},{17,25},{25,17},{2,10},{10... | collective-permute-start | bytes 786440 | tf_op jit(solution)/shard_map/ppermute | solution.py:572
  81.5 17.3 %collective-permute-start.24 = (bf16[128,1024]{1,0:T(8,128)(2,1)S(1)}, bf16[128,1024]{1,0:T(8,128)(2,1)S(1)}, u32[]{:S(2)}, u32[]{:S(2)}) collective-permute-start(bf16[128,1024]{1,0:T(8,128)(2,1)S(1)} %add.2), channel_id=1, source_target_pairs={{0,16},{8,24},{16,0},{24,8},{1,17},{9,25},{17,1},{25,9},{2,18},{10... | collective-permute-start | bytes 786440 | tf_op jit(solution)/shard_map/ppermute | solution.py:572
  94.9 11.0 %collective-permute-start.27 = (bf16[128,1024]{1,0:T(8,128)(2,1)S(1)}, bf16[128,1024]{1,0:T(8,128)(2,1)S(1)}, u32[]{:S(2)}, u32[]{:S(2)}) collective-permute-start(bf16[128,1024]{1,0:T(8,128)(2,1)S(1)} %add.3), channel_id=1, source_target_pairs={{0,16},{8,24},{16,0},{24,8},{1,17},{9,25},{17,1},{25,9},{2,18},{10... | collective-permute-start | bytes 786440 | tf_op jit(solution)/shard_map/ppermute | solution.py:572

commit v2 on v1

--- a/solution.py
+++ b/solution.py
@@ -151,112 +151,113 @@
     )(in_hbm(x), in_hbm(w))
 
 
-def back_body(places, given, rows, *refs):
-    refs = list(refs)
-    sems, w = refs.pop(), refs.pop()
-    out_ref, w_ref = refs.pop(), refs.pop()
-    me = lax.axis_index("head")
-    depth = w.shape[2]
-    step = depth // PARTS
-    copies = {}
-    for i, k in enumerate(places):
-        for j in range(PARTS):
-            columns = pl.ds(pl.multiple_of((me ^ k) * depth + j * step, step), step)
-            part = slice(j * step, (j + 1) * step)
-            copies[i, j] = fetch(w_ref.at[:, columns], w.at[i, :, part], sems.at[i, j])
+def back_body(given, rows, spans, *refs):
+    refs, out_ref = list(refs[:-1]), refs[-1]
     total = refs.pop(0)[...] if given else None
-    for i in range(len(places)):
-        x = refs.pop(0)[...]
-        if x.shape[0] < rows:
-            x = jnp.concatenate([x, refs.pop(0)[...]], axis=0)
-        for j in range(PARTS):
-            copies[i, j].wait()
-            part = slice(j * step, (j + 1) * step)
-            term = mm_nt(x[:, part], w[i, :, part])
+    stacks = [refs.pop() for _ in spans][::-1]
+    for w, (low, high) in zip(stacks, spans):
+        for i in range(low, high):
+            x = refs.pop(0)[...]
+            if x.shape[0] < rows:
+                x = jnp.concatenate([x, refs.pop(0)[...]], axis=0)
+            term = mm_nt(x, w[i])
             total = term if total is None else total + term
     out_ref[...] = total.astype(out_ref.dtype)
 
 
-def back_project(blocks, places, w, total, dtype):
-    rows, depth = blocks[0][0].shape[0] * len(blocks[0]), blocks[0][0].shape[1]
+def back_project(blocks, stacks, spans, total, dtype):
+    rows = blocks[0][0].shape[0] * len(blocks[0])
     given = [] if total is None else [total]
     flat = [x for block in blocks for x in block]
-    return pl.pallas_call(
-        functools.partial(back_body, places, len(given), rows),
-        in_specs=[pl.BlockSpec(memory_space=VMEM)] * (len(given) + len(flat))
-        + [pl.BlockSpec(memory_space=HBM)],
+    operands = (*given, *flat, *stacks)
+    return pl.pallas_call(
+        functools.partial(back_body, len(given), rows, spans),
+        in_specs=[pl.BlockSpec(memory_space=VMEM)] * len(operands),
         out_specs=pl.BlockSpec(memory_space=VMEM),
-        out_shape=jax.ShapeDtypeStruct((rows, w.shape[0]), dtype),
-        scratch_shapes=[
-            VMEM((len(places), w.shape[0], depth), w.dtype),
-            pltpu.SemaphoreType.DMA((len(places), PARTS)),
-        ],
-        compiler_params=params(),
-        cost_estimate=cost(3.4),
+        out_shape=jax.ShapeDtypeStruct((rows, stacks[0].shape[1]), dtype),
+        compiler_params=params(),
+        cost_estimate=cost(3),
         name="context_grad",
-    )(*given, *flat, in_hbm(w))
-
-
-def query_terms_body(places, upper_ref, lower_ref, w_ref, upper_out, lower_out, w, sems):
+    )(*operands)
+
+
+def fetch_columns(places, ref, out, sems):
     me = lax.axis_index("head")
-    share = w.shape[1]
-    step = w.shape[2] // PARTS
-    parts = [slice(j * step, (j + 1) * step) for j in range(PARTS)]
-    copies = {}
-    for i, k in enumerate(places):
-        rows = pl.ds(pl.multiple_of((me ^ k) * share, share), share)
-        for j, part in enumerate(parts):
-            copies[i, j] = fetch(w_ref.at[rows, part], w.at[i, :, part], sems.at[i, j])
+    depth = out.shape[2]
+    return [
+        fetch(ref.at[:, pl.ds(pl.multiple_of((me ^ k) * depth, depth), depth)], out.at[i], sems.at[i])
+        for i, k in enumerate(places)
+    ]
+
+
+def fetch_rows(places, ref, out, sems, at):
+    me = lax.axis_index("head")
+    share = out.shape[1]
+    return [
+        fetch(ref.at[pl.ds(pl.multiple_of((me ^ k) * share, share), share)], out.at[i], sems.at[i, at])
+        for i, k in enumerate(places)
+    ]
+
+
+def rows_shape(places, w, heads):
+    return jax.ShapeDtypeStruct((len(places), w.shape[0] // heads, w.shape[1]), w.dtype)
+
+
+def query_terms_body(places, upper_ref, lower_ref, w_ref, *refs):
+    upper_out, lower_out = refs[:2]
+    copies, w = [], w_ref
+    if places is not None:
+        w, sems = refs[2:]
+        copies = fetch_rows(places, w_ref, w, sems, 0)
     half = upper_ref.shape[0]
     x = jnp.concatenate([upper_ref[...], lower_ref[...]], axis=0)
-    for i in range(len(places)):
-        total = None
-        for j, part in enumerate(parts):
-            copies[i, j].wait()
-            term = mm_nt(x[:, part], w[i, :, part])
-            total = term if total is None else total + term
+    for i in range(w.shape[0]):
+        if copies:
+            copies[i].wait()
+        total = mm_nt(x, w[i])
         upper_out[i] = total[:half]
         lower_out[i] = total[half:]
 
 
 def query_terms(upper, lower, w, heads, places):
     rows, depth = upper.shape
-    share = w.shape[0] // heads
-    size = len(places)
+    scratch = []
+    shape = w
+    if w.ndim == 2:
+        shape = rows_shape(places, w, heads)
+        scratch = [VMEM(shape.shape, w.dtype), pltpu.SemaphoreType.DMA((len(places), 1))]
+        w = in_hbm(w)
+    else:
+        places = None
+    size, share = shape.shape[:2]
     return pl.pallas_call(
         functools.partial(query_terms_body, places),
-        in_specs=[pl.BlockSpec(memory_space=VMEM)] * 2 + [pl.BlockSpec(memory_space=HBM)],
+        in_specs=[pl.BlockSpec(memory_space=VMEM)] * 2
+        + [pl.BlockSpec(memory_space=HBM if scratch else VMEM)],
         out_specs=[pl.BlockSpec(memory_space=VMEM)] * 2,
         out_shape=[jax.ShapeDtypeStruct((size, rows, share), jnp.float32)] * 2,
-        scratch_shapes=[
-            VMEM((size, share, depth), w.dtype),
-            pltpu.SemaphoreType.DMA((size, PARTS)),
-        ],
-        compiler_params=params(),
-        cost_estimate=cost(4.6),
+        scratch_shapes=scratch,
+        compiler_params=params(),
+        cost_estimate=cost(3),
         name="query_terms",
-    )(upper, lower, in_hbm(w))
+    )(upper, lower, w)
 
 
 def all_terms_body(places, count, first_ref, *refs):
     terms, (wk_ref, wv_ref), refs = refs[:count], refs[count : count + 2], refs[count + 2 :]
-    outs, (wk, wv, sems) = refs[:-3], refs[-3:]
-    me = lax.axis_index("head")
-    size, share, width = wk.shape
-    copies = {}
-    for i, k in enumerate(places):
-        rows = pl.ds(pl.multiple_of((me ^ k) * share, share), share)
-        copies[i] = [
-            fetch(wk_ref.at[rows], wk.at[i], sems.at[i, 0]),
-            fetch(wv_ref.at[rows], wv.at[i], sems.at[i, 1]),
-        ]
+    wk, wv, copies = wk_ref, wv_ref, []
+    if places is not None:
+        refs, (wk, wv, sems) = refs[:-3], refs[-3:]
+        copies = [fetch_rows(places, wk_ref, wk, sems, 0), fetch_rows(places, wv_ref, wv, sems, 1)]
+    outs = refs
+    width = wk.shape[2]
     grads = terms[0][...].astype(jnp.float32)
     for term in terms[1:]:
         grads = grads + term[...].astype(jnp.float32)
     grads = grads.astype(jnp.bfloat16)
-    for i, pair in copies.items():
-        for copy in pair:
-            copy.wait()
+    for i in range(wk.shape[0]):
+        for some in copies:
+            some[i].wait()
         total = first_ref[i] + mm_nt(grads[:, :width], wk[i])
         total = total + mm_nt(grads[:, width:], wv[i])
         if len(outs) == 1:
@@ -265,26 +266,32 @@
             outs[i][...] = total.astype(outs[i].dtype)
 
 
-def all_terms(first, terms, wk, wv, places, stacked):
+def all_terms(first, terms, wk, wv, heads, places, stacked):
     size, rows, share = first.shape
-    width = wk.shape[1]
+    scratch = []
+    if wk.ndim == 2:
+        shape = rows_shape(places, wk, heads).shape
+        scratch = [
+            VMEM(shape, wk.dtype),
+            VMEM(shape, wv.dtype),
+            pltpu.SemaphoreType.DMA((size, 2)),
+        ]
+        wk, wv = in_hbm(wk), in_hbm(wv)
+    else:
+        places = None
     return pl.pallas_call(
         functools.partial(all_terms_body, places, len(terms)),
         in_specs=[pl.BlockSpec(memory_space=VMEM)] * (1 + len(terms))
-        + [pl.BlockSpec(memory_space=HBM)] * 2,
+        + [pl.BlockSpec(memory_space=HBM if scratch else VMEM)] * 2,
         out_specs=[pl.BlockSpec(memory_space=VMEM)] * (1 if stacked else size),
         out_shape=[jax.ShapeDtypeStruct((size, rows, share), jnp.bfloat16)]
         if stacked
         else [jax.ShapeDtypeStruct((rows, share), jnp.bfloat16)] * size,
-        scratch_shapes=[
-            VMEM((size, share, width), wk.dtype),
-            VMEM((size, share, width), wv.dtype),
-            pltpu.SemaphoreType.DMA((size, 2)),
-        ],
-        compiler_params=params(),
-        cost_estimate=cost(3.2),
+        scratch_shapes=scratch,
+        compiler_params=params(),
+        cost_estimate=cost(2),
         name="all_terms",
-    )(first, *terms, in_hbm(wk), in_hbm(wv))
+    )(first, *terms, wk, wv)
 
 
 def part_of(ref, at):
@@ -304,6 +311,22 @@
         compiler_params=params(),
         cost_estimate=cost(0.5),
         name="add",
+    )(a, b)
+
+
+def merge_body(at, a_ref, b_ref, out_ref):
+    out_ref[...] = a_ref[...].astype(jnp.float32) + part_of(b_ref, at)
+
+
+def merge(a, b, at):
+    return pl.pallas_call(
+        functools.partial(merge_body, at),
+        in_specs=[pl.BlockSpec(memory_space=VMEM)] * 2,
+        out_specs=pl.BlockSpec(memory_space=VMEM),
+        out_shape=jax.ShapeDtypeStruct(a.shape, jnp.float32),
+        compiler_params=params(),
+        cost_estimate=cost(0.5),
+        name="merge",
     )(a, b)
 
 
@@ -386,13 +409,15 @@
     )
 
 
-def stats_body(sizes, upper, order, lengths, q_ref, *refs):
+def stats_body(sizes, upper, spare, order, lengths, q_ref, *refs):
     peers, half, groups, share, dim, docs = sizes
     if upper:
-        level_ref, mixed_ref, held, kept, places = refs[peers:]
+        w_ref, level_ref, mixed_ref, w, held, kept, places, sems = refs[peers:]
+    else:
+        held, w_ref, level_ref, mixed_ref, w, kept, places, sems = refs
+    copies = fetch_columns(spare, w_ref, w, sems)
+    if upper:
         load_blocks(refs[:peers], held)
-    else:
-        held, level_ref, mixed_ref, kept, places = refs
     me = lax.axis_index("ctx")
     width = groups * dim
     factor = math.log2(math.e) / math.sqrt(dim)
@@ -442,39 +467,49 @@
         total = jnp.sum(total, axis=0, keepdims=True)
         level_ref[g] = top * factor + jnp.log2(total)
         mixed_ref[g] = mixed / total
+    for copy in copies:
+        copy.wait()
 
 
 def stats(upper, q, *args):
-    *blocks, span_order, doc_lengths, sizes = args
+    *blocks, w, span_order, doc_lengths, sizes = args
+    heads = lax.axis_size("head")
+    spare = list(range(heads))[: heads // 2] if upper else list(range(heads))[heads // 2 :]
     peers, half, groups, share, dim, docs = sizes
     columns = share * half
     return pl.pallas_call(
-        functools.partial(stats_body, sizes, upper),
+        functools.partial(stats_body, sizes, upper, spare),
         in_specs=[pl.BlockSpec(memory_space=pltpu.SMEM)] * 2
-        + [pl.BlockSpec(memory_space=VMEM)] * (1 + len(blocks)),
-        out_specs=[pl.BlockSpec(memory_space=VMEM)] * (3 if upper else 2),
+        + [pl.BlockSpec(memory_space=VMEM)] * (1 + len(blocks))
+        + [pl.BlockSpec(memory_space=HBM)],
+        out_specs=[pl.BlockSpec(memory_space=VMEM)] * (4 if upper else 3),
         out_shape=[
             jax.ShapeDtypeStruct((groups, 1, columns), jnp.float32),
             jax.ShapeDtypeStruct((groups, dim, columns), jnp.float32),
+            jax.ShapeDtypeStruct((len(spare), w.shape[0], w.shape[1] // heads), w.dtype),
         ]
         + [jax.ShapeDtypeStruct((2 * peers * half, 2 * groups * dim), jnp.bfloat16)] * upper,
         scratch_shapes=[
             VMEM((groups, (2 * peers + AT_ONCE) * half, columns), jnp.float32),
             pltpu.SMEM((2 * peers,), jnp.int32),
+            pltpu.SemaphoreType.DMA((len(spare),)),
         ],
         compiler_params=params(),
         cost_estimate=cost(2.4),
         name="upper_stats" if upper else "lower_stats",
-    )(span_order, doc_lengths, q, *blocks)
-
-
-def grads_body(sizes, upper, order, lengths, q_ref, g_ref, level_ref, mixed_ref, *refs):
+    )(span_order, doc_lengths, q, *blocks, in_hbm(w))
+
+
+def grads_body(sizes, upper, spare, order, lengths, q_ref, g_ref, level_ref, mixed_ref, *refs):
     peers, half, groups, share, dim, docs = sizes
     spans = 2 * peers
     if upper:
-        held, dq_ref, even_ref, *odd_refs, rest_ref, sums, places = refs
+        held, dq_ref, even_ref, *odd_refs, sums, places = refs
     else:
-        rest_ref, held, dq_ref, even_ref, *odd_refs, sums, places = refs
+        rest_ref, held, wq_ref, wk_ref, wv_ref, dq_ref, even_ref, *odd_refs, wq, wk, wv, sums, places, sems = refs
+        copies = []
+        for i, (w_ref, w) in enumerate(((wq_ref, wq), (wk_ref, wk), (wv_ref, wv))):
+            copies += fetch_rows(spare, w_ref, w, sems, i)
     me = lax.axis_index("ctx")
     width = groups * dim
     scale = 1.0 / math.sqrt(dim)
@@ -484,10 +519,18 @@
     at = upper_half(order)
     j = at if upper else 1 - at
     span, position, start, lowest = own_span(order, lengths, docs, me, j, half)
-    if upper:
-        sums[...] = jnp.zeros_like(sums)
-    else:
-        sums[...] = rest_ref[...]
+    steps = (span - lowest) // AT_ONCE + 1
+
+    def fill(p, carry):
+        target = pl.ds(pl.multiple_of(p * half, half), half)
+        if upper:
+            sums[target, :] = jnp.zeros((half, 2 * width), jnp.float32)
+        else:
+            sums[target, :] = rest_ref[target, :]
+        return carry
+
+    lax.fori_loop(0, jnp.maximum(span - AT_ONCE * steps + 1, 0), fill, 0)
+    lax.fori_loop(span + 1, sums.shape[0] // half, fill, 0)
     rows = pl.ds(pl.multiple_of(j * half, half), half)
     queries = [stack_heads(q_ref, rows, g, share, dim) for g in range(groups)]
     outs = [stack_heads(g_ref, rows, g, share, dim) for g in range(groups)]
@@ -516,13 +559,16 @@
             value_term = mm(chance.astype(jnp.bfloat16), outs[g])
             for j, target in enumerate(targets):
                 part = slice(j * half, (j + 1) * half)
-                sums[target, g * dim : (g + 1) * dim] += key_term[part]
-                sums[target, width + g * dim : width + (g + 1) * dim] += value_term[part]
+                for at, term in ((g * dim, key_term[part]), (width + g * dim, value_term[part])):
+                    columns_at = slice(at, at + dim)
+                    if not upper:
+                        term = term + rest_ref[target, columns_at]
+                    sums[target, columns_at] = term
             fresh.append(carry[g] + mm_tn(keys, score))
         return tuple(fresh)
 
     empty = jnp.zeros((dim, columns), jnp.float32)
-    done = lax.fori_loop(0, (span - lowest) // AT_ONCE + 1, visit, (empty,) * groups)
+    done = lax.fori_loop(0, steps, visit, (empty,) * groups)
     for g in range(groups):
         for h in range(share):
             head = g * share + h
@@ -539,33 +585,43 @@
         part = pl.ds(pl.multiple_of(pick * half, half), half)
         out[slot, :, :width] = (sums[part, :width] * scale).astype(out.dtype)
         out[slot, :, width:] = sums[part, width:].astype(out.dtype)
-    if upper:
-        rest_ref[...] = sums[: peers * half, :]
+    if not upper:
+        for copy in copies:
+            copy.wait()
 
 
 def grads(upper, q, g, level, mixed, *args):
     *blocks, span_order, doc_lengths, sizes = args
+    weights, spare, scratch = [], [], []
+    if not upper:
+        heads = lax.axis_size("head")
+        spare = list(range(heads - 1, 0, -2))
+        weights, blocks = [in_hbm(w) for w in blocks[-3:]], blocks[:-3]
+        scratch = [pltpu.SemaphoreType.DMA((len(spare), 3))]
     peers, half, groups, share, dim, docs = sizes
     tokens, width = 2 * half, groups * dim
     columns = share * half
     terms = jax.ShapeDtypeStruct((peers // 2, half, 2 * width), jnp.bfloat16)
     odds = jax.ShapeDtypeStruct((peers // 4, half, 2 * width), jnp.bfloat16)
-    rests = jax.ShapeDtypeStruct((peers * half, 2 * width), jnp.float32)
+    rests = jax.ShapeDtypeStruct((peers * tokens, 2 * width), jnp.float32)
     outs = [jax.ShapeDtypeStruct((half, g.shape[1]), jnp.bfloat16), terms, odds, odds] + [rests] * upper
-    return pl.pallas_call(
-        functools.partial(grads_body, sizes, upper),
+    outs += [rows_shape(spare, w, heads) for w in weights]
+    return pl.pallas_call(
+        functools.partial(grads_body, sizes, upper, spare),
         in_specs=[pl.BlockSpec(memory_space=pltpu.SMEM)] * 2
-        + [pl.BlockSpec(memory_space=VMEM)] * (4 + len(blocks)),
+        + [pl.BlockSpec(memory_space=VMEM)] * (4 + len(blocks))
+        + [pl.BlockSpec(memory_space=HBM)] * len(weights),
         out_specs=[pl.BlockSpec(memory_space=VMEM)] * len(outs),
         out_shape=outs,
-        scratch_shapes=[
-            VMEM(((2 if upper else 1) * peers * half, 2 * width), jnp.float32),
+        scratch_shapes=[VMEM((peers * half, 2 * width), jnp.float32)] * (not upper)
+        + [
             pltpu.SMEM((2 * peers,), jnp.int32),
-        ],
+        ]
+        + scratch,
         compiler_params=params(),
         cost_estimate=cost(3.0),
         name="upper_grads" if upper else "lower_grads",
-    )(span_order, doc_lengths, q, g, level, mixed, *blocks)
+    )(span_order, doc_lengths, q, g, level, mixed, *blocks, *weights)
 
 
 def swap(x, k, axis):
@@ -634,19 +690,19 @@
     def attend(upper, call, *args):
         return turn(lambda *a: call(upper, *a, span_order, doc_lengths, sizes), *args)
 
-    def context(blocks, places, total, dtype):
-        shape = jax.tree.structure((blocks, total))
+    def context(blocks, stacks, spans, total, dtype):
+        shape = jax.tree.structure((blocks, stacks, total))
 
         def call(*flat):
-            parts, given = jax.tree.unflatten(shape, flat)
-            return back_project(parts, places, w_out, given, dtype)
-
-        return turn(call, *jax.tree.leaves((blocks, total)))
-
-    def send_first(parts, stack):
+            parts, weights, given = jax.tree.unflatten(shape, flat)
+            return back_project(parts, weights, spans, given, dtype)
+
+        return turn(call, *jax.tree.leaves((blocks, stacks, total)))
+
+    def send_first(parts, stack, places=None):
+        if stack is None:
+            return {k ^ 1: (swap(parts[k], 1, "head"), None) for k in places} | {0: None}
         places = range(heads - 1, 0, -2)
-        if stack is None:
-            return {k ^ 1: (swap(parts[k], 1, "head"), None) for k in places}
         got = swap(stack, 1, "head")
         return {k ^ 1: (got, i) for i, k in enumerate(places)}
 
@@ -675,38 +731,67 @@
     query, near_blocks = lax.optimization_barrier((query, near_blocks))
     blocks = (*near_blocks, *[swap(block, 1, "ctx") for block in near_blocks])
     query, far[1], near[1] = lax.optimization_barrier((query, far[1], near[1]))
-    *upper_stats, held = attend(True, stats, query, *blocks)
-    lower_stats = attend(False, stats, query, held)
+    *upper_stats, w_first, held = attend(True, stats, query, *blocks, w_out)
+    *lower_stats, w_second = attend(False, stats, query, held, w_out)
     passed = [{k ^ 1: swap(x, 1, "head") for k, x in got.items() if k} for got in far]
-    firsts = {0: (out_grad,), 1: tuple(near)}
-    firsts |= {k: (far[0][k], far[1][k]) for k in range(2, heads, 2)}
-    lasts = {k: (passed[0][k], passed[1][k]) for k in range(3, heads, 2)}
-    total = context(list(firsts.values()), list(firsts), None, jnp.float32)
-    context_grad = context(list(lasts.values()), list(lasts), total, jnp.bfloat16)
+    come = {0: (out_grad,), 1: tuple(near)}
+    come |= {k: (far[0][k], far[1][k]) for k in range(2, heads, 2)}
+    come |= {k: (passed[0][k], passed[1][k]) for k in range(3, heads, 2)}
+    blocks = [come[k] for k in range(heads)]
+    mid = heads // 2
+    total = context(
+        blocks[:-1], (w_first, w_second), [(0, mid), (0, mid - 1)], None, jnp.float32
+    )
+    context_grad = context(blocks[-1:], (w_second,), [(mid - 1, mid)], total, jnp.bfloat16)
     upper_dq, even, *odd, rest = attend(True, grads, query, context_grad, *upper_stats, held)
     upper = scatter_ctx(turn(pair_sums, even, *[swap(x, 1, "ctx") for x in odd]))
-    lower_dq, even, *odd = attend(
-        False, grads, query, context_grad, *lower_stats, rest, held
+    weights = (w_query, w_key, value_projection)
+    lower_dq, even, *odd, wq, wk, wv = attend(
+        False, grads, query, context_grad, *lower_stats, rest, held, *weights
     )
     sides = [list(range(heads - 1, 0, -2)), list(range(heads - 2, -1, -2))]
-
-    def firsts_of(places):
-        return turn(lambda a, b: query_terms(a, b, w_query, heads, places), upper_dq, lower_dq)
-
-    def terms_of(first, terms, places, stacked=False):
+    weights = [(wq, wk, wv), weights]
+
+    def firsts_of(side):
+        return turn(
+            lambda a, b, w: query_terms(a, b, w, heads, sides[side]),
+            upper_dq,
+            lower_dq,
+            weights[side][0],
+        )
+
+    def terms_of(first, terms, side, stacked=False):
         outs = turn(
-            lambda a, *b: all_terms(a, b, w_key, value_projection, places, stacked), first, *terms
+            lambda a, k, v, *b: all_terms(a, b, k, v, heads, sides[side], stacked),
+            first,
+            *weights[side][1:],
+            *terms,
         )
-        return outs[0] if stacked else dict(zip(places, outs))
-
-    first = [firsts_of(sides[0])]
+        return outs[0] if stacked else dict(zip(sides[side], outs))
+
+    first = [firsts_of(0)]
     lower_odd = [swap(x, 1, "ctx") for x in odd]
-    upper_got = send_first(None, terms_of(first[0][0], upper, sides[0], True))
+    upper_got = send_first(None, terms_of(first[0][0], upper, 0, True))
     lower = scatter_ctx(turn(pair_sums, even, *lower_odd))
-    first.append(firsts_of(sides[1]))
-    lower_got = send_first(terms_of(first[0][1], lower, sides[0]), None)
-    upper = send_rest(terms_of(first[1][0], upper, sides[1]), upper_got)
-    lower = send_rest(terms_of(first[1][1], lower, sides[1]), lower_got)
+    first.append(firsts_of(1))
+    upper = terms_of(first[1][0], upper, 1)
+    parts = terms_of(first[0][1], lower, 0)
+    lower_got = send_first(parts, None, sides[0][:-1])
+    upper = send_rest(upper, upper_got)
+    lower = terms_of(first[1][1], lower, 1)
+    lower = send_rest(lower, lower_got)
+    stack, at = upper[1]
+    upper = [(turn(lambda a, b: merge(a, b, at), upper[0][0], stack), None)] + upper[2:]
+    last_part, held = lax.optimization_barrier((parts[1], last[0]))
+    last_part = (swap(last_part, 1, "head"), None)
+    total = upper[0][0]
+    for block, at in upper[1:]:
+        total = turn(lambda a, b: merge(a, b, None), total, block)
+    upper = [(total, None)]
+    total = lower[0][0]
+    for block, at in lower[2:]:
+        total = turn(lambda a, b: merge(a, b, None), total, block)
+    lower = [(total, None), last_part]
     return join_rows(upper, lower, span_order)
 
 

time: 108 us -> 103 us (0.954)
  Pallas kernels: 40.7 us -> 35.4 us
    pallas_call x4, Pallas kernels: 8.79 us -> 6.33 us  [all_terms(): pl.pallas_call(functools.partial(all_terms_body, places, len(terms)), in_...]
    pallas_call x2, Pallas kernels: 6.3 us -> 4.4 us  [query_terms(): pl.pallas_call(functools.partial(query_terms_body, places), in_specs=[pl....]
    pallas_call x6 -> x9, Pallas kernels: 15.5 us -> 14.7 us  [the longest x2 6.29 us: grads(): pl.pallas_call(functools.partial(grads_body, sizes, upper, spare), in_spe...]
  transfers between devices with their start and end apart: 28 -> 28, of which waited for: 11 -> 13; matrix products, arithmetic and copies ran while one was open for 0% -> 0% of each run, Pallas kernels for 32% -> 29%
where the time goes in v2:
time: 103 us
  Pallas kernels  35.4 us (34%)
  waiting for transfers between devices  35 us (34%)
  starting transfers between devices  30.9 us (30%)
  local copies, waits for them, and re-layouts  1.08 us (1%)
    ppermute x28, waiting for transfers between devices, swap(): lax.ppermute(x, axis, [(i, i ^ k) for i in range(lax.axis_size(axis))])  35 us
    ppermute x28, starting transfers between devices, swap(): lax.ppermute(x, axis, [(i, i ^ k) for i in range(lax.axis_size(axis))])  30.9 us
    pallas_call x4, Pallas kernels, all_terms(): pl.pallas_call(functools.partial(all_terms_body, places, len(terms)), in_...  6.33 us
    pallas_call x2, Pallas kernels, grads(): pl.pallas_call(functools.partial(grads_body, sizes, upper, spare), in_spe...  6.29 us
    pallas_call x2, Pallas kernels, stats(): pl.pallas_call(functools.partial(stats_body, sizes, upper, spare), in_spe...  5.66 us
    pallas_call x1, Pallas kernels, project(): pl.pallas_call(functools.partial(project_body, parts), in_specs=[pl.Block...  4.87 us
    pallas_call x2, Pallas kernels, query_terms(): pl.pallas_call(functools.partial(query_terms_body, places), in_specs=[pl....  4.4 us
    pallas_call x1, Pallas kernels, project_kv(): pl.pallas_call(functools.partial(kv_body, parts), in_specs=[pl.BlockSpec(...  3.32 us
  transfers between devices with their start and end apart: 28, of which 13 were waited for; matrix products, arithmetic and copies ran while one was open for 0% of the time, Pallas kernels for 29%

profile of v2, /device:TPU:0, one launch (start us, length us, event | category | flops | bytes accessed | tf_op | source)
XLA Modules:
  0.0 102.7 jit_solution(11339238983091954090)
XLA Ops:
  0.0 1.1 %fusion = (bf16[128,1024]{1,0:T(8,128)(2,1)S(1)}, bf16[128,1024]{1,0:T(8,128)(2,1)S(1)}) fusion(bf16[256,1024]{1,0:T(8,128)(2,1)} %refs_0_), kind=kLoop, calls=%fused_computation | loop fusion | bytes 1048576 | tf_op jit(solution)/shard_map/slice | solution.py:722
  1.1 3.1 %collective-permute-start.2 = (bf16[128,1024]{1,0:T(8,128)(2,1)S(1)}, bf16[128,1024]{1,0:T(8,128)(2,1)S(1)}, u32[]{:S(2)}, u32[]{:S(2)}) collective-permute-start(bf16[128,1024]{1,0:T(8,128)(2,1)S(1)} %get-tuple-element.294), channel_id=1, source_target_pairs={{0,8},{8,0},{16,24},{24,16},{1,9},{9,1},{17,25},{25,17},{2,10},{10... | collective-permute-start | bytes 786440 | tf_op jit(solution)/shard_map/ppermute | solution.py:628
  4.2 2.6 %collective-permute-start.1 = (bf16[128,1024]{1,0:T(8,128)(2,1)S(1)}, bf16[128,1024]{1,0:T(8,128)(2,1)S(1)}, u32[]{:S(2)}, u32[]{:S(2)}) collective-permute-start(bf16[128,1024]{1,0:T(8,128)(2,1)S(1)} %get-tuple-element.294), channel_id=1, source_target_pairs={{0,16},{8,24},{16,0},{24,8},{1,17},{9,25},{17,1},{25,9},{2,18},{10... | collective-permute-start | bytes 786440 | tf_op jit(solution)/shard_map/ppermute | solution.py:628
  6.7 3.3 %project_kv.1.refs_0_ = bf16[256,512]{1,0:T(8,128)(2,1)S(1)} custom-call(bf16[256,4096]{1,0:T(8,128)(2,1)} %x_ref.1, bf16[4096,256]{1,0:T(8,128)(2,1)} %refs_4_.2, bf16[4096,256]{1,0:T(8,128)(2,1)} %refs_5_.1), custom_call_target="tpu_custom_call" | custom-call | bytes 1 | tf_op jit(solution)/shard_map/project_kv/pallas_call | solution.py:91
  10.1 1.6 %collective-permute-start = (bf16[256,512]{1,0:T(8,128)(2,1)S(1)}, bf16[256,512]{1,0:T(8,128)(2,1)S(1)}, u32[]{:S(2)}, u32[]{:S(2)}) collective-permute-start(bf16[256,512]{1,0:T(8,128)(2,1)S(1)} %project_kv.1.refs_0_), channel_id=1, source_target_pairs={{0,2},{1,3},{2,0},{3,1},{4,6},{5,7},{6,4},{7,5},{8,10},{9,11},{10,... | collective-permute-start | bytes 786440 | tf_op jit(solution)/shard_map/ppermute | solution.py:628
  11.6 1.5 %collective-permute-start.4 = (bf16[256,512]{1,0:T(8,128)(2,1)S(1)}, bf16[256,512]{1,0:T(8,128)(2,1)S(1)}, u32[]{:S(2)}, u32[]{:S(2)}) collective-permute-start(bf16[256,512]{1,0:T(8,128)(2,1)S(1)} %project_kv.1.refs_0_), channel_id=1, source_target_pairs={{0,4},{1,5},{2,6},{3,7},{4,0},{5,1},{6,2},{7,3},{8,12},{9,13},{10,... | collective-permute-start | bytes 786440 | tf_op jit(solution)/shard_map/ppermute | solution.py:628
  13.2 2.8 %collective-permute-done.2.refs_1_ = bf16[128,1024]{1,0:T(8,128)(2,1)S(1)} collective-permute-done((bf16[128,1024]{1,0:T(8,128)(2,1)S(1)}, bf16[128,1024]{1,0:T(8,128)(2,1)S(1)}, u32[]{:S(2)}, u32[]{:S(2)}) %collective-permute-start.2) | collective-permute-done | bytes 262176 | tf_op jit(solution)/shard_map/ppermute | solution.py:628
  16.0 2.5 %collective-permute-done.1.refs_3_ = bf16[128,1024]{1,0:T(8,128)(2,1)S(1)} collective-permute-done((bf16[128,1024]{1,0:T(8,128)(2,1)S(1)}, bf16[128,1024]{1,0:T(8,128)(2,1)S(1)}, u32[]{:S(2)}, u32[]{:S(2)}) %collective-permute-start.1) | collective-permute-done | bytes 262176 | tf_op jit(solution)/shard_map/ppermute | solution.py:628
  18.5 1.5 %collective-permute-start.5 = (bf16[256,512]{1,0:T(8,128)(2,1)S(1)}, bf16[256,512]{1,0:T(8,128)(2,1)S(1)}, u32[]{:S(2)}, u32[]{:S(2)}) collective-permute-start(bf16[256,512]{1,0:T(8,128)(2,1)S(1)} %collective-permute-done.refs_1_), channel_id=1, source_target_pairs={{0,4},{1,5},{2,6},{3,7},{4,0},{5,1},{6,2},{7,3},{8,12},{9,13},{10,... | collective-permute-start | bytes 786440 | tf_op jit(solution)/shard_map/ppermute | solution.py:628
  20.0 0.4 collective-permute-start.7
  20.5 2.6 %collective-permute-start.6 = (bf16[128,1024]{1,0:T(8,128)(2,1)S(1)}, bf16[128,1024]{1,0:T(8,128)(2,1)S(1)}, u32[]{:S(2)}, u32[]{:S(2)}) collective-permute-start(bf16[128,1024]{1,0:T(8,128)(2,1)S(1)} %get-tuple-element.293), channel_id=1, source_target_pairs={{0,16},{8,24},{16,0},{24,8},{1,17},{9,25},{17,1},{25,9},{2,18},{10... | collective-permute-start | bytes 786440 | tf_op jit(solution)/shard_map/ppermute | solution.py:628
  23.1 4.9 %project.1.q_ref = bf16[256,1024]{1,0:T(8,128)(2,1)S(1)} custom-call(bf16[256,4096]{1,0:T(8,128)(2,1)} %x_ref.1, bf16[4096,1024]{1,0:T(8,128)(2,1)} %w_ref.1), custom_call_target="tpu_custom_call" | custom-call | bytes 1 | tf_op jit(solution)/shard_map/project/pallas_call | solution.py:137
  28.1 0.5 collective-permute-start.10
  28.7 1.2 %collective-permute-done.7.refs_2_ = bf16[128,1024]{1,0:T(8,128)(2,1)S(1)} collective-permute-done((bf16[128,1024]{1,0:T(8,128)(2,1)S(1)}, bf16[128,1024]{1,0:T(8,128)(2,1)S(1)}, u32[]{:S(2)}, u32[]{:S(2)}) %collective-permute-start.7) | collective-permute-done | bytes 262176 | tf_op jit(solution)/shard_map/ppermute | solution.py:628
  29.8 3.8 %collective-permute-done.6.refs_4_ = bf16[128,1024]{1,0:T(8,128)(2,1)S(1)} collective-permute-done((bf16[128,1024]{1,0:T(8,128)(2,1)S(1)}, bf16[128,1024]{1,0:T(8,128)(2,1)S(1)}, u32[]{:S(2)}, u32[]{:S(2)}) %collective-permute-start.6) | collective-permute-done | bytes 262176 | tf_op jit(solution)/shard_map/ppermute | solution.py:628
  33.7 2.0 %collective-permute-start.8 = (bf16[128,1024]{1,0:T(8,128)(2,1)S(1)}, bf16[128,1024]{1,0:T(8,128)(2,1)S(1)}, u32[]{:S(2)}, u32[]{:S(2)}) collective-permute-start(bf16[128,1024]{1,0:T(8,128)(2,1)S(1)} %collective-permute-done.6.refs_4_), channel_id=1, source_target_pairs={{0,8},{8,0},{16,24},{24,16},{1,9},{9,1},{17,25},{25,17},{2,10},{10... | collective-permute-start | bytes 786440 | tf_op jit(solution)/shard_map/ppermute | solution.py:628
  35.7 2.8 %upper_stats.1 = (f32[2,1,512]{2,1,0:T(1,128)S(1)}, f32[2,128,512]{2,1,0:T(8,128)S(1)}, bf16[2,1024,1024]{2,1,0:T(8,128)(2,1)S(1)}, bf16[2048,512]{1,0:T(8,128)(2,1)S(1)}) custom-call(s32[16]{0:T(128)S(1)} %copy-done.1, s32[8]{0:T(128)S(1)} %copy-done.2, bf16[256,1024]{1,0:T(8,128)(2,1)S(1)} %project.1.q_ref, bf16[256,512]{1,0:T(8,128)(2,1)S(1)} %project_kv.1.refs_0_, ...), custom_call_target="tpu_custom_call" | custom-call | bytes 1 | tf_op jit(solution)/shard_map/upper_stats/pallas_call | solution.py:480
  38.6 2.8 %lower_stats.1 = (f32[2,1,512]{2,1,0:T(1,128)S(1)}, f32[2,128,512]{2,1,0:T(8,128)S(1)}, bf16[2,1024,1024]{2,1,0:T(8,128)(2,1)S(1)}) custom-call(s32[16]{0:T(128)S(1)} %copy-done.1, s32[8]{0:T(128)S(1)} %copy-done.2, bf16[256,1024]{1,0:T(8,128)(2,1)S(1)} %project.1.q_ref, bf16[2048,512]{1,0:T(8,128)(2,1)S(1)} %get-tuple-element.217.refs_0_.refs_1_, ...), custom_call_target="tpu_custom_call" | custom-call | bytes 1 | tf_op jit(solution)/shard_map/lower_stats/pallas_call | solution.py:480
  41.4 1.9 %context_grad.2.refs_0_ = f32[256,1024]{1,0:T(8,128)S(1)} custom-call(bf16[256,1024]{1,0:T(8,128)(2,1)S(1)} %copy-done, bf16[128,1024]{1,0:T(8,128)(2,1)S(1)} %collective-permute-done.2.refs_1_, bf16[128,1024]{1,0:T(8,128)(2,1)S(1)} %collective-permute-done.7.refs_2_, bf16[128,1024]{1,0:T(8,128)(2,1)S(1)} %collective-permute-done.1.refs_3_, ...), custom_call_target="tpu_custom_call" | custom-call | bytes 1 | tf_op jit(solution)/shard_map/context_grad/pallas_call | solution.py:173
  43.3 1.5 %collective-permute-done.8.refs_2_ = bf16[128,1024]{1,0:T(8,128)(2,1)S(1)} collective-permute-done((bf16[128,1024]{1,0:T(8,128)(2,1)S(1)}, bf16[128,1024]{1,0:T(8,128)(2,1)S(1)}, u32[]{:S(2)}, u32[]{:S(2)}) %collective-permute-start.8) | collective-permute-done | bytes 262176 | tf_op jit(solution)/shard_map/ppermute | solution.py:628
  44.8 0.7 context_grad.3.g_ref
  45.6 2.9 %upper_grads.1 = (bf16[128,1024]{1,0:T(8,128)(2,1)S(1)}, bf16[4,128,512]{2,1,0:T(8,128)(2,1)S(1)}, bf16[2,128,512]{2,1,0:T(8,128)(2,1)S(1)}, bf16[2,128,512]{2,1,0:T(8,128)(2,1)S(1)}, f32[2048,512]{1,0:T(8,128)S(1)}) custom-call(s32[16]{0:T(128)S(1)} %copy-done.1, s32[8]{0:T(128)S(1)} %copy-done.2, bf16[256,1024]{1,0:T(8,128)(2,1)S(1)} %project.1.q_ref, ...), custom_call_target="tpu_custom_call" | custom-call | bytes 1 | tf_op jit(solution)/shard_map/upper_grads/pallas_call | solution.py:609
  48.6 0.5 collective-permute-start.14
  49.1 1.0 collective-permute-done.13.refs_0_
  50.6 1.5 %collective-permute-start.15 = (bf16[128,512]{1,0:T(8,128)(2,1)S(1)}, bf16[128,512]{1,0:T(8,128)(2,1)S(1)}, u32[]{:S(2)}, u32[]{:S(2)}) collective-permute-start(bf16[128,512]{1,0:T(8,128)(2,1)S(1)} %get-tuple-element.229), channel_id=1, source_target_pairs={{0,2},{1,3},{2,0},{3,1},{4,6},{5,7},{6,4},{7,5},{8,10},{9,11},{10,... | collective-permute-start | bytes 393224 | tf_op jit(solution)/shard_map/ppermute | solution.py:628
  52.1 2.0 %collective-permute-start.16 = (bf16[128,512]{1,0:T(8,128)(2,1)S(1)}, bf16[128,512]{1,0:T(8,128)(2,1)S(1)}, u32[]{:S(2)}, u32[]{:S(2)}) collective-permute-start(bf16[128,512]{1,0:T(8,128)(2,1)S(1)} %get-tuple-element.230), channel_id=1, source_target_pairs={{0,4},{1,5},{2,6},{3,7},{4,0},{5,1},{6,2},{7,3},{8,12},{9,13},{10,... | collective-permute-start | bytes 393224 | tf_op jit(solution)/shard_map/ppermute | solution.py:628
  54.2 1.4 %collective-permute-start.17 = (bf16[128,512]{1,0:T(8,128)(2,1)S(1)}, bf16[128,512]{1,0:T(8,128)(2,1)S(1)}, u32[]{:S(2)}, u32[]{:S(2)}) collective-permute-start(bf16[128,512]{1,0:T(8,128)(2,1)S(1)} %get-tuple-element.231), channel_id=1, source_target_pairs={{0,6},{1,7},{2,4},{3,5},{4,2},{5,3},{6,0},{7,1},{8,14},{9,15},{10,... | collective-permute-start | bytes 393224 | tf_op jit(solution)/shard_map/ppermute | solution.py:628
  55.6 3.4 %lower_grads.1 = (bf16[128,1024]{1,0:T(8,128)(2,1)S(1)}, bf16[4,128,512]{2,1,0:T(8,128)(2,1)S(1)}, bf16[2,128,512]{2,1,0:T(8,128)(2,1)S(1)}, bf16[2,128,512]{2,1...) custom-call(s32[16]{0:T(128)S(1)} %copy-done.1, ...), custom_call_target="tpu_custom_call" | custom-call | bytes 1 | tf_op jit(solution)/shard_map/lower_grads/pallas_call | solution.py:609
  58.9 0.8 collective-permute-start.18
  59.8 1.3 %query_terms.2 = (f32[2,128,1024]{2,1,0:T(8,128)S(1)}, f32[2,128,1024]{2,1,0:T(8,128)S(1)}) custom-call(bf16[128,1024]{1,0:T(8,128)(2,1)S(1)} %get-tuple-element.246.upper_ref, bf16[128,1024]{1,0:T(8,128)(2,1)S(1)} %get-tuple-element.247.lower_ref, bf16[2,1024,1024]{2,1,0:T(8,128)(2,1)S(1)} %get-tuple-element.225.w_ref), custom_call_target="tpu_custom_call" | custom-call | bytes 1 | tf_op jit(solution)/shard_map/query_terms/pallas_call | solution.py:233
  61.1 0.7 collective-permute-done.17.refs_3_
  61.9 0.8 all_terms.4
  62.9 0.6 collective-permute-start.20
  63.6 1.7 %collective-permute-start.21 = (bf16[128,512]{1,0:T(8,128)(2,1)S(1)}, bf16[128,512]{1,0:T(8,128)(2,1)S(1)}, u32[]{:S(2)}, u32[]{:S(2)}) collective-permute-start(bf16[128,512]{1,0:T(8,128)(2,1)S(1)} %get-tuple-element.260), channel_id=1, source_target_pairs={{0,4},{1,5},{2,6},{3,7},{4,0},{5,1},{6,2},{7,3},{8,12},{9,13},{10,... | collective-permute-start | bytes 393224 | tf_op jit(solution)/shard_map/ppermute | solution.py:628
  65.3 1.3 %collective-permute-start.22 = (bf16[128,512]{1,0:T(8,128)(2,1)S(1)}, bf16[128,512]{1,0:T(8,128)(2,1)S(1)}, u32[]{:S(2)}, u32[]{:S(2)}) collective-permute-start(bf16[128,512]{1,0:T(8,128)(2,1)S(1)} %get-tuple-element.261), channel_id=1, source_target_pairs={{0,6},{1,7},{2,4},{3,5},{4,2},{5,3},{6,0},{7,1},{8,14},{9,15},{10,... | collective-permute-start | bytes 393224 | tf_op jit(solution)/shard_map/ppermute | solution.py:628
  66.6 3.1 %query_terms.3 = (f32[2,128,1024]{2,1,0:T(8,128)S(1)}, f32[2,128,1024]{2,1,0:T(8,128)S(1)}) custom-call(bf16[128,1024]{1,0:T(8,128)(2,1)S(1)} %get-tuple-element.246.upper_ref, bf16[128,1024]{1,0:T(8,128)(2,1)S(1)} %get-tuple-element.247.lower_ref, bf16[4096,1024]{1,0:T(8,128)(2,1)} %w_ref.1), custom_call_target="tpu_custom_call" | custom-call | bytes 1 | tf_op jit(solution)/shard_map/query_terms/pallas_call | solution.py:233
  69.7 2.4 %all_terms.5 = (bf16[128,1024]{1,0:T(8,128)(2,1)S(1)}, bf16[128,1024]{1,0:T(8,128)(2,1)S(1)}) custom-call(f32[2,128,1024]{2,1,0:T(8,128)S(1)} %get-tuple-element.250.first_ref, bf16[128,512]{1,0:T(8,128)(2,1)S(1)} %get-tuple-element.251.refs_0_, bf16[128,512]{1,0:T(8,128)(2,1)S(1)} %collective-permute-done.15.refs_1_, ...), custom_call_target="tpu_custom_call" | custom-call | bytes 1 | tf_op jit(solution)/shard_map/all_terms/pallas_call | solution.py:282
  72.1 0.8 collective-permute-done.22.refs_3_
  72.8 0.8 all_terms.6
  73.6 1.8 %collective-permute-start.24 = (bf16[128,1024]{1,0:T(8,128)(2,1)S(1)}, bf16[128,1024]{1,0:T(8,128)(2,1)S(1)}, u32[]{:S(2)}, u32[]{:S(2)}) collective-permute-start(bf16[128,1024]{1,0:T(8,128)(2,1)S(1)} %get-tuple-element.269), channel_id=1, source_target_pairs={{0,8},{8,0},{16,24},{24,16},{1,9},{9,1},{17,25},{25,17},{2,10},{10... | collective-permute-start | bytes 786440 | tf_op jit(solution)/shard_map/ppermute | solution.py:628
  75.4 1.5 %collective-permute-done.23.b_ref = bf16[2,128,1024]{2,1,0:T(8,128)(2,1)S(1)} collective-permute-done((bf16[2,128,1024]{2,1,0:T(8,128)(2,1)S(1)}, bf16[2,128,1024]{2,1,0:T(8,128)(2,1)S(1)}, u32[]{:S(2)}, u32[]{:S(2)}) %collective-permute-start.23) | collective-permute-done | bytes 524320 | tf_op jit(solution)/shard_map/ppermute | solution.py:628
  77.0 0.7 collective-permute-start.25
  77.8 2.4 %all_terms.7 = (bf16[128,1024]{1,0:T(8,128)(2,1)S(1)}, bf16[128,1024]{1,0:T(8,128)(2,1)S(1)}) custom-call(f32[2,128,1024]{2,1,0:T(8,128)S(1)} %get-tuple-element.273.first_ref, bf16[128,512]{1,0:T(8,128)(2,1)S(1)} %get-tuple-element.274.refs_0_, bf16[128,512]{1,0:T(8,128)(2,1)S(1)} %collective-permute-done.20.refs_1_, ...), custom_call_target="tpu_custom_call" | custom-call | bytes 1 | tf_op jit(solution)/shard_map/all_terms/pallas_call | solution.py:282
  80.1 5.9 %collective-permute-done.24.b_ref = bf16[128,1024]{1,0:T(8,128)(2,1)S(1)} collective-permute-done((bf16[128,1024]{1,0:T(8,128)(2,1)S(1)}, bf16[128,1024]{1,0:T(8,128)(2,1)S(1)}, u32[]{:S(2)}, u32[]{:S(2)}) %collective-permute-start.24) | collective-permute-done | bytes 262176 | tf_op jit(solution)/shard_map/ppermute | solution.py:628
  86.3 2.1 %collective-permute-start.27 = (bf16[128,1024]{1,0:T(8,128)(2,1)S(1)}, bf16[128,1024]{1,0:T(8,128)(2,1)S(1)}, u32[]{:S(2)}, u32[]{:S(2)}) collective-permute-start(bf16[128,1024]{1,0:T(8,128)(2,1)S(1)} %get-tuple-element.292), channel_id=1, source_target_pairs={{0,8},{8,0},{16,24},{24,16},{1,9},{9,1},{17,25},{25,17},{2,10},{10... | collective-permute-start | bytes 786440 | tf_op jit(solution)/shard_map/ppermute | solution.py:628
  88.4 8.7 %collective-permute-done.25.b_ref = bf16[128,1024]{1,0:T(8,128)(2,1)S(1)} collective-permute-done((bf16[128,1024]{1,0:T(8,128)(2,1)S(1)}, bf16[128,1024]{1,0:T(8,128)(2,1)S(1)}, u32[]{:S(2)}, u32[]{:S(2)}) %collective-permute-start.25) | collective-permute-done | bytes 262176 | tf_op jit(solution)/shard_map/ppermute | solution.py:628
  97.1 4.2 %collective-permute-done.26.b_ref = bf16[128,1024]{1,0:T(8,128)(2,1)S(1)} collective-permute-done((bf16[128,1024]{1,0:T(8,128)(2,1)S(1)}, bf16[128,1024]{1,0:T(8,128)(2,1)S(1)}, u32[]{:S(2)}, u32[]{:S(2)}) %collective-permute-start.26) | collective-permute-done | bytes 262176 | tf_op jit(solution)/shard_map/ppermute | solution.py:628
  101.3 1.4 %join_rows.1 = bf16[256,1024]{1,0:T(8,128)(2,1)} custom-call(s32[16]{0:T(128)S(1)} %copy-done.1, f32[128,1024]{1,0:T(8,128)S(1)} %merge.4.refs_0_, f32[128,1024]{1,0:T(8,128)S(1)} %merge.5.refs_1_, bf16[128,1024]{1,0:T(8,128)(2,1)S(1)} %collective-permute-done.27.refs_2_), custom_call_target="tpu_custom_call" | custom-call | bytes 1 | tf_op jit(solution)/shard_map/join_rows/pallas_call | solution.py:349
  (37 shorter events, 1.4 us)
Async XLA Ops:
  1.1 14.9 %collective-permute-start.2 = (bf16[128,1024]{1,0:T(8,128)(2,1)S(1)}, bf16[128,1024]{1,0:T(8,128)(2,1)S(1)}, u32[]{:S(2)}, u32[]{:S(2)}) collective-permute-start(bf16[128,1024]{1,0:T(8,128)(2,1)S(1)} %get-tuple-element.294), channel_id=1, source_target_pairs={{0,8},{8,0},{16,24},{24,16},{1,9},{9,1},{17,25},{25,17},{2,10},{10... | collective-permute-start | bytes 786440 | tf_op jit(solution)/shard_map/ppermute | solution.py:628
  4.2 14.3 %collective-permute-start.1 = (bf16[128,1024]{1,0:T(8,128)(2,1)S(1)}, bf16[128,1024]{1,0:T(8,128)(2,1)S(1)}, u32[]{:S(2)}, u32[]{:S(2)}) collective-permute-start(bf16[128,1024]{1,0:T(8,128)(2,1)S(1)} %get-tuple-element.294), channel_id=1, source_target_pairs={{0,16},{8,24},{16,0},{24,8},{1,17},{9,25},{17,1},{25,9},{2,18},{10... | collective-permute-start | bytes 786440 | tf_op jit(solution)/shard_map/ppermute | solution.py:628
  10.1 8.4 %collective-permute-start = (bf16[256,512]{1,0:T(8,128)(2,1)S(1)}, bf16[256,512]{1,0:T(8,128)(2,1)S(1)}, u32[]{:S(2)}, u32[]{:S(2)}) collective-permute-start(bf16[256,512]{1,0:T(8,128)(2,1)S(1)} %project_kv.1.refs_0_), channel_id=1, source_target_pairs={{0,2},{1,3},{2,0},{3,1},{4,6},{5,7},{6,4},{7,5},{8,10},{9,11},{10,... | collective-permute-start | bytes 786440 | tf_op jit(solution)/shard_map/ppermute | solution.py:628
  11.6 16.4 %collective-permute-start.4 = (bf16[256,512]{1,0:T(8,128)(2,1)S(1)}, bf16[256,512]{1,0:T(8,128)(2,1)S(1)}, u32[]{:S(2)}, u32[]{:S(2)}) collective-permute-start(bf16[256,512]{1,0:T(8,128)(2,1)S(1)} %project_kv.1.refs_0_), channel_id=1, source_target_pairs={{0,4},{1,5},{2,6},{3,7},{4,0},{5,1},{6,2},{7,3},{8,12},{9,13},{10,... | collective-permute-start | bytes 786440 | tf_op jit(solution)/shard_map/ppermute | solution.py:628
  18.5 9.5 %collective-permute-start.5 = (bf16[256,512]{1,0:T(8,128)(2,1)S(1)}, bf16[256,512]{1,0:T(8,128)(2,1)S(1)}, u32[]{:S(2)}, u32[]{:S(2)}) collective-permute-start(bf16[256,512]{1,0:T(8,128)(2,1)S(1)} %collective-permute-done.refs_1_), channel_id=1, source_target_pairs={{0,4},{1,5},{2,6},{3,7},{4,0},{5,1},{6,2},{7,3},{8,12},{9,13},{10,... | collective-permute-start | bytes 786440 | tf_op jit(solution)/shard_map/ppermute | solution.py:628
  20.0 15.7 %copy-start.1 = (s32[16]{0:T(128)S(1)}, s32[16]{0:T(128)}, u32[]{:S(2)}) copy-start(s32[16]{0:T(128)} %order.9) | copy-start | bytes 196
  20.0 15.7 %copy-start.2 = (s32[8]{0:T(128)S(1)}, s32[8]{0:T(128)}, u32[]{:S(2)}) copy-start(s32[8]{0:T(128)} %lengths.7) | copy-start | bytes 100
  20.0 9.8 %collective-permute-start.7 = (bf16[128,1024]{1,0:T(8,128)(2,1)S(1)}, bf16[128,1024]{1,0:T(8,128)(2,1)S(1)}, u32[]{:S(2)}, u32[]{:S(2)}) collective-permute-start(bf16[128,1024]{1,0:T(8,128)(2,1)S(1)} %get-tuple-element.293), channel_id=1, source_target_pairs={{0,8},{8,0},{16,24},{24,16},{1,9},{9,1},{17,25},{25,17},{2,10},{10... | collective-permute-start | bytes 786440 | tf_op jit(solution)/shard_map/ppermute | solution.py:628
  20.5 13.2 %collective-permute-start.6 = (bf16[128,1024]{1,0:T(8,128)(2,1)S(1)}, bf16[128,1024]{1,0:T(8,128)(2,1)S(1)}, u32[]{:S(2)}, u32[]{:S(2)}) collective-permute-start(bf16[128,1024]{1,0:T(8,128)(2,1)S(1)} %get-tuple-element.293), channel_id=1, source_target_pairs={{0,16},{8,24},{16,0},{24,8},{1,17},{9,25},{17,1},{25,9},{2,18},{10... | collective-permute-start | bytes 786440 | tf_op jit(solution)/shard_map/ppermute | solution.py:628
  28.0 5.6 %collective-permute-start.9 = (bf16[256,512]{1,0:T(8,128)(2,1)S(1)}, bf16[256,512]{1,0:T(8,128)(2,1)S(1)}, u32[]{:S(2)}, u32[]{:S(2)}) collective-permute-start(bf16[256,512]{1,0:T(8,128)(2,1)S(1)} %project_kv.1.refs_0_), channel_id=1, source_target_pairs={{0,1},{1,0},{2,3},{3,2},{4,5},{5,4},{6,7},{7,6},{8,9},{9,8},{10,11... | collective-permute-start | bytes 786440 | tf_op jit(solution)/shard_map/ppermute | solution.py:628
  28.1 7.6 %collective-permute-start.10 = (bf16[256,512]{1,0:T(8,128)(2,1)S(1)}, bf16[256,512]{1,0:T(8,128)(2,1)S(1)}, u32[]{:S(2)}, u32[]{:S(2)}) collective-permute-start(bf16[256,512]{1,0:T(8,128)(2,1)S(1)} %collective-permute-done.refs_1_), channel_id=1, source_target_pairs={{0,1},{1,0},{2,3},{3,2},{4,5},{5,4},{6,7},{7,6},{8,9},{9,8},{10,11... | collective-permute-start | bytes 786440 | tf_op jit(solution)/shard_map/ppermute | solution.py:628
  28.6 7.1 %collective-permute-start.11 = (bf16[256,512]{1,0:T(8,128)(2,1)S(1)}, bf16[256,512]{1,0:T(8,128)(2,1)S(1)}, u32[]{:S(2)}, u32[]{:S(2)}) collective-permute-start(bf16[256,512]{1,0:T(8,128)(2,1)S(1)} %collective-permute-done.4.refs_2_), channel_id=1, source_target_pairs={{0,1},{1,0},{2,3},{3,2},{4,5},{5,4},{6,7},{7,6},{8,9},{9,8},{10,11... | collective-permute-start | bytes 786440 | tf_op jit(solution)/shard_map/ppermute | solution.py:628
  29.8 5.9 %collective-permute-start.12 = (bf16[256,512]{1,0:T(8,128)(2,1)S(1)}, bf16[256,512]{1,0:T(8,128)(2,1)S(1)}, u32[]{:S(2)}, u32[]{:S(2)}) collective-permute-start(bf16[256,512]{1,0:T(8,128)(2,1)S(1)} %collective-permute-done.5.refs_3_), channel_id=1, source_target_pairs={{0,1},{1,0},{2,3},{3,2},{4,5},{5,4},{6,7},{7,6},{8,9},{9,8},{10,11... | collective-permute-start | bytes 786440 | tf_op jit(solution)/shard_map/ppermute | solution.py:628
  33.7 9.6 %collective-permute-start.3 = (bf16[128,1024]{1,0:T(8,128)(2,1)S(1)}, bf16[128,1024]{1,0:T(8,128)(2,1)S(1)}, u32[]{:S(2)}, u32[]{:S(2)}) collective-permute-start(bf16[128,1024]{1,0:T(8,128)(2,1)S(1)} %collective-permute-done.1.refs_3_), channel_id=1, source_target_pairs={{0,8},{8,0},{16,24},{24,16},{1,9},{9,1},{17,25},{25,17},{2,10},{10... | collective-permute-start | bytes 786440 | tf_op jit(solution)/shard_map/ppermute | solution.py:628
  33.7 11.2 %collective-permute-start.8 = (bf16[128,1024]{1,0:T(8,128)(2,1)S(1)}, bf16[128,1024]{1,0:T(8,128)(2,1)S(1)}, u32[]{:S(2)}, u32[]{:S(2)}) collective-permute-start(bf16[128,1024]{1,0:T(8,128)(2,1)S(1)} %collective-permute-done.6.refs_4_), channel_id=1, source_target_pairs={{0,8},{8,0},{16,24},{24,16},{1,9},{9,1},{17,25},{25,17},{2,10},{10... | collective-permute-start | bytes 786440 | tf_op jit(solution)/shard_map/ppermute | solution.py:628
  38.6 2.9 %copy-start = (bf16[256,1024]{1,0:T(8,128)(2,1)S(1)}, bf16[256,1024]{1,0:T(8,128)(2,1)}, u32[]{:S(2)}) copy-start(bf16[256,1024]{1,0:T(8,128)(2,1)} %refs_0_) | copy-start | bytes 1572868
  48.5 1.6 %collective-permute-start.13 = (bf16[2,128,512]{2,1,0:T(8,128)(2,1)S(1)}, bf16[2,128,512]{2,1,0:T(8,128)(2,1)S(1)}, u32[]{:S(2)}, u32[]{:S(2)}) collective-permute-start(bf16[2,128,512]{2,1,0:T(8,128)(2,1)S(1)} %get-tuple-element.204), channel_id=1, source_target_pairs={{0,1},{1,0},{2,3},{3,2},{4,5},{5,4},{6,7},{7,6},{8,9},{9,8},{10,11... | collective-permute-start | bytes 786440 | tf_op jit(solution)/shard_map/ppermute | solution.py:628
  48.6 1.9 %collective-permute-start.14 = (bf16[2,128,512]{2,1,0:T(8,128)(2,1)S(1)}, bf16[2,128,512]{2,1,0:T(8,128)(2,1)S(1)}, u32[]{:S(2)}, u32[]{:S(2)}) collective-permute-start(bf16[2,128,512]{2,1,0:T(8,128)(2,1)S(1)} %get-tuple-element.205), channel_id=1, source_target_pairs={{0,1},{1,0},{2,3},{3,2},{4,5},{5,4},{6,7},{7,6},{8,9},{9,8},{10,11... | collective-permute-start | bytes 786440 | tf_op jit(solution)/shard_map/ppermute | solution.py:628
  50.6 10.5 %collective-permute-start.15 = (bf16[128,512]{1,0:T(8,128)(2,1)S(1)}, bf16[128,512]{1,0:T(8,128)(2,1)S(1)}, u32[]{:S(2)}, u32[]{:S(2)}) collective-permute-start(bf16[128,512]{1,0:T(8,128)(2,1)S(1)} %get-tuple-element.229), channel_id=1, source_target_pairs={{0,2},{1,3},{2,0},{3,1},{4,6},{5,7},{6,4},{7,5},{8,10},{9,11},{10,... | collective-permute-start | bytes 393224 | tf_op jit(solution)/shard_map/ppermute | solution.py:628
  52.1 9.0 %collective-permute-start.16 = (bf16[128,512]{1,0:T(8,128)(2,1)S(1)}, bf16[128,512]{1,0:T(8,128)(2,1)S(1)}, u32[]{:S(2)}, u32[]{:S(2)}) collective-permute-start(bf16[128,512]{1,0:T(8,128)(2,1)S(1)} %get-tuple-element.230), channel_id=1, source_target_pairs={{0,4},{1,5},{2,6},{3,7},{4,0},{5,1},{6,2},{7,3},{8,12},{9,13},{10,... | collective-permute-start | bytes 393224 | tf_op jit(solution)/shard_map/ppermute | solution.py:628
  54.2 7.7 %collective-permute-start.17 = (bf16[128,512]{1,0:T(8,128)(2,1)S(1)}, bf16[128,512]{1,0:T(8,128)(2,1)S(1)}, u32[]{:S(2)}, u32[]{:S(2)}) collective-permute-start(bf16[128,512]{1,0:T(8,128)(2,1)S(1)} %get-tuple-element.231), channel_id=1, source_target_pairs={{0,6},{1,7},{2,4},{3,5},{4,2},{5,3},{6,0},{7,1},{8,14},{9,15},{10,... | collective-permute-start | bytes 393224 | tf_op jit(solution)/shard_map/ppermute | solution.py:628
  58.9 3.8 %collective-permute-start.18 = (bf16[2,128,512]{2,1,0:T(8,128)(2,1)S(1)}, bf16[2,128,512]{2,1,0:T(8,128)(2,1)S(1)}, u32[]{:S(2)}, u32[]{:S(2)}) collective-permute-start(bf16[2,128,512]{2,1,0:T(8,128)(2,1)S(1)} %get-tuple-element.240), channel_id=1, source_target_pairs={{0,1},{1,0},{2,3},{3,2},{4,5},{5,4},{6,7},{7,6},{8,9},{9,8},{10,11... | collective-permute-start | bytes 786440 | tf_op jit(solution)/shard_map/ppermute | solution.py:628
  59.7 3.1 %collective-permute-start.19 = (bf16[2,128,512]{2,1,0:T(8,128)(2,1)S(1)}, bf16[2,128,512]{2,1,0:T(8,128)(2,1)S(1)}, u32[]{:S(2)}, u32[]{:S(2)}) collective-permute-start(bf16[2,128,512]{2,1,0:T(8,128)(2,1)S(1)} %get-tuple-element.241), channel_id=1, source_target_pairs={{0,1},{1,0},{2,3},{3,2},{4,5},{5,4},{6,7},{7,6},{8,9},{9,8},{10,11... | collective-permute-start | bytes 786440 | tf_op jit(solution)/shard_map/ppermute | solution.py:628
  62.7 14.3 %collective-permute-start.23 = (bf16[2,128,1024]{2,1,0:T(8,128)(2,1)S(1)}, bf16[2,128,1024]{2,1,0:T(8,128)(2,1)S(1)}, u32[]{:S(2)}, u32[]{:S(2)}) collective-permute-start(bf16[2,128,1024]{2,1,0:T(8,128)(2,1)S(1)} %all_terms.4), channel_id=1, source_target_pairs={{0,8},{8,0},{16,24},{24,16},{1,9},{9,1},{17,25},{25,17},{2,10},{10... | collective-permute-start | bytes 1572872 | tf_op jit(solution)/shard_map/ppermute | solution.py:628
  62.9 9.1 %collective-permute-start.20 = (bf16[128,512]{1,0:T(8,128)(2,1)S(1)}, bf16[128,512]{1,0:T(8,128)(2,1)S(1)}, u32[]{:S(2)}, u32[]{:S(2)}) collective-permute-start(bf16[128,512]{1,0:T(8,128)(2,1)S(1)} %get-tuple-element.259), channel_id=1, source_target_pairs={{0,2},{1,3},{2,0},{3,1},{4,6},{5,7},{6,4},{7,5},{8,10},{9,11},{10,... | collective-permute-start | bytes 393224 | tf_op jit(solution)/shard_map/ppermute | solution.py:628
  63.6 8.5 %collective-permute-start.21 = (bf16[128,512]{1,0:T(8,128)(2,1)S(1)}, bf16[128,512]{1,0:T(8,128)(2,1)S(1)}, u32[]{:S(2)}, u32[]{:S(2)}) collective-permute-start(bf16[128,512]{1,0:T(8,128)(2,1)S(1)} %get-tuple-element.260), channel_id=1, source_target_pairs={{0,4},{1,5},{2,6},{3,7},{4,0},{5,1},{6,2},{7,3},{8,12},{9,13},{10,... | collective-permute-start | bytes 393224 | tf_op jit(solution)/shard_map/ppermute | solution.py:628
  65.3 7.5 %collective-permute-start.22 = (bf16[128,512]{1,0:T(8,128)(2,1)S(1)}, bf16[128,512]{1,0:T(8,128)(2,1)S(1)}, u32[]{:S(2)}, u32[]{:S(2)}) collective-permute-start(bf16[128,512]{1,0:T(8,128)(2,1)S(1)} %get-tuple-element.261), channel_id=1, source_target_pairs={{0,6},{1,7},{2,4},{3,5},{4,2},{5,3},{6,0},{7,1},{8,14},{9,15},{10,... | collective-permute-start | bytes 393224 | tf_op jit(solution)/shard_map/ppermute | solution.py:628
  73.6 12.4 %collective-permute-start.24 = (bf16[128,1024]{1,0:T(8,128)(2,1)S(1)}, bf16[128,1024]{1,0:T(8,128)(2,1)S(1)}, u32[]{:S(2)}, u32[]{:S(2)}) collective-permute-start(bf16[128,1024]{1,0:T(8,128)(2,1)S(1)} %get-tuple-element.269), channel_id=1, source_target_pairs={{0,8},{8,0},{16,24},{24,16},{1,9},{9,1},{17,25},{25,17},{2,10},{10... | collective-permute-start | bytes 786440 | tf_op jit(solution)/shard_map/ppermute | solution.py:628
  77.0 20.0 %collective-permute-start.25 = (bf16[128,1024]{1,0:T(8,128)(2,1)S(1)}, bf16[128,1024]{1,0:T(8,128)(2,1)S(1)}, u32[]{:S(2)}, u32[]{:S(2)}) collective-permute-start(bf16[128,1024]{1,0:T(8,128)(2,1)S(1)} %add.2), channel_id=1, source_target_pairs={{0,16},{8,24},{16,0},{24,8},{1,17},{9,25},{17,1},{25,9},{2,18},{10... | collective-permute-start | bytes 786440 | tf_op jit(solution)/shard_map/ppermute | solution.py:628
  86.1 15.1 %collective-permute-start.26 = (bf16[128,1024]{1,0:T(8,128)(2,1)S(1)}, bf16[128,1024]{1,0:T(8,128)(2,1)S(1)}, u32[]{:S(2)}, u32[]{:S(2)}) collective-permute-start(bf16[128,1024]{1,0:T(8,128)(2,1)S(1)} %add.3), channel_id=1, source_target_pairs={{0,16},{8,24},{16,0},{24,8},{1,17},{9,25},{17,1},{25,9},{2,18},{10... | collective-permute-start | bytes 786440 | tf_op jit(solution)/shard_map/ppermute | solution.py:628
  86.3 15.1 %collective-permute-start.27 = (bf16[128,1024]{1,0:T(8,128)(2,1)S(1)}, bf16[128,1024]{1,0:T(8,128)(2,1)S(1)}, u32[]{:S(2)}, u32[]{:S(2)}) collective-permute-start(bf16[128,1024]{1,0:T(8,128)(2,1)S(1)} %get-tuple-element.292), channel_id=1, source_target_pairs={{0,8},{8,0},{16,24},{24,16},{1,9},{9,1},{17,25},{25,17},{2,10},{10... | collective-permute-start | bytes 786440 | tf_op jit(solution)/shard_map/ppermute | solution.py:628

commit v3 on v2

--- a/solution.py
+++ b/solution.py
@@ -389,12 +389,12 @@
         held[k * rows : (k + 1) * rows, :] = ref[...]
 
 
-def span_group(i, span, held, places, half):
-    numbers = [span - AT_ONCE * i - j for j in range(AT_ONCE - 1, -1, -1)]
+def span_group(i, span, held, places, half, count):
+    numbers = [span - count * i - j for j in range(count - 1, -1, -1)]
     known = [jnp.maximum(p, 0) for p in numbers]
     at = [pl.multiple_of(places[p] * half, half) for p in known]
     block = jnp.concatenate([held[pl.ds(place, half), :] for place in at], axis=0)
-    key = numbers[0] * half + lax.broadcasted_iota(jnp.int32, (AT_ONCE * half, 1), 0)
+    key = numbers[0] * half + lax.broadcasted_iota(jnp.int32, (count * half, 1), 0)
     return known, block, key
 
 
@@ -433,7 +433,7 @@
     steps = (span - lowest) // AT_ONCE + 1
 
     def score(i, carry):
-        known, block, key = span_group(i, span, held, places, half)
+        known, block, key = span_group(i, span, held, places, half, AT_ONCE)
         allowed = (key <= position) & (key >= start)
         fresh = []
         for g in range(groups):
@@ -448,7 +448,7 @@
     tops = [jnp.max(top, axis=0, keepdims=True) for top in tops]
 
     def mix(i, carry):
-        known, block, key = span_group(i, span, held, places, half)
+        known, block, key = span_group(i, span, held, places, half, AT_ONCE)
         fresh = []
         for g in range(groups):
             total, mixed = carry[g]
@@ -503,6 +503,7 @@
 def grads_body(sizes, upper, spare, order, lengths, q_ref, g_ref, level_ref, mixed_ref, *refs):
     peers, half, groups, share, dim, docs = sizes
     spans = 2 * peers
+    count = 3 if upper else AT_ONCE
     if upper:
         held, dq_ref, even_ref, *odd_refs, sums, places = refs
     else:
@@ -519,7 +520,7 @@
     at = upper_half(order)
     j = at if upper else 1 - at
     span, position, start, lowest = own_span(order, lengths, docs, me, j, half)
-    steps = (span - lowest) // AT_ONCE + 1
+    steps = (span - lowest) // count + 1
 
     def fill(p, carry):
         target = pl.ds(pl.multiple_of(p * half, half), half)
@@ -529,7 +530,7 @@
             sums[target, :] = rest_ref[target, :]
         return carry
 
-    lax.fori_loop(0, jnp.maximum(span - AT_ONCE * steps + 1, 0), fill, 0)
+    lax.fori_loop(0, jnp.maximum(span - count * steps + 1, 0), fill, 0)
     lax.fori_loop(span + 1, sums.shape[0] // half, fill, 0)
     rows = pl.ds(pl.multiple_of(j * half, half), half)
     queries = [stack_heads(q_ref, rows, g, share, dim) for g in range(groups)]
@@ -544,7 +545,7 @@
         deltas.append(jnp.sum(turned * mixed_ref[g], axis=0, keepdims=True))
 
     def visit(i, carry):
-        known, block, key = span_group(i, span, held, places, half)
+        known, block, key = span_group(i, span, held, places, half, count)
         allowed = (key <= position) & (key >= start)
         targets = [pl.ds(pl.multiple_of(p * half, half), half) for p in known]
         fresh = []

time: 103 us -> 103 us (level)
  Pallas kernels: 35.4 us -> 38.7 us
  starting transfers between devices: 30.9 us -> 29.1 us
    pallas_call x2, Pallas kernels: 6.29 us -> 8.41 us  [grads(): pl.pallas_call(functools.partial(grads_body, sizes, upper, spare), in_spe...]
    ppermute x28, starting transfers between devices: 30.9 us -> 29.1 us  [swap(): lax.ppermute(x, axis, [(i, i ^ k) for i in range(lax.axis_size(axis))])]
    pallas_call x2, Pallas kernels: 5.66 us -> 6.83 us  [stats(): pl.pallas_call(functools.partial(stats_body, sizes, upper, spare), in_spe...]
    ppermute x28, waiting for transfers between devices: 35 us -> 34 us  [swap(): lax.ppermute(x, axis, [(i, i ^ k) for i in range(lax.axis_size(axis))])]
  transfers between devices with their start and end apart: 28 -> 28, of which waited for: 13 -> 12; matrix products, arithmetic and copies ran while one was open for 0% -> 0% of each run, Pallas kernels for 29% -> 30%
where the time goes in v3:
time: 103 us
  Pallas kernels  38.7 us (38%)
  waiting for transfers between devices  34 us (33%)
  starting transfers between devices  29.1 us (28%)
  local copies, waits for them, and re-layouts  1.08 us (1%)
    ppermute x28, waiting for transfers between devices, swap(): lax.ppermute(x, axis, [(i, i ^ k) for i in range(lax.axis_size(axis))])  34 us
    ppermute x28, starting transfers between devices, swap(): lax.ppermute(x, axis, [(i, i ^ k) for i in range(lax.axis_size(axis))])  29.1 us
    pallas_call x2, Pallas kernels, grads(): pl.pallas_call(functools.partial(grads_body, sizes, upper, spare), in_spe...  8.41 us
    pallas_call x2, Pallas kernels, stats(): pl.pallas_call(functools.partial(stats_body, sizes, upper, spare), in_spe...  6.83 us
    pallas_call x4, Pallas kernels, all_terms(): pl.pallas_call(functools.partial(all_terms_body, places, len(terms)), in_...  6.34 us
    pallas_call x1, Pallas kernels, project(): pl.pallas_call(functools.partial(project_body, parts), in_specs=[pl.Block...  4.87 us
    pallas_call x2, Pallas kernels, query_terms(): pl.pallas_call(functools.partial(query_terms_body, places), in_specs=[pl....  4.4 us
    pallas_call x1, Pallas kernels, project_kv(): pl.pallas_call(functools.partial(kv_body, parts), in_specs=[pl.BlockSpec(...  3.32 us
  transfers between devices with their start and end apart: 28, of which 12 were waited for; matrix products, arithmetic and copies ran while one was open for 0% of the time, Pallas kernels for 30%

profile of v3, /device:TPU:0, one launch (start us, length us, event | category | flops | bytes accessed | tf_op | source)
XLA Modules:
  0.0 103.2 jit_solution(13186909103723196006)
XLA Ops:
  0.0 1.1 %fusion = (bf16[128,1024]{1,0:T(8,128)(2,1)S(1)}, bf16[128,1024]{1,0:T(8,128)(2,1)S(1)}) fusion(bf16[256,1024]{1,0:T(8,128)(2,1)} %refs_0_), kind=kLoop, calls=%fused_computation | loop fusion | bytes 1048576 | tf_op jit(solution)/shard_map/slice | solution.py:723
  1.1 3.1 %collective-permute-start.2 = (bf16[128,1024]{1,0:T(8,128)(2,1)S(1)}, bf16[128,1024]{1,0:T(8,128)(2,1)S(1)}, u32[]{:S(2)}, u32[]{:S(2)}) collective-permute-start(bf16[128,1024]{1,0:T(8,128)(2,1)S(1)} %get-tuple-element.294), channel_id=1, source_target_pairs={{0,8},{8,0},{16,24},{24,16},{1,9},{9,1},{17,25},{25,17},{2,10},{10... | collective-permute-start | bytes 786440 | tf_op jit(solution)/shard_map/ppermute | solution.py:629
  4.2 2.6 %collective-permute-start.1 = (bf16[128,1024]{1,0:T(8,128)(2,1)S(1)}, bf16[128,1024]{1,0:T(8,128)(2,1)S(1)}, u32[]{:S(2)}, u32[]{:S(2)}) collective-permute-start(bf16[128,1024]{1,0:T(8,128)(2,1)S(1)} %get-tuple-element.294), channel_id=1, source_target_pairs={{0,16},{8,24},{16,0},{24,8},{1,17},{9,25},{17,1},{25,9},{2,18},{10... | collective-permute-start | bytes 786440 | tf_op jit(solution)/shard_map/ppermute | solution.py:629
  6.7 3.3 %project_kv.1.refs_0_ = bf16[256,512]{1,0:T(8,128)(2,1)S(1)} custom-call(bf16[256,4096]{1,0:T(8,128)(2,1)} %x_ref.1, bf16[4096,256]{1,0:T(8,128)(2,1)} %refs_4_.2, bf16[4096,256]{1,0:T(8,128)(2,1)} %refs_5_.1), custom_call_target="tpu_custom_call" | custom-call | bytes 1 | tf_op jit(solution)/shard_map/project_kv/pallas_call | solution.py:91
  10.1 1.6 %collective-permute-start = (bf16[256,512]{1,0:T(8,128)(2,1)S(1)}, bf16[256,512]{1,0:T(8,128)(2,1)S(1)}, u32[]{:S(2)}, u32[]{:S(2)}) collective-permute-start(bf16[256,512]{1,0:T(8,128)(2,1)S(1)} %project_kv.1.refs_0_), channel_id=1, source_target_pairs={{0,2},{1,3},{2,0},{3,1},{4,6},{5,7},{6,4},{7,5},{8,10},{9,11},{10,... | collective-permute-start | bytes 786440 | tf_op jit(solution)/shard_map/ppermute | solution.py:629
  11.6 1.5 %collective-permute-start.4 = (bf16[256,512]{1,0:T(8,128)(2,1)S(1)}, bf16[256,512]{1,0:T(8,128)(2,1)S(1)}, u32[]{:S(2)}, u32[]{:S(2)}) collective-permute-start(bf16[256,512]{1,0:T(8,128)(2,1)S(1)} %project_kv.1.refs_0_), channel_id=1, source_target_pairs={{0,4},{1,5},{2,6},{3,7},{4,0},{5,1},{6,2},{7,3},{8,12},{9,13},{10,... | collective-permute-start | bytes 786440 | tf_op jit(solution)/shard_map/ppermute | solution.py:629
  13.2 2.8 %collective-permute-done.2.refs_1_ = bf16[128,1024]{1,0:T(8,128)(2,1)S(1)} collective-permute-done((bf16[128,1024]{1,0:T(8,128)(2,1)S(1)}, bf16[128,1024]{1,0:T(8,128)(2,1)S(1)}, u32[]{:S(2)}, u32[]{:S(2)}) %collective-permute-start.2) | collective-permute-done | bytes 262176 | tf_op jit(solution)/shard_map/ppermute | solution.py:629
  16.0 2.5 %collective-permute-done.1.refs_3_ = bf16[128,1024]{1,0:T(8,128)(2,1)S(1)} collective-permute-done((bf16[128,1024]{1,0:T(8,128)(2,1)S(1)}, bf16[128,1024]{1,0:T(8,128)(2,1)S(1)}, u32[]{:S(2)}, u32[]{:S(2)}) %collective-permute-start.1) | collective-permute-done | bytes 262176 | tf_op jit(solution)/shard_map/ppermute | solution.py:629
  18.5 1.5 %collective-permute-start.5 = (bf16[256,512]{1,0:T(8,128)(2,1)S(1)}, bf16[256,512]{1,0:T(8,128)(2,1)S(1)}, u32[]{:S(2)}, u32[]{:S(2)}) collective-permute-start(bf16[256,512]{1,0:T(8,128)(2,1)S(1)} %collective-permute-done.refs_1_), channel_id=1, source_target_pairs={{0,4},{1,5},{2,6},{3,7},{4,0},{5,1},{6,2},{7,3},{8,12},{9,13},{10,... | collective-permute-start | bytes 786440 | tf_op jit(solution)/shard_map/ppermute | solution.py:629
  20.0 0.4 collective-permute-start.7
  20.5 2.6 %collective-permute-start.6 = (bf16[128,1024]{1,0:T(8,128)(2,1)S(1)}, bf16[128,1024]{1,0:T(8,128)(2,1)S(1)}, u32[]{:S(2)}, u32[]{:S(2)}) collective-permute-start(bf16[128,1024]{1,0:T(8,128)(2,1)S(1)} %get-tuple-element.293), channel_id=1, source_target_pairs={{0,16},{8,24},{16,0},{24,8},{1,17},{9,25},{17,1},{25,9},{2,18},{10... | collective-permute-start | bytes 786440 | tf_op jit(solution)/shard_map/ppermute | solution.py:629
  23.1 4.9 %project.1.q_ref = bf16[256,1024]{1,0:T(8,128)(2,1)S(1)} custom-call(bf16[256,4096]{1,0:T(8,128)(2,1)} %x_ref.1, bf16[4096,1024]{1,0:T(8,128)(2,1)} %w_ref.1), custom_call_target="tpu_custom_call" | custom-call | bytes 1 | tf_op jit(solution)/shard_map/project/pallas_call | solution.py:137
  28.1 0.5 collective-permute-start.10
  28.7 1.2 %collective-permute-done.7.refs_2_ = bf16[128,1024]{1,0:T(8,128)(2,1)S(1)} collective-permute-done((bf16[128,1024]{1,0:T(8,128)(2,1)S(1)}, bf16[128,1024]{1,0:T(8,128)(2,1)S(1)}, u32[]{:S(2)}, u32[]{:S(2)}) %collective-permute-start.7) | collective-permute-done | bytes 262176 | tf_op jit(solution)/shard_map/ppermute | solution.py:629
  29.8 3.8 %collective-permute-done.6.refs_4_ = bf16[128,1024]{1,0:T(8,128)(2,1)S(1)} collective-permute-done((bf16[128,1024]{1,0:T(8,128)(2,1)S(1)}, bf16[128,1024]{1,0:T(8,128)(2,1)S(1)}, u32[]{:S(2)}, u32[]{:S(2)}) %collective-permute-start.6) | collective-permute-done | bytes 262176 | tf_op jit(solution)/shard_map/ppermute | solution.py:629
  33.7 2.0 %collective-permute-start.8 = (bf16[128,1024]{1,0:T(8,128)(2,1)S(1)}, bf16[128,1024]{1,0:T(8,128)(2,1)S(1)}, u32[]{:S(2)}, u32[]{:S(2)}) collective-permute-start(bf16[128,1024]{1,0:T(8,128)(2,1)S(1)} %collective-permute-done.6.refs_4_), channel_id=1, source_target_pairs={{0,8},{8,0},{16,24},{24,16},{1,9},{9,1},{17,25},{25,17},{2,10},{10... | collective-permute-start | bytes 786440 | tf_op jit(solution)/shard_map/ppermute | solution.py:629
  35.7 4.0 %upper_stats.1 = (f32[2,1,512]{2,1,0:T(1,128)S(1)}, f32[2,128,512]{2,1,0:T(8,128)S(1)}, bf16[2,1024,1024]{2,1,0:T(8,128)(2,1)S(1)}, bf16[2048,512]{1,0:T(8,128)(2,1)S(1)}) custom-call(s32[16]{0:T(128)S(1)} %copy-done.1, s32[8]{0:T(128)S(1)} %copy-done.2, bf16[256,1024]{1,0:T(8,128)(2,1)S(1)} %project.1.q_ref, bf16[256,512]{1,0:T(8,128)(2,1)S(1)} %project_kv.1.refs_0_, ...), custom_call_target="tpu_custom_call" | custom-call | bytes 1 | tf_op jit(solution)/shard_map/upper_stats/pallas_call | solution.py:480
  39.7 2.8 %lower_stats.1 = (f32[2,1,512]{2,1,0:T(1,128)S(1)}, f32[2,128,512]{2,1,0:T(8,128)S(1)}, bf16[2,1024,1024]{2,1,0:T(8,128)(2,1)S(1)}) custom-call(s32[16]{0:T(128)S(1)} %copy-done.1, s32[8]{0:T(128)S(1)} %copy-done.2, bf16[256,1024]{1,0:T(8,128)(2,1)S(1)} %project.1.q_ref, bf16[2048,512]{1,0:T(8,128)(2,1)S(1)} %get-tuple-element.217.refs_0_.refs_1_, ...), custom_call_target="tpu_custom_call" | custom-call | bytes 1 | tf_op jit(solution)/shard_map/lower_stats/pallas_call | solution.py:480
  42.6 1.9 %context_grad.2.refs_0_ = f32[256,1024]{1,0:T(8,128)S(1)} custom-call(bf16[256,1024]{1,0:T(8,128)(2,1)S(1)} %copy-done, bf16[128,1024]{1,0:T(8,128)(2,1)S(1)} %collective-permute-done.2.refs_1_, bf16[128,1024]{1,0:T(8,128)(2,1)S(1)} %collective-permute-done.7.refs_2_, bf16[128,1024]{1,0:T(8,128)(2,1)S(1)} %collective-permute-done.1.refs_3_, ...), custom_call_target="tpu_custom_call" | custom-call | bytes 1 | tf_op jit(solution)/shard_map/context_grad/pallas_call | solution.py:173
  44.5 0.4 collective-permute-done.8.refs_2_
  44.8 0.7 context_grad.3.g_ref
  45.6 5.0 %upper_grads.1 = (bf16[128,1024]{1,0:T(8,128)(2,1)S(1)}, bf16[4,128,512]{2,1,0:T(8,128)(2,1)S(1)}, bf16[2,128,512]{2,1,0:T(8,128)(2,1)S(1)}, bf16[2,128,512]{2,1,0:T(8,128)(2,1)S(1)}, f32[2048,512]{1,0:T(8,128)S(1)}) custom-call(s32[16]{0:T(128)S(1)} %copy-done.1, s32[8]{0:T(128)S(1)} %copy-done.2, bf16[256,1024]{1,0:T(8,128)(2,1)S(1)} %project.1.q_ref, ...), custom_call_target="tpu_custom_call" | custom-call | bytes 1 | tf_op jit(solution)/shard_map/upper_grads/pallas_call | solution.py:610
  50.7 0.5 collective-permute-start.14
  51.2 1.0 collective-permute-done.13.refs_0_
  52.2 0.4 collective-permute-done.14.refs_1_
  52.8 2.0 %collective-permute-start.16 = (bf16[128,512]{1,0:T(8,128)(2,1)S(1)}, bf16[128,512]{1,0:T(8,128)(2,1)S(1)}, u32[]{:S(2)}, u32[]{:S(2)}) collective-permute-start(bf16[128,512]{1,0:T(8,128)(2,1)S(1)} %get-tuple-element.230), channel_id=1, source_target_pairs={{0,4},{1,5},{2,6},{3,7},{4,0},{5,1},{6,2},{7,3},{8,12},{9,13},{10,... | collective-permute-start | bytes 393224 | tf_op jit(solution)/shard_map/ppermute | solution.py:629
  54.8 1.5 %collective-permute-start.17 = (bf16[128,512]{1,0:T(8,128)(2,1)S(1)}, bf16[128,512]{1,0:T(8,128)(2,1)S(1)}, u32[]{:S(2)}, u32[]{:S(2)}) collective-permute-start(bf16[128,512]{1,0:T(8,128)(2,1)S(1)} %get-tuple-element.231), channel_id=1, source_target_pairs={{0,6},{1,7},{2,4},{3,5},{4,2},{5,3},{6,0},{7,1},{8,14},{9,15},{10,... | collective-permute-start | bytes 393224 | tf_op jit(solution)/shard_map/ppermute | solution.py:629
  56.3 3.4 %lower_grads.1 = (bf16[128,1024]{1,0:T(8,128)(2,1)S(1)}, bf16[4,128,512]{2,1,0:T(8,128)(2,1)S(1)}, bf16[2,128,512]{2,1,0:T(8,128)(2,1)S(1)}, bf16[2,128,512]{2,1...) custom-call(s32[16]{0:T(128)S(1)} %copy-done.1, ...), custom_call_target="tpu_custom_call" | custom-call | bytes 1 | tf_op jit(solution)/shard_map/lower_grads/pallas_call | solution.py:610
  59.7 0.5 collective-permute-start.19
  60.2 1.3 %query_terms.2 = (f32[2,128,1024]{2,1,0:T(8,128)S(1)}, f32[2,128,1024]{2,1,0:T(8,128)S(1)}) custom-call(bf16[128,1024]{1,0:T(8,128)(2,1)S(1)} %get-tuple-element.246.upper_ref, bf16[128,1024]{1,0:T(8,128)(2,1)S(1)} %get-tuple-element.247.lower_ref, bf16[2,1024,1024]{2,1,0:T(8,128)(2,1)S(1)} %get-tuple-element.225.w_ref), custom_call_target="tpu_custom_call" | custom-call | bytes 1 | tf_op jit(solution)/shard_map/query_terms/pallas_call | solution.py:233
  61.6 0.8 all_terms.4
  62.5 0.1 pair_sums.3
  62.6 1.4 %collective-permute-start.20 = (bf16[128,512]{1,0:T(8,128)(2,1)S(1)}, bf16[128,512]{1,0:T(8,128)(2,1)S(1)}, u32[]{:S(2)}, u32[]{:S(2)}) collective-permute-start(bf16[128,512]{1,0:T(8,128)(2,1)S(1)} %get-tuple-element.259), channel_id=1, source_target_pairs={{0,2},{1,3},{2,0},{3,1},{4,6},{5,7},{6,4},{7,5},{8,10},{9,11},{10,... | collective-permute-start | bytes 393224 | tf_op jit(solution)/shard_map/ppermute | solution.py:629
  64.0 1.8 %collective-permute-start.21 = (bf16[128,512]{1,0:T(8,128)(2,1)S(1)}, bf16[128,512]{1,0:T(8,128)(2,1)S(1)}, u32[]{:S(2)}, u32[]{:S(2)}) collective-permute-start(bf16[128,512]{1,0:T(8,128)(2,1)S(1)} %get-tuple-element.260), channel_id=1, source_target_pairs={{0,4},{1,5},{2,6},{3,7},{4,0},{5,1},{6,2},{7,3},{8,12},{9,13},{10,... | collective-permute-start | bytes 393224 | tf_op jit(solution)/shard_map/ppermute | solution.py:629
  65.8 0.4 collective-permute-start.22
  66.2 3.1 %query_terms.3 = (f32[2,128,1024]{2,1,0:T(8,128)S(1)}, f32[2,128,1024]{2,1,0:T(8,128)S(1)}) custom-call(bf16[128,1024]{1,0:T(8,128)(2,1)S(1)} %get-tuple-element.246.upper_ref, bf16[128,1024]{1,0:T(8,128)(2,1)S(1)} %get-tuple-element.247.lower_ref, bf16[4096,1024]{1,0:T(8,128)(2,1)} %w_ref.1), custom_call_target="tpu_custom_call" | custom-call | bytes 1 | tf_op jit(solution)/shard_map/query_terms/pallas_call | solution.py:233
  69.3 2.4 %all_terms.5 = (bf16[128,1024]{1,0:T(8,128)(2,1)S(1)}, bf16[128,1024]{1,0:T(8,128)(2,1)S(1)}) custom-call(f32[2,128,1024]{2,1,0:T(8,128)S(1)} %get-tuple-element.250.first_ref, bf16[128,512]{1,0:T(8,128)(2,1)S(1)} %get-tuple-element.251.refs_0_, bf16[128,512]{1,0:T(8,128)(2,1)S(1)} %collective-permute-done.15.refs_1_, ...), custom_call_target="tpu_custom_call" | custom-call | bytes 1 | tf_op jit(solution)/shard_map/all_terms/pallas_call | solution.py:282
  71.7 0.4 collective-permute-done.21.refs_2_
  72.1 0.8 all_terms.6
  72.9 1.8 %collective-permute-start.24 = (bf16[128,1024]{1,0:T(8,128)(2,1)S(1)}, bf16[128,1024]{1,0:T(8,128)(2,1)S(1)}, u32[]{:S(2)}, u32[]{:S(2)}) collective-permute-start(bf16[128,1024]{1,0:T(8,128)(2,1)S(1)} %get-tuple-element.269), channel_id=1, source_target_pairs={{0,8},{8,0},{16,24},{24,16},{1,9},{9,1},{17,25},{25,17},{2,10},{10... | collective-permute-start | bytes 786440 | tf_op jit(solution)/shard_map/ppermute | solution.py:629
  74.7 2.6 %collective-permute-done.23.b_ref = bf16[2,128,1024]{2,1,0:T(8,128)(2,1)S(1)} collective-permute-done((bf16[2,128,1024]{2,1,0:T(8,128)(2,1)S(1)}, bf16[2,128,1024]{2,1,0:T(8,128)(2,1)S(1)}, u32[]{:S(2)}, u32[]{:S(2)}) %collective-permute-start.23) | collective-permute-done | bytes 524320 | tf_op jit(solution)/shard_map/ppermute | solution.py:629
  77.4 2.4 %all_terms.7 = (bf16[128,1024]{1,0:T(8,128)(2,1)S(1)}, bf16[128,1024]{1,0:T(8,128)(2,1)S(1)}) custom-call(f32[2,128,1024]{2,1,0:T(8,128)S(1)} %get-tuple-element.273.first_ref, bf16[128,512]{1,0:T(8,128)(2,1)S(1)} %get-tuple-element.274.refs_0_, bf16[128,512]{1,0:T(8,128)(2,1)S(1)} %collective-permute-done.20.refs_1_, ...), custom_call_target="tpu_custom_call" | custom-call | bytes 1 | tf_op jit(solution)/shard_map/all_terms/pallas_call | solution.py:282
  79.7 5.1 %collective-permute-done.24.b_ref = bf16[128,1024]{1,0:T(8,128)(2,1)S(1)} collective-permute-done((bf16[128,1024]{1,0:T(8,128)(2,1)S(1)}, bf16[128,1024]{1,0:T(8,128)(2,1)S(1)}, u32[]{:S(2)}, u32[]{:S(2)}) %collective-permute-start.24) | collective-permute-done | bytes 262176 | tf_op jit(solution)/shard_map/ppermute | solution.py:629
  84.9 0.3 collective-permute-start.26
  85.3 2.5 %collective-permute-start.27 = (bf16[128,1024]{1,0:T(8,128)(2,1)S(1)}, bf16[128,1024]{1,0:T(8,128)(2,1)S(1)}, u32[]{:S(2)}, u32[]{:S(2)}) collective-permute-start(bf16[128,1024]{1,0:T(8,128)(2,1)S(1)} %get-tuple-element.292), channel_id=1, source_target_pairs={{0,8},{8,0},{16,24},{24,16},{1,9},{9,1},{17,25},{25,17},{2,10},{10... | collective-permute-start | bytes 786440 | tf_op jit(solution)/shard_map/ppermute | solution.py:629
  87.8 9.9 %collective-permute-done.25.b_ref = bf16[128,1024]{1,0:T(8,128)(2,1)S(1)} collective-permute-done((bf16[128,1024]{1,0:T(8,128)(2,1)S(1)}, bf16[128,1024]{1,0:T(8,128)(2,1)S(1)}, u32[]{:S(2)}, u32[]{:S(2)}) %collective-permute-start.25) | collective-permute-done | bytes 262176 | tf_op jit(solution)/shard_map/ppermute | solution.py:629
  97.7 4.0 %collective-permute-done.26.b_ref = bf16[128,1024]{1,0:T(8,128)(2,1)S(1)} collective-permute-done((bf16[128,1024]{1,0:T(8,128)(2,1)S(1)}, bf16[128,1024]{1,0:T(8,128)(2,1)S(1)}, u32[]{:S(2)}, u32[]{:S(2)}) %collective-permute-start.26) | collective-permute-done | bytes 262176 | tf_op jit(solution)/shard_map/ppermute | solution.py:629
  101.8 1.4 %join_rows.1 = bf16[256,1024]{1,0:T(8,128)(2,1)} custom-call(s32[16]{0:T(128)S(1)} %copy-done.1, f32[128,1024]{1,0:T(8,128)S(1)} %merge.4.refs_0_, f32[128,1024]{1,0:T(8,128)S(1)} %merge.5.refs_1_, bf16[128,1024]{1,0:T(8,128)(2,1)S(1)} %collective-permute-done.27.refs_2_), custom_call_target="tpu_custom_call" | custom-call | bytes 1 | tf_op jit(solution)/shard_map/join_rows/pallas_call | solution.py:349
  (37 shorter events, 1.0 us)
Async XLA Ops:
  1.1 14.9 %collective-permute-start.2 = (bf16[128,1024]{1,0:T(8,128)(2,1)S(1)}, bf16[128,1024]{1,0:T(8,128)(2,1)S(1)}, u32[]{:S(2)}, u32[]{:S(2)}) collective-permute-start(bf16[128,1024]{1,0:T(8,128)(2,1)S(1)} %get-tuple-element.294), channel_id=1, source_target_pairs={{0,8},{8,0},{16,24},{24,16},{1,9},{9,1},{17,25},{25,17},{2,10},{10... | collective-permute-start | bytes 786440 | tf_op jit(solution)/shard_map/ppermute | solution.py:629
  4.2 14.3 %collective-permute-start.1 = (bf16[128,1024]{1,0:T(8,128)(2,1)S(1)}, bf16[128,1024]{1,0:T(8,128)(2,1)S(1)}, u32[]{:S(2)}, u32[]{:S(2)}) collective-permute-start(bf16[128,1024]{1,0:T(8,128)(2,1)S(1)} %get-tuple-element.294), channel_id=1, source_target_pairs={{0,16},{8,24},{16,0},{24,8},{1,17},{9,25},{17,1},{25,9},{2,18},{10... | collective-permute-start | bytes 786440 | tf_op jit(solution)/shard_map/ppermute | solution.py:629
  10.1 8.4 %collective-permute-start = (bf16[256,512]{1,0:T(8,128)(2,1)S(1)}, bf16[256,512]{1,0:T(8,128)(2,1)S(1)}, u32[]{:S(2)}, u32[]{:S(2)}) collective-permute-start(bf16[256,512]{1,0:T(8,128)(2,1)S(1)} %project_kv.1.refs_0_), channel_id=1, source_target_pairs={{0,2},{1,3},{2,0},{3,1},{4,6},{5,7},{6,4},{7,5},{8,10},{9,11},{10,... | collective-permute-start | bytes 786440 | tf_op jit(solution)/shard_map/ppermute | solution.py:629
  11.6 16.4 %collective-permute-start.4 = (bf16[256,512]{1,0:T(8,128)(2,1)S(1)}, bf16[256,512]{1,0:T(8,128)(2,1)S(1)}, u32[]{:S(2)}, u32[]{:S(2)}) collective-permute-start(bf16[256,512]{1,0:T(8,128)(2,1)S(1)} %project_kv.1.refs_0_), channel_id=1, source_target_pairs={{0,4},{1,5},{2,6},{3,7},{4,0},{5,1},{6,2},{7,3},{8,12},{9,13},{10,... | collective-permute-start | bytes 786440 | tf_op jit(solution)/shard_map/ppermute | solution.py:629
  18.5 9.5 %collective-permute-start.5 = (bf16[256,512]{1,0:T(8,128)(2,1)S(1)}, bf16[256,512]{1,0:T(8,128)(2,1)S(1)}, u32[]{:S(2)}, u32[]{:S(2)}) collective-permute-start(bf16[256,512]{1,0:T(8,128)(2,1)S(1)} %collective-permute-done.refs_1_), channel_id=1, source_target_pairs={{0,4},{1,5},{2,6},{3,7},{4,0},{5,1},{6,2},{7,3},{8,12},{9,13},{10,... | collective-permute-start | bytes 786440 | tf_op jit(solution)/shard_map/ppermute | solution.py:629
  20.0 15.7 %copy-start.1 = (s32[16]{0:T(128)S(1)}, s32[16]{0:T(128)}, u32[]{:S(2)}) copy-start(s32[16]{0:T(128)} %order.9) | copy-start | bytes 196
  20.0 15.7 %copy-start.2 = (s32[8]{0:T(128)S(1)}, s32[8]{0:T(128)}, u32[]{:S(2)}) copy-start(s32[8]{0:T(128)} %lengths.7) | copy-start | bytes 100
  20.0 9.8 %collective-permute-start.7 = (bf16[128,1024]{1,0:T(8,128)(2,1)S(1)}, bf16[128,1024]{1,0:T(8,128)(2,1)S(1)}, u32[]{:S(2)}, u32[]{:S(2)}) collective-permute-start(bf16[128,1024]{1,0:T(8,128)(2,1)S(1)} %get-tuple-element.293), channel_id=1, source_target_pairs={{0,8},{8,0},{16,24},{24,16},{1,9},{9,1},{17,25},{25,17},{2,10},{10... | collective-permute-start | bytes 786440 | tf_op jit(solution)/shard_map/ppermute | solution.py:629
  20.5 13.2 %collective-permute-start.6 = (bf16[128,1024]{1,0:T(8,128)(2,1)S(1)}, bf16[128,1024]{1,0:T(8,128)(2,1)S(1)}, u32[]{:S(2)}, u32[]{:S(2)}) collective-permute-start(bf16[128,1024]{1,0:T(8,128)(2,1)S(1)} %get-tuple-element.293), channel_id=1, source_target_pairs={{0,16},{8,24},{16,0},{24,8},{1,17},{9,25},{17,1},{25,9},{2,18},{10... | collective-permute-start | bytes 786440 | tf_op jit(solution)/shard_map/ppermute | solution.py:629
  28.0 5.6 %collective-permute-start.9 = (bf16[256,512]{1,0:T(8,128)(2,1)S(1)}, bf16[256,512]{1,0:T(8,128)(2,1)S(1)}, u32[]{:S(2)}, u32[]{:S(2)}) collective-permute-start(bf16[256,512]{1,0:T(8,128)(2,1)S(1)} %project_kv.1.refs_0_), channel_id=1, source_target_pairs={{0,1},{1,0},{2,3},{3,2},{4,5},{5,4},{6,7},{7,6},{8,9},{9,8},{10,11... | collective-permute-start | bytes 786440 | tf_op jit(solution)/shard_map/ppermute | solution.py:629
  28.1 7.6 %collective-permute-start.10 = (bf16[256,512]{1,0:T(8,128)(2,1)S(1)}, bf16[256,512]{1,0:T(8,128)(2,1)S(1)}, u32[]{:S(2)}, u32[]{:S(2)}) collective-permute-start(bf16[256,512]{1,0:T(8,128)(2,1)S(1)} %collective-permute-done.refs_1_), channel_id=1, source_target_pairs={{0,1},{1,0},{2,3},{3,2},{4,5},{5,4},{6,7},{7,6},{8,9},{9,8},{10,11... | collective-permute-start | bytes 786440 | tf_op jit(solution)/shard_map/ppermute | solution.py:629
  28.6 7.1 %collective-permute-start.11 = (bf16[256,512]{1,0:T(8,128)(2,1)S(1)}, bf16[256,512]{1,0:T(8,128)(2,1)S(1)}, u32[]{:S(2)}, u32[]{:S(2)}) collective-permute-start(bf16[256,512]{1,0:T(8,128)(2,1)S(1)} %collective-permute-done.4.refs_2_), channel_id=1, source_target_pairs={{0,1},{1,0},{2,3},{3,2},{4,5},{5,4},{6,7},{7,6},{8,9},{9,8},{10,11... | collective-permute-start | bytes 786440 | tf_op jit(solution)/shard_map/ppermute | solution.py:629
  29.8 5.9 %collective-permute-start.12 = (bf16[256,512]{1,0:T(8,128)(2,1)S(1)}, bf16[256,512]{1,0:T(8,128)(2,1)S(1)}, u32[]{:S(2)}, u32[]{:S(2)}) collective-permute-start(bf16[256,512]{1,0:T(8,128)(2,1)S(1)} %collective-permute-done.5.refs_3_), channel_id=1, source_target_pairs={{0,1},{1,0},{2,3},{3,2},{4,5},{5,4},{6,7},{7,6},{8,9},{9,8},{10,11... | collective-permute-start | bytes 786440 | tf_op jit(solution)/shard_map/ppermute | solution.py:629
  33.7 10.8 %collective-permute-start.3 = (bf16[128,1024]{1,0:T(8,128)(2,1)S(1)}, bf16[128,1024]{1,0:T(8,128)(2,1)S(1)}, u32[]{:S(2)}, u32[]{:S(2)}) collective-permute-start(bf16[128,1024]{1,0:T(8,128)(2,1)S(1)} %collective-permute-done.1.refs_3_), channel_id=1, source_target_pairs={{0,8},{8,0},{16,24},{24,16},{1,9},{9,1},{17,25},{25,17},{2,10},{10... | collective-permute-start | bytes 786440 | tf_op jit(solution)/shard_map/ppermute | solution.py:629
  33.7 11.2 %collective-permute-start.8 = (bf16[128,1024]{1,0:T(8,128)(2,1)S(1)}, bf16[128,1024]{1,0:T(8,128)(2,1)S(1)}, u32[]{:S(2)}, u32[]{:S(2)}) collective-permute-start(bf16[128,1024]{1,0:T(8,128)(2,1)S(1)} %collective-permute-done.6.refs_4_), channel_id=1, source_target_pairs={{0,8},{8,0},{16,24},{24,16},{1,9},{9,1},{17,25},{25,17},{2,10},{10... | collective-permute-start | bytes 786440 | tf_op jit(solution)/shard_map/ppermute | solution.py:629
  39.7 2.9 %copy-start = (bf16[256,1024]{1,0:T(8,128)(2,1)S(1)}, bf16[256,1024]{1,0:T(8,128)(2,1)}, u32[]{:S(2)}) copy-start(bf16[256,1024]{1,0:T(8,128)(2,1)} %refs_0_) | copy-start | bytes 1572868
  50.6 1.6 %collective-permute-start.13 = (bf16[2,128,512]{2,1,0:T(8,128)(2,1)S(1)}, bf16[2,128,512]{2,1,0:T(8,128)(2,1)S(1)}, u32[]{:S(2)}, u32[]{:S(2)}) collective-permute-start(bf16[2,128,512]{2,1,0:T(8,128)(2,1)S(1)} %get-tuple-element.204), channel_id=1, source_target_pairs={{0,1},{1,0},{2,3},{3,2},{4,5},{5,4},{6,7},{7,6},{8,9},{9,8},{10,11... | collective-permute-start | bytes 786440 | tf_op jit(solution)/shard_map/ppermute | solution.py:629
  50.7 1.9 %collective-permute-start.14 = (bf16[2,128,512]{2,1,0:T(8,128)(2,1)S(1)}, bf16[2,128,512]{2,1,0:T(8,128)(2,1)S(1)}, u32[]{:S(2)}, u32[]{:S(2)}) collective-permute-start(bf16[2,128,512]{2,1,0:T(8,128)(2,1)S(1)} %get-tuple-element.205), channel_id=1, source_target_pairs={{0,1},{1,0},{2,3},{3,2},{4,5},{5,4},{6,7},{7,6},{8,9},{9,8},{10,11... | collective-permute-start | bytes 786440 | tf_op jit(solution)/shard_map/ppermute | solution.py:629
  52.7 8.8 %collective-permute-start.15 = (bf16[128,512]{1,0:T(8,128)(2,1)S(1)}, bf16[128,512]{1,0:T(8,128)(2,1)S(1)}, u32[]{:S(2)}, u32[]{:S(2)}) collective-permute-start(bf16[128,512]{1,0:T(8,128)(2,1)S(1)} %get-tuple-element.229), channel_id=1, source_target_pairs={{0,2},{1,3},{2,0},{3,1},{4,6},{5,7},{6,4},{7,5},{8,10},{9,11},{10,... | collective-permute-start | bytes 393224 | tf_op jit(solution)/shard_map/ppermute | solution.py:629
  52.8 8.8 %collective-permute-start.16 = (bf16[128,512]{1,0:T(8,128)(2,1)S(1)}, bf16[128,512]{1,0:T(8,128)(2,1)S(1)}, u32[]{:S(2)}, u32[]{:S(2)}) collective-permute-start(bf16[128,512]{1,0:T(8,128)(2,1)S(1)} %get-tuple-element.230), channel_id=1, source_target_pairs={{0,4},{1,5},{2,6},{3,7},{4,0},{5,1},{6,2},{7,3},{8,12},{9,13},{10,... | collective-permute-start | bytes 393224 | tf_op jit(solution)/shard_map/ppermute | solution.py:629
  54.8 6.8 %collective-permute-start.17 = (bf16[128,512]{1,0:T(8,128)(2,1)S(1)}, bf16[128,512]{1,0:T(8,128)(2,1)S(1)}, u32[]{:S(2)}, u32[]{:S(2)}) collective-permute-start(bf16[128,512]{1,0:T(8,128)(2,1)S(1)} %get-tuple-element.231), channel_id=1, source_target_pairs={{0,6},{1,7},{2,4},{3,5},{4,2},{5,3},{6,0},{7,1},{8,14},{9,15},{10,... | collective-permute-start | bytes 393224 | tf_op jit(solution)/shard_map/ppermute | solution.py:629
  59.6 2.8 %collective-permute-start.18 = (bf16[2,128,512]{2,1,0:T(8,128)(2,1)S(1)}, bf16[2,128,512]{2,1,0:T(8,128)(2,1)S(1)}, u32[]{:S(2)}, u32[]{:S(2)}) collective-permute-start(bf16[2,128,512]{2,1,0:T(8,128)(2,1)S(1)} %get-tuple-element.240), channel_id=1, source_target_pairs={{0,1},{1,0},{2,3},{3,2},{4,5},{5,4},{6,7},{7,6},{8,9},{9,8},{10,11... | collective-permute-start | bytes 786440 | tf_op jit(solution)/shard_map/ppermute | solution.py:629
  59.7 2.7 %collective-permute-start.19 = (bf16[2,128,512]{2,1,0:T(8,128)(2,1)S(1)}, bf16[2,128,512]{2,1,0:T(8,128)(2,1)S(1)}, u32[]{:S(2)}, u32[]{:S(2)}) collective-permute-start(bf16[2,128,512]{2,1,0:T(8,128)(2,1)S(1)} %get-tuple-element.241), channel_id=1, source_target_pairs={{0,1},{1,0},{2,3},{3,2},{4,5},{5,4},{6,7},{7,6},{8,9},{9,8},{10,11... | collective-permute-start | bytes 786440 | tf_op jit(solution)/shard_map/ppermute | solution.py:629
  62.4 14.8 %collective-permute-start.23 = (bf16[2,128,1024]{2,1,0:T(8,128)(2,1)S(1)}, bf16[2,128,1024]{2,1,0:T(8,128)(2,1)S(1)}, u32[]{:S(2)}, u32[]{:S(2)}) collective-permute-start(bf16[2,128,1024]{2,1,0:T(8,128)(2,1)S(1)} %all_terms.4), channel_id=1, source_target_pairs={{0,8},{8,0},{16,24},{24,16},{1,9},{9,1},{17,25},{25,17},{2,10},{10... | collective-permute-start | bytes 1572872 | tf_op jit(solution)/shard_map/ppermute | solution.py:629
  62.6 9.0 %collective-permute-start.20 = (bf16[128,512]{1,0:T(8,128)(2,1)S(1)}, bf16[128,512]{1,0:T(8,128)(2,1)S(1)}, u32[]{:S(2)}, u32[]{:S(2)}) collective-permute-start(bf16[128,512]{1,0:T(8,128)(2,1)S(1)} %get-tuple-element.259), channel_id=1, source_target_pairs={{0,2},{1,3},{2,0},{3,1},{4,6},{5,7},{6,4},{7,5},{8,10},{9,11},{10,... | collective-permute-start | bytes 393224 | tf_op jit(solution)/shard_map/ppermute | solution.py:629
  64.0 8.1 %collective-permute-start.21 = (bf16[128,512]{1,0:T(8,128)(2,1)S(1)}, bf16[128,512]{1,0:T(8,128)(2,1)S(1)}, u32[]{:S(2)}, u32[]{:S(2)}) collective-permute-start(bf16[128,512]{1,0:T(8,128)(2,1)S(1)} %get-tuple-element.260), channel_id=1, source_target_pairs={{0,4},{1,5},{2,6},{3,7},{4,0},{5,1},{6,2},{7,3},{8,12},{9,13},{10,... | collective-permute-start | bytes 393224 | tf_op jit(solution)/shard_map/ppermute | solution.py:629
  65.8 6.3 %collective-permute-start.22 = (bf16[128,512]{1,0:T(8,128)(2,1)S(1)}, bf16[128,512]{1,0:T(8,128)(2,1)S(1)}, u32[]{:S(2)}, u32[]{:S(2)}) collective-permute-start(bf16[128,512]{1,0:T(8,128)(2,1)S(1)} %get-tuple-element.261), channel_id=1, source_target_pairs={{0,6},{1,7},{2,4},{3,5},{4,2},{5,3},{6,0},{7,1},{8,14},{9,15},{10,... | collective-permute-start | bytes 393224 | tf_op jit(solution)/shard_map/ppermute | solution.py:629
  72.9 11.9 %collective-permute-start.24 = (bf16[128,1024]{1,0:T(8,128)(2,1)S(1)}, bf16[128,1024]{1,0:T(8,128)(2,1)S(1)}, u32[]{:S(2)}, u32[]{:S(2)}) collective-permute-start(bf16[128,1024]{1,0:T(8,128)(2,1)S(1)} %get-tuple-element.269), channel_id=1, source_target_pairs={{0,8},{8,0},{16,24},{24,16},{1,9},{9,1},{17,25},{25,17},{2,10},{10... | collective-permute-start | bytes 786440 | tf_op jit(solution)/shard_map/ppermute | solution.py:629
  77.3 20.4 %collective-permute-start.25 = (bf16[128,1024]{1,0:T(8,128)(2,1)S(1)}, bf16[128,1024]{1,0:T(8,128)(2,1)S(1)}, u32[]{:S(2)}, u32[]{:S(2)}) collective-permute-start(bf16[128,1024]{1,0:T(8,128)(2,1)S(1)} %add.2), channel_id=1, source_target_pairs={{0,16},{8,24},{16,0},{24,8},{1,17},{9,25},{17,1},{25,9},{2,18},{10... | collective-permute-start | bytes 786440 | tf_op jit(solution)/shard_map/ppermute | solution.py:629
  84.9 16.8 %collective-permute-start.26 = (bf16[128,1024]{1,0:T(8,128)(2,1)S(1)}, bf16[128,1024]{1,0:T(8,128)(2,1)S(1)}, u32[]{:S(2)}, u32[]{:S(2)}) collective-permute-start(bf16[128,1024]{1,0:T(8,128)(2,1)S(1)} %add.3), channel_id=1, source_target_pairs={{0,16},{8,24},{16,0},{24,8},{1,17},{9,25},{17,1},{25,9},{2,18},{10... | collective-permute-start | bytes 786440 | tf_op jit(solution)/shard_map/ppermute | solution.py:629
  85.3 16.5 %collective-permute-start.27 = (bf16[128,1024]{1,0:T(8,128)(2,1)S(1)}, bf16[128,1024]{1,0:T(8,128)(2,1)S(1)}, u32[]{:S(2)}, u32[]{:S(2)}) collective-permute-start(bf16[128,1024]{1,0:T(8,128)(2,1)S(1)} %get-tuple-element.292), channel_id=1, source_target_pairs={{0,8},{8,0},{16,24},{24,16},{1,9},{9,1},{17,25},{25,17},{2,10},{10... | collective-permute-start | bytes 786440 | tf_op jit(solution)/shard_map/ppermute | solution.py:629

commit v4 on v3

--- a/solution.py
+++ b/solution.py
@@ -14,9 +14,7 @@
 
 masked_score = -1e30
 MIB = 1 << 20
-COST = 0
 AT_ONCE = 4
-PARTS = 2
 VMEM = pltpu.VMEM
 HBM = pltpu.HBM
 
@@ -37,8 +35,8 @@
     return pltpu.CompilerParams(vmem_limit_bytes=24 * MIB)
 
 
-def cost(micros):
-    return pl.CostEstimate(flops=int(micros * COST), bytes_accessed=1, transcendentals=0)
+def cost():
+    return pl.CostEstimate(flops=0, bytes_accessed=1, transcendentals=0)
 
 
 def upper_half(order):
@@ -101,7 +99,7 @@
             pltpu.SemaphoreType.DMA((parts, 3)),
         ],
         compiler_params=params(),
-        cost_estimate=cost(3.4),
+        cost_estimate=cost(),
         name="project_kv",
     )(in_hbm(x), in_hbm(wk), in_hbm(wv))
 
@@ -146,7 +144,7 @@
             pltpu.SemaphoreType.DMA((parts, 2)),
         ],
         compiler_params=params(),
-        cost_estimate=cost(4.9),
+        cost_estimate=cost(),
         name="project",
     )(in_hbm(x), in_hbm(w))
 
@@ -176,7 +174,7 @@
         out_specs=pl.BlockSpec(memory_space=VMEM),
         out_shape=jax.ShapeDtypeStruct((rows, stacks[0].shape[1]), dtype),
         compiler_params=params(),
-        cost_estimate=cost(3),
+        cost_estimate=cost(),
         name="context_grad",
     )(*operands)
 
@@ -238,7 +236,7 @@
         out_shape=[jax.ShapeDtypeStruct((size, rows, share), jnp.float32)] * 2,
         scratch_shapes=scratch,
         compiler_params=params(),
-        cost_estimate=cost(3),
+        cost_estimate=cost(),
         name="query_terms",
     )(upper, lower, w)
 
@@ -289,7 +287,7 @@
         else [jax.ShapeDtypeStruct((rows, share), jnp.bfloat16)] * size,
         scratch_shapes=scratch,
         compiler_params=params(),
-        cost_estimate=cost(2),
+        cost_estimate=cost(),
         name="all_terms",
     )(first, *terms, wk, wv)
 
@@ -309,7 +307,7 @@
         out_specs=pl.BlockSpec(memory_space=VMEM),
         out_shape=jax.ShapeDtypeStruct(a.shape, a.dtype),
         compiler_params=params(),
-        cost_estimate=cost(0.5),
+        cost_estimate=cost(),
         name="add",
     )(a, b)
 
@@ -325,7 +323,7 @@
         out_specs=pl.BlockSpec(memory_space=VMEM),
         out_shape=jax.ShapeDtypeStruct(a.shape, jnp.float32),
         compiler_params=params(),
-        cost_estimate=cost(0.5),
+        cost_estimate=cost(),
         name="merge",
     )(a, b)
 
@@ -353,7 +351,7 @@
         out_specs=pl.BlockSpec(memory_space=VMEM),
         out_shape=jax.ShapeDtypeStruct((2 * rows, width), jnp.bfloat16),
         compiler_params=params(),
-        cost_estimate=cost(1.5),
+        cost_estimate=cost(),
         name="join_rows",
     )(span_order, *blocks)
 
@@ -465,7 +463,8 @@
     for g in range(groups):
         top, (total, mixed) = tops[g], done[g]
         total = jnp.sum(total, axis=0, keepdims=True)
-        level_ref[g] = top * factor + jnp.log2(total)
+        level_ref[g, 0:1] = top
+        level_ref[g, 1:2] = jnp.log2(total)
         mixed_ref[g] = mixed / total
     for copy in copies:
         copy.wait()
@@ -484,7 +483,7 @@
         + [pl.BlockSpec(memory_space=HBM)],
         out_specs=[pl.BlockSpec(memory_space=VMEM)] * (4 if upper else 3),
         out_shape=[
-            jax.ShapeDtypeStruct((groups, 1, columns), jnp.float32),
+            jax.ShapeDtypeStruct((groups, 2, columns), jnp.float32),
             jax.ShapeDtypeStruct((groups, dim, columns), jnp.float32),
             jax.ShapeDtypeStruct((len(spare), w.shape[0], w.shape[1] // heads), w.dtype),
         ]
@@ -495,7 +494,7 @@
             pltpu.SemaphoreType.DMA((len(spare),)),
         ],
         compiler_params=params(),
-        cost_estimate=cost(2.4),
+        cost_estimate=cost(),
         name="upper_stats" if upper else "lower_stats",
     )(span_order, doc_lengths, q, *blocks, in_hbm(w))
 
@@ -535,7 +534,8 @@
     rows = pl.ds(pl.multiple_of(j * half, half), half)
     queries = [stack_heads(q_ref, rows, g, share, dim) for g in range(groups)]
     outs = [stack_heads(g_ref, rows, g, share, dim) for g in range(groups)]
-    levels = [level_ref[g] for g in range(groups)]
+    tops = [level_ref[g, 0:1] for g in range(groups)]
+    levels = [level_ref[g, 1:2] for g in range(groups)]
     deltas = []
     for g in range(groups):
         turned = jnp.concatenate(
@@ -552,8 +552,8 @@
         for g in range(groups):
             keys = block[:, g * dim : (g + 1) * dim]
             values = block[:, width + g * dim : width + (g + 1) * dim]
-            logits = mm_nt(keys, queries[g]) * factor
-            chance = keep(allowed, jnp.exp2(logits - levels[g]), 0.0)
+            logits = mm_nt(keys, queries[g])
+            chance = keep(allowed, jnp.exp2((logits - tops[g]) * factor - levels[g]), 0.0)
             slopes = mm_nt(values, outs[g])
             score = (chance * (slopes - deltas[g])).astype(jnp.bfloat16)
             key_term = mm(score, queries[g])
@@ -620,7 +620,7 @@
         ]
         + scratch,
         compiler_params=params(),
-        cost_estimate=cost(3.0),
+        cost_estimate=cost(),
         name="upper_grads" if upper else "lower_grads",
     )(span_order, doc_lengths, q, g, level, mixed, *blocks, *weights)
 
@@ -658,7 +658,7 @@
         out_specs=[pl.BlockSpec(memory_space=VMEM)] * count,
         out_shape=[jax.ShapeDtypeStruct((rows, width), jnp.bfloat16)] * count,
         compiler_params=params(),
-        cost_estimate=cost(0.7),
+        cost_estimate=cost(),
         name="pair_sums",
     )(even, *got)
 

time: 103 us -> 103 us (level)
  Pallas kernels: 38.7 us -> 37.5 us
    pallas_call x2, Pallas kernels: 6.83 us -> 5.72 us  [stats(): pl.pallas_call(functools.partial(stats_body, sizes, upper, spare), in_spe...]
  transfers between devices with their start and end apart: 28 -> 28, of which waited for: 12 -> 11; matrix products, arithmetic and copies ran while one was open for 0% -> 0% of each run, Pallas kernels for 30% -> 30%
where the time goes in v4:
time: 103 us
  Pallas kernels  37.5 us (36%)
  waiting for transfers between devices  34.8 us (34%)
  starting transfers between devices  29.4 us (29%)
  local copies, waits for them, and re-layouts  1.08 us (1%)
    ppermute x28, waiting for transfers between devices, swap(): lax.ppermute(x, axis, [(i, i ^ k) for i in range(lax.axis_size(axis))])  34.8 us
    ppermute x28, starting transfers between devices, swap(): lax.ppermute(x, axis, [(i, i ^ k) for i in range(lax.axis_size(axis))])  29.4 us
    pallas_call x2, Pallas kernels, grads(): pl.pallas_call(functools.partial(grads_body, sizes, upper, spare), in_spe...  8.39 us
    pallas_call x4, Pallas kernels, all_terms(): pl.pallas_call(functools.partial(all_terms_body, places, len(terms)), in_...  6.35 us
    pallas_call x2, Pallas kernels, stats(): pl.pallas_call(functools.partial(stats_body, sizes, upper, spare), in_spe...  5.72 us
    pallas_call x1, Pallas kernels, project(): pl.pallas_call(functools.partial(project_body, parts), in_specs=[pl.Block...  4.87 us
    pallas_call x2, Pallas kernels, query_terms(): pl.pallas_call(functools.partial(query_terms_body, places), in_specs=[pl....  4.38 us
    pallas_call x1, Pallas kernels, project_kv(): pl.pallas_call(functools.partial(kv_body, parts), in_specs=[pl.BlockSpec(...  3.32 us
  transfers between devices with their start and end apart: 28, of which 11 were waited for; matrix products, arithmetic and copies ran while one was open for 0% of the time, Pallas kernels for 30%

profile of v4, /device:TPU:0, one launch (start us, length us, event | category | flops | bytes accessed | tf_op | source)
XLA Modules:
  0.0 103.2 jit_solution(2140068507259886232)
XLA Ops:
  0.0 1.1 %fusion = (bf16[128,1024]{1,0:T(8,128)(2,1)S(1)}, bf16[128,1024]{1,0:T(8,128)(2,1)S(1)}) fusion(bf16[256,1024]{1,0:T(8,128)(2,1)} %refs_0_), kind=kLoop, calls=%fused_computation | loop fusion | bytes 1048576 | tf_op jit(solution)/shard_map/slice | solution.py:723
  1.1 3.1 %collective-permute-start.2 = (bf16[128,1024]{1,0:T(8,128)(2,1)S(1)}, bf16[128,1024]{1,0:T(8,128)(2,1)S(1)}, u32[]{:S(2)}, u32[]{:S(2)}) collective-permute-start(bf16[128,1024]{1,0:T(8,128)(2,1)S(1)} %get-tuple-element.294), channel_id=1, source_target_pairs={{0,8},{8,0},{16,24},{24,16},{1,9},{9,1},{17,25},{25,17},{2,10},{10... | collective-permute-start | bytes 786440 | tf_op jit(solution)/shard_map/ppermute | solution.py:629
  4.2 2.6 %collective-permute-start.1 = (bf16[128,1024]{1,0:T(8,128)(2,1)S(1)}, bf16[128,1024]{1,0:T(8,128)(2,1)S(1)}, u32[]{:S(2)}, u32[]{:S(2)}) collective-permute-start(bf16[128,1024]{1,0:T(8,128)(2,1)S(1)} %get-tuple-element.294), channel_id=1, source_target_pairs={{0,16},{8,24},{16,0},{24,8},{1,17},{9,25},{17,1},{25,9},{2,18},{10... | collective-permute-start | bytes 786440 | tf_op jit(solution)/shard_map/ppermute | solution.py:629
  6.7 3.3 %project_kv.1.refs_0_ = bf16[256,512]{1,0:T(8,128)(2,1)S(1)} custom-call(bf16[256,4096]{1,0:T(8,128)(2,1)} %x_ref.1, bf16[4096,256]{1,0:T(8,128)(2,1)} %refs_4_.2, bf16[4096,256]{1,0:T(8,128)(2,1)} %refs_5_.1), custom_call_target="tpu_custom_call" | custom-call | bytes 1 | tf_op jit(solution)/shard_map/project_kv/pallas_call | solution.py:89
  10.1 1.6 %collective-permute-start = (bf16[256,512]{1,0:T(8,128)(2,1)S(1)}, bf16[256,512]{1,0:T(8,128)(2,1)S(1)}, u32[]{:S(2)}, u32[]{:S(2)}) collective-permute-start(bf16[256,512]{1,0:T(8,128)(2,1)S(1)} %project_kv.1.refs_0_), channel_id=1, source_target_pairs={{0,2},{1,3},{2,0},{3,1},{4,6},{5,7},{6,4},{7,5},{8,10},{9,11},{10,... | collective-permute-start | bytes 786440 | tf_op jit(solution)/shard_map/ppermute | solution.py:629
  11.6 1.5 %collective-permute-start.4 = (bf16[256,512]{1,0:T(8,128)(2,1)S(1)}, bf16[256,512]{1,0:T(8,128)(2,1)S(1)}, u32[]{:S(2)}, u32[]{:S(2)}) collective-permute-start(bf16[256,512]{1,0:T(8,128)(2,1)S(1)} %project_kv.1.refs_0_), channel_id=1, source_target_pairs={{0,4},{1,5},{2,6},{3,7},{4,0},{5,1},{6,2},{7,3},{8,12},{9,13},{10,... | collective-permute-start | bytes 786440 | tf_op jit(solution)/shard_map/ppermute | solution.py:629
  13.2 2.8 %collective-permute-done.2.refs_1_ = bf16[128,1024]{1,0:T(8,128)(2,1)S(1)} collective-permute-done((bf16[128,1024]{1,0:T(8,128)(2,1)S(1)}, bf16[128,1024]{1,0:T(8,128)(2,1)S(1)}, u32[]{:S(2)}, u32[]{:S(2)}) %collective-permute-start.2) | collective-permute-done | bytes 262176 | tf_op jit(solution)/shard_map/ppermute | solution.py:629
  16.0 2.5 %collective-permute-done.1.refs_3_ = bf16[128,1024]{1,0:T(8,128)(2,1)S(1)} collective-permute-done((bf16[128,1024]{1,0:T(8,128)(2,1)S(1)}, bf16[128,1024]{1,0:T(8,128)(2,1)S(1)}, u32[]{:S(2)}, u32[]{:S(2)}) %collective-permute-start.1) | collective-permute-done | bytes 262176 | tf_op jit(solution)/shard_map/ppermute | solution.py:629
  18.5 1.5 %collective-permute-start.5 = (bf16[256,512]{1,0:T(8,128)(2,1)S(1)}, bf16[256,512]{1,0:T(8,128)(2,1)S(1)}, u32[]{:S(2)}, u32[]{:S(2)}) collective-permute-start(bf16[256,512]{1,0:T(8,128)(2,1)S(1)} %collective-permute-done.refs_1_), channel_id=1, source_target_pairs={{0,4},{1,5},{2,6},{3,7},{4,0},{5,1},{6,2},{7,3},{8,12},{9,13},{10,... | collective-permute-start | bytes 786440 | tf_op jit(solution)/shard_map/ppermute | solution.py:629
  20.0 0.4 collective-permute-start.7
  20.5 2.6 %collective-permute-start.6 = (bf16[128,1024]{1,0:T(8,128)(2,1)S(1)}, bf16[128,1024]{1,0:T(8,128)(2,1)S(1)}, u32[]{:S(2)}, u32[]{:S(2)}) collective-permute-start(bf16[128,1024]{1,0:T(8,128)(2,1)S(1)} %get-tuple-element.293), channel_id=1, source_target_pairs={{0,16},{8,24},{16,0},{24,8},{1,17},{9,25},{17,1},{25,9},{2,18},{10... | collective-permute-start | bytes 786440 | tf_op jit(solution)/shard_map/ppermute | solution.py:629
  23.1 4.9 %project.1.q_ref = bf16[256,1024]{1,0:T(8,128)(2,1)S(1)} custom-call(bf16[256,4096]{1,0:T(8,128)(2,1)} %x_ref.1, bf16[4096,1024]{1,0:T(8,128)(2,1)} %w_ref.1), custom_call_target="tpu_custom_call" | custom-call | bytes 1 | tf_op jit(solution)/shard_map/project/pallas_call | solution.py:135
  28.1 0.5 collective-permute-start.10
  28.7 1.2 %collective-permute-done.7.refs_2_ = bf16[128,1024]{1,0:T(8,128)(2,1)S(1)} collective-permute-done((bf16[128,1024]{1,0:T(8,128)(2,1)S(1)}, bf16[128,1024]{1,0:T(8,128)(2,1)S(1)}, u32[]{:S(2)}, u32[]{:S(2)}) %collective-permute-start.7) | collective-permute-done | bytes 262176 | tf_op jit(solution)/shard_map/ppermute | solution.py:629
  29.8 3.8 %collective-permute-done.6.refs_4_ = bf16[128,1024]{1,0:T(8,128)(2,1)S(1)} collective-permute-done((bf16[128,1024]{1,0:T(8,128)(2,1)S(1)}, bf16[128,1024]{1,0:T(8,128)(2,1)S(1)}, u32[]{:S(2)}, u32[]{:S(2)}) %collective-permute-start.6) | collective-permute-done | bytes 262176 | tf_op jit(solution)/shard_map/ppermute | solution.py:629
  33.7 2.0 %collective-permute-start.8 = (bf16[128,1024]{1,0:T(8,128)(2,1)S(1)}, bf16[128,1024]{1,0:T(8,128)(2,1)S(1)}, u32[]{:S(2)}, u32[]{:S(2)}) collective-permute-start(bf16[128,1024]{1,0:T(8,128)(2,1)S(1)} %collective-permute-done.6.refs_4_), channel_id=1, source_target_pairs={{0,8},{8,0},{16,24},{24,16},{1,9},{9,1},{17,25},{25,17},{2,10},{10... | collective-permute-start | bytes 786440 | tf_op jit(solution)/shard_map/ppermute | solution.py:629
  35.7 2.8 %upper_stats.1 = (f32[2,2,512]{2,1,0:T(2,128)S(1)}, f32[2,128,512]{2,1,0:T(8,128)S(1)}, bf16[2,1024,1024]{2,1,0:T(8,128)(2,1)S(1)}, bf16[2048,512]{1,0:T(8,128)(2,1)S(1)}) custom-call(s32[16]{0:T(128)S(1)} %copy-done.1, s32[8]{0:T(128)S(1)} %copy-done.2, bf16[256,1024]{1,0:T(8,128)(2,1)S(1)} %project.1.q_ref, bf16[256,512]{1,0:T(8,128)(2,1)S(1)} %project_kv.1.refs_0_, ...), custom_call_target="tpu_custom_call" | custom-call | bytes 1 | tf_op jit(solution)/shard_map/upper_stats/pallas_call | solution.py:479
  38.6 2.9 %lower_stats.1 = (f32[2,2,512]{2,1,0:T(2,128)S(1)}, f32[2,128,512]{2,1,0:T(8,128)S(1)}, bf16[2,1024,1024]{2,1,0:T(8,128)(2,1)S(1)}) custom-call(s32[16]{0:T(128)S(1)} %copy-done.1, s32[8]{0:T(128)S(1)} %copy-done.2, bf16[256,1024]{1,0:T(8,128)(2,1)S(1)} %project.1.q_ref, bf16[2048,512]{1,0:T(8,128)(2,1)S(1)} %get-tuple-element.217.refs_0_.refs_1_, ...), custom_call_target="tpu_custom_call" | custom-call | bytes 1 | tf_op jit(solution)/shard_map/lower_stats/pallas_call | solution.py:479
  41.5 1.8 %context_grad.2.refs_0_ = f32[256,1024]{1,0:T(8,128)S(1)} custom-call(bf16[256,1024]{1,0:T(8,128)(2,1)S(1)} %copy-done, bf16[128,1024]{1,0:T(8,128)(2,1)S(1)} %collective-permute-done.2.refs_1_, bf16[128,1024]{1,0:T(8,128)(2,1)S(1)} %collective-permute-done.7.refs_2_, bf16[128,1024]{1,0:T(8,128)(2,1)S(1)} %collective-permute-done.1.refs_3_, ...), custom_call_target="tpu_custom_call" | custom-call | bytes 1 | tf_op jit(solution)/shard_map/context_grad/pallas_call | solution.py:171
  43.3 1.5 %collective-permute-done.8.refs_2_ = bf16[128,1024]{1,0:T(8,128)(2,1)S(1)} collective-permute-done((bf16[128,1024]{1,0:T(8,128)(2,1)S(1)}, bf16[128,1024]{1,0:T(8,128)(2,1)S(1)}, u32[]{:S(2)}, u32[]{:S(2)}) %collective-permute-start.8) | collective-permute-done | bytes 262176 | tf_op jit(solution)/shard_map/ppermute | solution.py:629
  44.8 0.7 context_grad.3.g_ref
  45.6 3.9 %upper_grads.1 = (bf16[128,1024]{1,0:T(8,128)(2,1)S(1)}, bf16[4,128,512]{2,1,0:T(8,128)(2,1)S(1)}, bf16[2,128,512]{2,1,0:T(8,128)(2,1)S(1)}, bf16[2,128,512]{2,1,0:T(8,128)(2,1)S(1)}, f32[2048,512]{1,0:T(8,128)S(1)}) custom-call(s32[16]{0:T(128)S(1)} %copy-done.1, s32[8]{0:T(128)S(1)} %copy-done.2, bf16[256,1024]{1,0:T(8,128)(2,1)S(1)} %project.1.q_ref, ...), custom_call_target="tpu_custom_call" | custom-call | bytes 1 | tf_op jit(solution)/shard_map/upper_grads/pallas_call | solution.py:610
  49.5 0.5 collective-permute-start.14
  50.0 1.0 collective-permute-done.13.refs_0_
  51.0 0.4 collective-permute-done.14.refs_1_
  51.5 0.4 collective-permute-start.15
  51.9 0.5 collective-permute-start.16
  52.4 2.7 %collective-permute-start.17 = (bf16[128,512]{1,0:T(8,128)(2,1)S(1)}, bf16[128,512]{1,0:T(8,128)(2,1)S(1)}, u32[]{:S(2)}, u32[]{:S(2)}) collective-permute-start(bf16[128,512]{1,0:T(8,128)(2,1)S(1)} %get-tuple-element.231), channel_id=1, source_target_pairs={{0,6},{1,7},{2,4},{3,5},{4,2},{5,3},{6,0},{7,1},{8,14},{9,15},{10,... | collective-permute-start | bytes 393224 | tf_op jit(solution)/shard_map/ppermute | solution.py:629
  55.1 4.5 %lower_grads.1 = (bf16[128,1024]{1,0:T(8,128)(2,1)S(1)}, bf16[4,128,512]{2,1,0:T(8,128)(2,1)S(1)}, bf16[2,128,512]{2,1,0:T(8,128)(2,1)S(1)}, bf16[2,128,512]{2,1...) custom-call(s32[16]{0:T(128)S(1)} %copy-done.1, ...), custom_call_target="tpu_custom_call" | custom-call | bytes 1 | tf_op jit(solution)/shard_map/lower_grads/pallas_call | solution.py:610
  59.7 0.5 collective-permute-start.19
  60.2 1.3 %query_terms.2 = (f32[2,128,1024]{2,1,0:T(8,128)S(1)}, f32[2,128,1024]{2,1,0:T(8,128)S(1)}) custom-call(bf16[128,1024]{1,0:T(8,128)(2,1)S(1)} %get-tuple-element.246.upper_ref, bf16[128,1024]{1,0:T(8,128)(2,1)S(1)} %get-tuple-element.247.lower_ref, bf16[2,1024,1024]{2,1,0:T(8,128)(2,1)S(1)} %get-tuple-element.225.w_ref), custom_call_target="tpu_custom_call" | custom-call | bytes 1 | tf_op jit(solution)/shard_map/query_terms/pallas_call | solution.py:231
  61.5 0.8 all_terms.4
  62.6 0.2 collective-permute-start.20
  62.8 0.3 collective-permute-start.21
  63.1 3.0 %collective-permute-start.22 = (bf16[128,512]{1,0:T(8,128)(2,1)S(1)}, bf16[128,512]{1,0:T(8,128)(2,1)S(1)}, u32[]{:S(2)}, u32[]{:S(2)}) collective-permute-start(bf16[128,512]{1,0:T(8,128)(2,1)S(1)} %get-tuple-element.261), channel_id=1, source_target_pairs={{0,6},{1,7},{2,4},{3,5},{4,2},{5,3},{6,0},{7,1},{8,14},{9,15},{10,... | collective-permute-start | bytes 393224 | tf_op jit(solution)/shard_map/ppermute | solution.py:629
  66.1 3.1 %query_terms.3 = (f32[2,128,1024]{2,1,0:T(8,128)S(1)}, f32[2,128,1024]{2,1,0:T(8,128)S(1)}) custom-call(bf16[128,1024]{1,0:T(8,128)(2,1)S(1)} %get-tuple-element.246.upper_ref, bf16[128,1024]{1,0:T(8,128)(2,1)S(1)} %get-tuple-element.247.lower_ref, bf16[4096,1024]{1,0:T(8,128)(2,1)} %w_ref.1), custom_call_target="tpu_custom_call" | custom-call | bytes 1 | tf_op jit(solution)/shard_map/query_terms/pallas_call | solution.py:231
  69.2 2.4 %all_terms.5 = (bf16[128,1024]{1,0:T(8,128)(2,1)S(1)}, bf16[128,1024]{1,0:T(8,128)(2,1)S(1)}) custom-call(f32[2,128,1024]{2,1,0:T(8,128)S(1)} %get-tuple-element.250.first_ref, bf16[128,512]{1,0:T(8,128)(2,1)S(1)} %get-tuple-element.251.refs_0_, bf16[128,512]{1,0:T(8,128)(2,1)S(1)} %collective-permute-done.15.refs_1_, ...), custom_call_target="tpu_custom_call" | custom-call | bytes 1 | tf_op jit(solution)/shard_map/all_terms/pallas_call | solution.py:280
  71.6 0.8 all_terms.6
  72.4 2.1 %collective-permute-start.24 = (bf16[128,1024]{1,0:T(8,128)(2,1)S(1)}, bf16[128,1024]{1,0:T(8,128)(2,1)S(1)}, u32[]{:S(2)}, u32[]{:S(2)}) collective-permute-start(bf16[128,1024]{1,0:T(8,128)(2,1)S(1)} %get-tuple-element.269), channel_id=1, source_target_pairs={{0,8},{8,0},{16,24},{24,16},{1,9},{9,1},{17,25},{25,17},{2,10},{10... | collective-permute-start | bytes 786440 | tf_op jit(solution)/shard_map/ppermute | solution.py:629
  74.5 2.7 %collective-permute-done.23.b_ref = bf16[2,128,1024]{2,1,0:T(8,128)(2,1)S(1)} collective-permute-done((bf16[2,128,1024]{2,1,0:T(8,128)(2,1)S(1)}, bf16[2,128,1024]{2,1,0:T(8,128)(2,1)S(1)}, u32[]{:S(2)}, u32[]{:S(2)}) %collective-permute-start.23) | collective-permute-done | bytes 524320 | tf_op jit(solution)/shard_map/ppermute | solution.py:629
  77.3 0.2 collective-permute-start.25
  77.5 2.4 %all_terms.7 = (bf16[128,1024]{1,0:T(8,128)(2,1)S(1)}, bf16[128,1024]{1,0:T(8,128)(2,1)S(1)}) custom-call(f32[2,128,1024]{2,1,0:T(8,128)S(1)} %get-tuple-element.273.first_ref, bf16[128,512]{1,0:T(8,128)(2,1)S(1)} %get-tuple-element.274.refs_0_, bf16[128,512]{1,0:T(8,128)(2,1)S(1)} %collective-permute-done.20.refs_1_, ...), custom_call_target="tpu_custom_call" | custom-call | bytes 1 | tf_op jit(solution)/shard_map/all_terms/pallas_call | solution.py:280
  79.8 4.9 %collective-permute-done.24.b_ref = bf16[128,1024]{1,0:T(8,128)(2,1)S(1)} collective-permute-done((bf16[128,1024]{1,0:T(8,128)(2,1)S(1)}, bf16[128,1024]{1,0:T(8,128)(2,1)S(1)}, u32[]{:S(2)}, u32[]{:S(2)}) %collective-permute-start.24) | collective-permute-done | bytes 262176 | tf_op jit(solution)/shard_map/ppermute | solution.py:629
  84.8 0.2 collective-permute-start.26
  85.1 2.5 %collective-permute-start.27 = (bf16[128,1024]{1,0:T(8,128)(2,1)S(1)}, bf16[128,1024]{1,0:T(8,128)(2,1)S(1)}, u32[]{:S(2)}, u32[]{:S(2)}) collective-permute-start(bf16[128,1024]{1,0:T(8,128)(2,1)S(1)} %get-tuple-element.292), channel_id=1, source_target_pairs={{0,8},{8,0},{16,24},{24,16},{1,9},{9,1},{17,25},{25,17},{2,10},{10... | collective-permute-start | bytes 786440 | tf_op jit(solution)/shard_map/ppermute | solution.py:629
  87.6 10.4 %collective-permute-done.25.b_ref = bf16[128,1024]{1,0:T(8,128)(2,1)S(1)} collective-permute-done((bf16[128,1024]{1,0:T(8,128)(2,1)S(1)}, bf16[128,1024]{1,0:T(8,128)(2,1)S(1)}, u32[]{:S(2)}, u32[]{:S(2)}) %collective-permute-start.25) | collective-permute-done | bytes 262176 | tf_op jit(solution)/shard_map/ppermute | solution.py:629
  98.1 3.6 %collective-permute-done.26.b_ref = bf16[128,1024]{1,0:T(8,128)(2,1)S(1)} collective-permute-done((bf16[128,1024]{1,0:T(8,128)(2,1)S(1)}, bf16[128,1024]{1,0:T(8,128)(2,1)S(1)}, u32[]{:S(2)}, u32[]{:S(2)}) %collective-permute-start.26) | collective-permute-done | bytes 262176 | tf_op jit(solution)/shard_map/ppermute | solution.py:629
  101.8 1.4 %join_rows.1 = bf16[256,1024]{1,0:T(8,128)(2,1)} custom-call(s32[16]{0:T(128)S(1)} %copy-done.1, f32[128,1024]{1,0:T(8,128)S(1)} %merge.4.refs_0_, f32[128,1024]{1,0:T(8,128)S(1)} %merge.5.refs_1_, bf16[128,1024]{1,0:T(8,128)(2,1)S(1)} %collective-permute-done.27.refs_2_), custom_call_target="tpu_custom_call" | custom-call | bytes 1 | tf_op jit(solution)/shard_map/join_rows/pallas_call | solution.py:347
  (37 shorter events, 0.9 us)
Async XLA Ops:
  1.1 14.9 %collective-permute-start.2 = (bf16[128,1024]{1,0:T(8,128)(2,1)S(1)}, bf16[128,1024]{1,0:T(8,128)(2,1)S(1)}, u32[]{:S(2)}, u32[]{:S(2)}) collective-permute-start(bf16[128,1024]{1,0:T(8,128)(2,1)S(1)} %get-tuple-element.294), channel_id=1, source_target_pairs={{0,8},{8,0},{16,24},{24,16},{1,9},{9,1},{17,25},{25,17},{2,10},{10... | collective-permute-start | bytes 786440 | tf_op jit(solution)/shard_map/ppermute | solution.py:629
  4.2 14.3 %collective-permute-start.1 = (bf16[128,1024]{1,0:T(8,128)(2,1)S(1)}, bf16[128,1024]{1,0:T(8,128)(2,1)S(1)}, u32[]{:S(2)}, u32[]{:S(2)}) collective-permute-start(bf16[128,1024]{1,0:T(8,128)(2,1)S(1)} %get-tuple-element.294), channel_id=1, source_target_pairs={{0,16},{8,24},{16,0},{24,8},{1,17},{9,25},{17,1},{25,9},{2,18},{10... | collective-permute-start | bytes 786440 | tf_op jit(solution)/shard_map/ppermute | solution.py:629
  10.1 8.4 %collective-permute-start = (bf16[256,512]{1,0:T(8,128)(2,1)S(1)}, bf16[256,512]{1,0:T(8,128)(2,1)S(1)}, u32[]{:S(2)}, u32[]{:S(2)}) collective-permute-start(bf16[256,512]{1,0:T(8,128)(2,1)S(1)} %project_kv.1.refs_0_), channel_id=1, source_target_pairs={{0,2},{1,3},{2,0},{3,1},{4,6},{5,7},{6,4},{7,5},{8,10},{9,11},{10,... | collective-permute-start | bytes 786440 | tf_op jit(solution)/shard_map/ppermute | solution.py:629
  11.6 16.4 %collective-permute-start.4 = (bf16[256,512]{1,0:T(8,128)(2,1)S(1)}, bf16[256,512]{1,0:T(8,128)(2,1)S(1)}, u32[]{:S(2)}, u32[]{:S(2)}) collective-permute-start(bf16[256,512]{1,0:T(8,128)(2,1)S(1)} %project_kv.1.refs_0_), channel_id=1, source_target_pairs={{0,4},{1,5},{2,6},{3,7},{4,0},{5,1},{6,2},{7,3},{8,12},{9,13},{10,... | collective-permute-start | bytes 786440 | tf_op jit(solution)/shard_map/ppermute | solution.py:629
  18.5 9.5 %collective-permute-start.5 = (bf16[256,512]{1,0:T(8,128)(2,1)S(1)}, bf16[256,512]{1,0:T(8,128)(2,1)S(1)}, u32[]{:S(2)}, u32[]{:S(2)}) collective-permute-start(bf16[256,512]{1,0:T(8,128)(2,1)S(1)} %collective-permute-done.refs_1_), channel_id=1, source_target_pairs={{0,4},{1,5},{2,6},{3,7},{4,0},{5,1},{6,2},{7,3},{8,12},{9,13},{10,... | collective-permute-start | bytes 786440 | tf_op jit(solution)/shard_map/ppermute | solution.py:629
  20.0 15.7 %copy-start.1 = (s32[16]{0:T(128)S(1)}, s32[16]{0:T(128)}, u32[]{:S(2)}) copy-start(s32[16]{0:T(128)} %order.9) | copy-start | bytes 196
  20.0 15.7 %copy-start.2 = (s32[8]{0:T(128)S(1)}, s32[8]{0:T(128)}, u32[]{:S(2)}) copy-start(s32[8]{0:T(128)} %lengths.7) | copy-start | bytes 100
  20.0 9.8 %collective-permute-start.7 = (bf16[128,1024]{1,0:T(8,128)(2,1)S(1)}, bf16[128,1024]{1,0:T(8,128)(2,1)S(1)}, u32[]{:S(2)}, u32[]{:S(2)}) collective-permute-start(bf16[128,1024]{1,0:T(8,128)(2,1)S(1)} %get-tuple-element.293), channel_id=1, source_target_pairs={{0,8},{8,0},{16,24},{24,16},{1,9},{9,1},{17,25},{25,17},{2,10},{10... | collective-permute-start | bytes 786440 | tf_op jit(solution)/shard_map/ppermute | solution.py:629
  20.5 13.2 %collective-permute-start.6 = (bf16[128,1024]{1,0:T(8,128)(2,1)S(1)}, bf16[128,1024]{1,0:T(8,128)(2,1)S(1)}, u32[]{:S(2)}, u32[]{:S(2)}) collective-permute-start(bf16[128,1024]{1,0:T(8,128)(2,1)S(1)} %get-tuple-element.293), channel_id=1, source_target_pairs={{0,16},{8,24},{16,0},{24,8},{1,17},{9,25},{17,1},{25,9},{2,18},{10... | collective-permute-start | bytes 786440 | tf_op jit(solution)/shard_map/ppermute | solution.py:629
  28.0 5.6 %collective-permute-start.9 = (bf16[256,512]{1,0:T(8,128)(2,1)S(1)}, bf16[256,512]{1,0:T(8,128)(2,1)S(1)}, u32[]{:S(2)}, u32[]{:S(2)}) collective-permute-start(bf16[256,512]{1,0:T(8,128)(2,1)S(1)} %project_kv.1.refs_0_), channel_id=1, source_target_pairs={{0,1},{1,0},{2,3},{3,2},{4,5},{5,4},{6,7},{7,6},{8,9},{9,8},{10,11... | collective-permute-start | bytes 786440 | tf_op jit(solution)/shard_map/ppermute | solution.py:629
  28.1 7.6 %collective-permute-start.10 = (bf16[256,512]{1,0:T(8,128)(2,1)S(1)}, bf16[256,512]{1,0:T(8,128)(2,1)S(1)}, u32[]{:S(2)}, u32[]{:S(2)}) collective-permute-start(bf16[256,512]{1,0:T(8,128)(2,1)S(1)} %collective-permute-done.refs_1_), channel_id=1, source_target_pairs={{0,1},{1,0},{2,3},{3,2},{4,5},{5,4},{6,7},{7,6},{8,9},{9,8},{10,11... | collective-permute-start | bytes 786440 | tf_op jit(solution)/shard_map/ppermute | solution.py:629
  28.6 7.1 %collective-permute-start.11 = (bf16[256,512]{1,0:T(8,128)(2,1)S(1)}, bf16[256,512]{1,0:T(8,128)(2,1)S(1)}, u32[]{:S(2)}, u32[]{:S(2)}) collective-permute-start(bf16[256,512]{1,0:T(8,128)(2,1)S(1)} %collective-permute-done.4.refs_2_), channel_id=1, source_target_pairs={{0,1},{1,0},{2,3},{3,2},{4,5},{5,4},{6,7},{7,6},{8,9},{9,8},{10,11... | collective-permute-start | bytes 786440 | tf_op jit(solution)/shard_map/ppermute | solution.py:629
  29.8 5.9 %collective-permute-start.12 = (bf16[256,512]{1,0:T(8,128)(2,1)S(1)}, bf16[256,512]{1,0:T(8,128)(2,1)S(1)}, u32[]{:S(2)}, u32[]{:S(2)}) collective-permute-start(bf16[256,512]{1,0:T(8,128)(2,1)S(1)} %collective-permute-done.5.refs_3_), channel_id=1, source_target_pairs={{0,1},{1,0},{2,3},{3,2},{4,5},{5,4},{6,7},{7,6},{8,9},{9,8},{10,11... | collective-permute-start | bytes 786440 | tf_op jit(solution)/shard_map/ppermute | solution.py:629
  33.7 9.7 %collective-permute-start.3 = (bf16[128,1024]{1,0:T(8,128)(2,1)S(1)}, bf16[128,1024]{1,0:T(8,128)(2,1)S(1)}, u32[]{:S(2)}, u32[]{:S(2)}) collective-permute-start(bf16[128,1024]{1,0:T(8,128)(2,1)S(1)} %collective-permute-done.1.refs_3_), channel_id=1, source_target_pairs={{0,8},{8,0},{16,24},{24,16},{1,9},{9,1},{17,25},{25,17},{2,10},{10... | collective-permute-start | bytes 786440 | tf_op jit(solution)/shard_map/ppermute | solution.py:629
  33.7 11.2 %collective-permute-start.8 = (bf16[128,1024]{1,0:T(8,128)(2,1)S(1)}, bf16[128,1024]{1,0:T(8,128)(2,1)S(1)}, u32[]{:S(2)}, u32[]{:S(2)}) collective-permute-start(bf16[128,1024]{1,0:T(8,128)(2,1)S(1)} %collective-permute-done.6.refs_4_), channel_id=1, source_target_pairs={{0,8},{8,0},{16,24},{24,16},{1,9},{9,1},{17,25},{25,17},{2,10},{10... | collective-permute-start | bytes 786440 | tf_op jit(solution)/shard_map/ppermute | solution.py:629
  38.6 2.9 %copy-start = (bf16[256,1024]{1,0:T(8,128)(2,1)S(1)}, bf16[256,1024]{1,0:T(8,128)(2,1)}, u32[]{:S(2)}) copy-start(bf16[256,1024]{1,0:T(8,128)(2,1)} %refs_0_) | copy-start | bytes 1572868
  49.4 1.6 %collective-permute-start.13 = (bf16[2,128,512]{2,1,0:T(8,128)(2,1)S(1)}, bf16[2,128,512]{2,1,0:T(8,128)(2,1)S(1)}, u32[]{:S(2)}, u32[]{:S(2)}) collective-permute-start(bf16[2,128,512]{2,1,0:T(8,128)(2,1)S(1)} %get-tuple-element.204), channel_id=1, source_target_pairs={{0,1},{1,0},{2,3},{3,2},{4,5},{5,4},{6,7},{7,6},{8,9},{9,8},{10,11... | collective-permute-start | bytes 786440 | tf_op jit(solution)/shard_map/ppermute | solution.py:629
  49.5 1.9 %collective-permute-start.14 = (bf16[2,128,512]{2,1,0:T(8,128)(2,1)S(1)}, bf16[2,128,512]{2,1,0:T(8,128)(2,1)S(1)}, u32[]{:S(2)}, u32[]{:S(2)}) collective-permute-start(bf16[2,128,512]{2,1,0:T(8,128)(2,1)S(1)} %get-tuple-element.205), channel_id=1, source_target_pairs={{0,1},{1,0},{2,3},{3,2},{4,5},{5,4},{6,7},{7,6},{8,9},{9,8},{10,11... | collective-permute-start | bytes 786440 | tf_op jit(solution)/shard_map/ppermute | solution.py:629
  51.5 9.9 %collective-permute-start.15 = (bf16[128,512]{1,0:T(8,128)(2,1)S(1)}, bf16[128,512]{1,0:T(8,128)(2,1)S(1)}, u32[]{:S(2)}, u32[]{:S(2)}) collective-permute-start(bf16[128,512]{1,0:T(8,128)(2,1)S(1)} %get-tuple-element.229), channel_id=1, source_target_pairs={{0,2},{1,3},{2,0},{3,1},{4,6},{5,7},{6,4},{7,5},{8,10},{9,11},{10,... | collective-permute-start | bytes 393224 | tf_op jit(solution)/shard_map/ppermute | solution.py:629
  51.9 9.6 %collective-permute-start.16 = (bf16[128,512]{1,0:T(8,128)(2,1)S(1)}, bf16[128,512]{1,0:T(8,128)(2,1)S(1)}, u32[]{:S(2)}, u32[]{:S(2)}) collective-permute-start(bf16[128,512]{1,0:T(8,128)(2,1)S(1)} %get-tuple-element.230), channel_id=1, source_target_pairs={{0,4},{1,5},{2,6},{3,7},{4,0},{5,1},{6,2},{7,3},{8,12},{9,13},{10,... | collective-permute-start | bytes 393224 | tf_op jit(solution)/shard_map/ppermute | solution.py:629
  52.4 9.1 %collective-permute-start.17 = (bf16[128,512]{1,0:T(8,128)(2,1)S(1)}, bf16[128,512]{1,0:T(8,128)(2,1)S(1)}, u32[]{:S(2)}, u32[]{:S(2)}) collective-permute-start(bf16[128,512]{1,0:T(8,128)(2,1)S(1)} %get-tuple-element.231), channel_id=1, source_target_pairs={{0,6},{1,7},{2,4},{3,5},{4,2},{5,3},{6,0},{7,1},{8,14},{9,15},{10,... | collective-permute-start | bytes 393224 | tf_op jit(solution)/shard_map/ppermute | solution.py:629
  59.6 2.8 %collective-permute-start.18 = (bf16[2,128,512]{2,1,0:T(8,128)(2,1)S(1)}, bf16[2,128,512]{2,1,0:T(8,128)(2,1)S(1)}, u32[]{:S(2)}, u32[]{:S(2)}) collective-permute-start(bf16[2,128,512]{2,1,0:T(8,128)(2,1)S(1)} %get-tuple-element.240), channel_id=1, source_target_pairs={{0,1},{1,0},{2,3},{3,2},{4,5},{5,4},{6,7},{7,6},{8,9},{9,8},{10,11... | collective-permute-start | bytes 786440 | tf_op jit(solution)/shard_map/ppermute | solution.py:629
  59.7 2.7 %collective-permute-start.19 = (bf16[2,128,512]{2,1,0:T(8,128)(2,1)S(1)}, bf16[2,128,512]{2,1,0:T(8,128)(2,1)S(1)}, u32[]{:S(2)}, u32[]{:S(2)}) collective-permute-start(bf16[2,128,512]{2,1,0:T(8,128)(2,1)S(1)} %get-tuple-element.241), channel_id=1, source_target_pairs={{0,1},{1,0},{2,3},{3,2},{4,5},{5,4},{6,7},{7,6},{8,9},{9,8},{10,11... | collective-permute-start | bytes 786440 | tf_op jit(solution)/shard_map/ppermute | solution.py:629
  62.3 14.8 %collective-permute-start.23 = (bf16[2,128,1024]{2,1,0:T(8,128)(2,1)S(1)}, bf16[2,128,1024]{2,1,0:T(8,128)(2,1)S(1)}, u32[]{:S(2)}, u32[]{:S(2)}) collective-permute-start(bf16[2,128,1024]{2,1,0:T(8,128)(2,1)S(1)} %all_terms.4), channel_id=1, source_target_pairs={{0,8},{8,0},{16,24},{24,16},{1,9},{9,1},{17,25},{25,17},{2,10},{10... | collective-permute-start | bytes 1572872 | tf_op jit(solution)/shard_map/ppermute | solution.py:629
  62.6 9.0 %collective-permute-start.20 = (bf16[128,512]{1,0:T(8,128)(2,1)S(1)}, bf16[128,512]{1,0:T(8,128)(2,1)S(1)}, u32[]{:S(2)}, u32[]{:S(2)}) collective-permute-start(bf16[128,512]{1,0:T(8,128)(2,1)S(1)} %get-tuple-element.259), channel_id=1, source_target_pairs={{0,2},{1,3},{2,0},{3,1},{4,6},{5,7},{6,4},{7,5},{8,10},{9,11},{10,... | collective-permute-start | bytes 393224 | tf_op jit(solution)/shard_map/ppermute | solution.py:629
  62.8 8.8 %collective-permute-start.21 = (bf16[128,512]{1,0:T(8,128)(2,1)S(1)}, bf16[128,512]{1,0:T(8,128)(2,1)S(1)}, u32[]{:S(2)}, u32[]{:S(2)}) collective-permute-start(bf16[128,512]{1,0:T(8,128)(2,1)S(1)} %get-tuple-element.260), channel_id=1, source_target_pairs={{0,4},{1,5},{2,6},{3,7},{4,0},{5,1},{6,2},{7,3},{8,12},{9,13},{10,... | collective-permute-start | bytes 393224 | tf_op jit(solution)/shard_map/ppermute | solution.py:629
  63.1 8.5 %collective-permute-start.22 = (bf16[128,512]{1,0:T(8,128)(2,1)S(1)}, bf16[128,512]{1,0:T(8,128)(2,1)S(1)}, u32[]{:S(2)}, u32[]{:S(2)}) collective-permute-start(bf16[128,512]{1,0:T(8,128)(2,1)S(1)} %get-tuple-element.261), channel_id=1, source_target_pairs={{0,6},{1,7},{2,4},{3,5},{4,2},{5,3},{6,0},{7,1},{8,14},{9,15},{10,... | collective-permute-start | bytes 393224 | tf_op jit(solution)/shard_map/ppermute | solution.py:629
  72.4 12.3 %collective-permute-start.24 = (bf16[128,1024]{1,0:T(8,128)(2,1)S(1)}, bf16[128,1024]{1,0:T(8,128)(2,1)S(1)}, u32[]{:S(2)}, u32[]{:S(2)}) collective-permute-start(bf16[128,1024]{1,0:T(8,128)(2,1)S(1)} %get-tuple-element.269), channel_id=1, source_target_pairs={{0,8},{8,0},{16,24},{24,16},{1,9},{9,1},{17,25},{25,17},{2,10},{10... | collective-permute-start | bytes 786440 | tf_op jit(solution)/shard_map/ppermute | solution.py:629
  77.3 20.7 %collective-permute-start.25 = (bf16[128,1024]{1,0:T(8,128)(2,1)S(1)}, bf16[128,1024]{1,0:T(8,128)(2,1)S(1)}, u32[]{:S(2)}, u32[]{:S(2)}) collective-permute-start(bf16[128,1024]{1,0:T(8,128)(2,1)S(1)} %add.2), channel_id=1, source_target_pairs={{0,16},{8,24},{16,0},{24,8},{1,17},{9,25},{17,1},{25,9},{2,18},{10... | collective-permute-start | bytes 786440 | tf_op jit(solution)/shard_map/ppermute | solution.py:629
  84.8 16.9 %collective-permute-start.26 = (bf16[128,1024]{1,0:T(8,128)(2,1)S(1)}, bf16[128,1024]{1,0:T(8,128)(2,1)S(1)}, u32[]{:S(2)}, u32[]{:S(2)}) collective-permute-start(bf16[128,1024]{1,0:T(8,128)(2,1)S(1)} %add.3), channel_id=1, source_target_pairs={{0,16},{8,24},{16,0},{24,8},{1,17},{9,25},{17,1},{25,9},{2,18},{10... | collective-permute-start | bytes 786440 | tf_op jit(solution)/shard_map/ppermute | solution.py:629
  85.1 16.7 %collective-permute-start.27 = (bf16[128,1024]{1,0:T(8,128)(2,1)S(1)}, bf16[128,1024]{1,0:T(8,128)(2,1)S(1)}, u32[]{:S(2)}, u32[]{:S(2)}) collective-permute-start(bf16[128,1024]{1,0:T(8,128)(2,1)S(1)} %get-tuple-element.292), channel_id=1, source_target_pairs={{0,8},{8,0},{16,24},{24,16},{1,9},{9,1},{17,25},{25,17},{2,10},{10... | collective-permute-start | bytes 786440 | tf_op jit(solution)/shard_map/ppermute | solution.py:629

commit v5 on v4

--- a/solution.py
+++ b/solution.py
@@ -504,12 +504,12 @@
     spans = 2 * peers
     count = 3 if upper else AT_ONCE
     if upper:
-        held, dq_ref, even_ref, *odd_refs, sums, places = refs
+        held, wq_ref, wk_ref, wv_ref, dq_ref, even_ref, *odd_refs, sums, wq, wk, wv, places, sems = refs
     else:
         rest_ref, held, wq_ref, wk_ref, wv_ref, dq_ref, even_ref, *odd_refs, wq, wk, wv, sums, places, sems = refs
-        copies = []
-        for i, (w_ref, w) in enumerate(((wq_ref, wq), (wk_ref, wk), (wv_ref, wv))):
-            copies += fetch_rows(spare, w_ref, w, sems, i)
+    copies = []
+    for i, (w_ref, w) in enumerate(((wq_ref, wq), (wk_ref, wk), (wv_ref, wv))):
+        copies += fetch_rows(spare, w_ref, w, sems, i)
     me = lax.axis_index("ctx")
     width = groups * dim
     scale = 1.0 / math.sqrt(dim)
@@ -586,19 +586,16 @@
         part = pl.ds(pl.multiple_of(pick * half, half), half)
         out[slot, :, :width] = (sums[part, :width] * scale).astype(out.dtype)
         out[slot, :, width:] = sums[part, width:].astype(out.dtype)
-    if not upper:
-        for copy in copies:
-            copy.wait()
+    for copy in copies:
+        copy.wait()
 
 
 def grads(upper, q, g, level, mixed, *args):
     *blocks, span_order, doc_lengths, sizes = args
-    weights, spare, scratch = [], [], []
-    if not upper:
-        heads = lax.axis_size("head")
-        spare = list(range(heads - 1, 0, -2))
-        weights, blocks = [in_hbm(w) for w in blocks[-3:]], blocks[:-3]
-        scratch = [pltpu.SemaphoreType.DMA((len(spare), 3))]
+    heads = lax.axis_size("head")
+    spare = list(range(heads - (2 if upper else 1), -1, -2))
+    weights, blocks = [in_hbm(w) for w in blocks[-3:]], blocks[:-3]
+    scratch = [pltpu.SemaphoreType.DMA((len(spare), 3))]
     peers, half, groups, share, dim, docs = sizes
     tokens, width = 2 * half, groups * dim
     columns = share * half
@@ -744,14 +741,16 @@
         blocks[:-1], (w_first, w_second), [(0, mid), (0, mid - 1)], None, jnp.float32
     )
     context_grad = context(blocks[-1:], (w_second,), [(mid - 1, mid)], total, jnp.bfloat16)
-    upper_dq, even, *odd, rest = attend(True, grads, query, context_grad, *upper_stats, held)
+    weights = (w_query, w_key, value_projection)
+    upper_dq, even, *odd, rest, stay_q, stay_k, stay_v = attend(
+        True, grads, query, context_grad, *upper_stats, held, *weights
+    )
     upper = scatter_ctx(turn(pair_sums, even, *[swap(x, 1, "ctx") for x in odd]))
-    weights = (w_query, w_key, value_projection)
     lower_dq, even, *odd, wq, wk, wv = attend(
         False, grads, query, context_grad, *lower_stats, rest, held, *weights
     )
     sides = [list(range(heads - 1, 0, -2)), list(range(heads - 2, -1, -2))]
-    weights = [(wq, wk, wv), weights]
+    weights = [(wq, wk, wv), (stay_q, stay_k, stay_v)]
 
     def firsts_of(side):
         return turn(

time: 103 us -> 103 us (level)
  waiting for transfers between devices: 34.8 us -> 39.8 us
  Pallas kernels: 37.5 us -> 32.8 us
    ppermute x28, waiting for transfers between devices: 34.8 us -> 39.8 us  [swap(): lax.ppermute(x, axis, [(i, i ^ k) for i in range(lax.axis_size(axis))])]
    pallas_call x4, Pallas kernels: 6.35 us -> 3.26 us  [all_terms(): pl.pallas_call(functools.partial(all_terms_body, places, len(terms)), in_...]
    pallas_call x2, Pallas kernels: 4.38 us -> 2.56 us  [query_terms(): pl.pallas_call(functools.partial(query_terms_body, places), in_specs=[pl....]
  transfers between devices with their start and end apart: 28 -> 28, of which waited for: 11 -> 13; matrix products, arithmetic and copies ran while one was open for 0% -> 0% of each run, Pallas kernels for 30% -> 25%
where the time goes in v5:
time: 103 us
  waiting for transfers between devices  39.8 us (39%)
  Pallas kernels  32.8 us (32%)
  starting transfers between devices  29.3 us (28%)
  local copies, waits for them, and re-layouts  1.08 us (1%)
    ppermute x28, waiting for transfers between devices, swap(): lax.ppermute(x, axis, [(i, i ^ k) for i in range(lax.axis_size(axis))])  39.8 us
    ppermute x28, starting transfers between devices, swap(): lax.ppermute(x, axis, [(i, i ^ k) for i in range(lax.axis_size(axis))])  29.3 us
    pallas_call x2, Pallas kernels, grads(): pl.pallas_call(functools.partial(grads_body, sizes, upper, spare), in_spe...  8.55 us
    pallas_call x2, Pallas kernels, stats(): pl.pallas_call(functools.partial(stats_body, sizes, upper, spare), in_spe...  5.79 us
    pallas_call x1, Pallas kernels, project(): pl.pallas_call(functools.partial(project_body, parts), in_specs=[pl.Block...  4.87 us
    pallas_call x1, Pallas kernels, project_kv(): pl.pallas_call(functools.partial(kv_body, parts), in_specs=[pl.BlockSpec(...  3.32 us
    pallas_call x4, Pallas kernels, all_terms(): pl.pallas_call(functools.partial(all_terms_body, places, len(terms)), in_...  3.26 us
    pallas_call x2, Pallas kernels, query_terms(): pl.pallas_call(functools.partial(query_terms_body, places), in_specs=[pl....  2.56 us
  transfers between devices with their start and end apart: 28, of which 13 were waited for; matrix products, arithmetic and copies ran while one was open for 0% of the time, Pallas kernels for 25%

profile of v5, /device:TPU:0, one launch (start us, length us, event | category | flops | bytes accessed | tf_op | source)
XLA Modules:
  0.0 103.3 jit_solution(12887947974597886220)
XLA Ops:
  0.0 1.1 %fusion = (bf16[128,1024]{1,0:T(8,128)(2,1)S(1)}, bf16[128,1024]{1,0:T(8,128)(2,1)S(1)}) fusion(bf16[256,1024]{1,0:T(8,128)(2,1)} %refs_0_), kind=kLoop, calls=%fused_computation | loop fusion | bytes 1048576 | tf_op jit(solution)/shard_map/slice | solution.py:720
  1.1 3.1 %collective-permute-start.2 = (bf16[128,1024]{1,0:T(8,128)(2,1)S(1)}, bf16[128,1024]{1,0:T(8,128)(2,1)S(1)}, u32[]{:S(2)}, u32[]{:S(2)}) collective-permute-start(bf16[128,1024]{1,0:T(8,128)(2,1)S(1)} %get-tuple-element.306), channel_id=1, source_target_pairs={{0,8},{8,0},{16,24},{24,16},{1,9},{9,1},{17,25},{25,17},{2,10},{10... | collective-permute-start | bytes 786440 | tf_op jit(solution)/shard_map/ppermute | solution.py:626
  4.2 2.6 %collective-permute-start.1 = (bf16[128,1024]{1,0:T(8,128)(2,1)S(1)}, bf16[128,1024]{1,0:T(8,128)(2,1)S(1)}, u32[]{:S(2)}, u32[]{:S(2)}) collective-permute-start(bf16[128,1024]{1,0:T(8,128)(2,1)S(1)} %get-tuple-element.306), channel_id=1, source_target_pairs={{0,16},{8,24},{16,0},{24,8},{1,17},{9,25},{17,1},{25,9},{2,18},{10... | collective-permute-start | bytes 786440 | tf_op jit(solution)/shard_map/ppermute | solution.py:626
  6.7 3.3 %project_kv.1.refs_0_ = bf16[256,512]{1,0:T(8,128)(2,1)S(1)} custom-call(bf16[256,4096]{1,0:T(8,128)(2,1)} %x_ref.1, bf16[4096,256]{1,0:T(8,128)(2,1)} %refs_3_.1, bf16[4096,256]{1,0:T(8,128)(2,1)} %refs_4_), custom_call_target="tpu_custom_call" | custom-call | bytes 1 | tf_op jit(solution)/shard_map/project_kv/pallas_call | solution.py:89
  10.1 1.6 %collective-permute-start = (bf16[256,512]{1,0:T(8,128)(2,1)S(1)}, bf16[256,512]{1,0:T(8,128)(2,1)S(1)}, u32[]{:S(2)}, u32[]{:S(2)}) collective-permute-start(bf16[256,512]{1,0:T(8,128)(2,1)S(1)} %project_kv.1.refs_0_), channel_id=1, source_target_pairs={{0,2},{1,3},{2,0},{3,1},{4,6},{5,7},{6,4},{7,5},{8,10},{9,11},{10,... | collective-permute-start | bytes 786440 | tf_op jit(solution)/shard_map/ppermute | solution.py:626
  11.6 1.5 %collective-permute-start.4 = (bf16[256,512]{1,0:T(8,128)(2,1)S(1)}, bf16[256,512]{1,0:T(8,128)(2,1)S(1)}, u32[]{:S(2)}, u32[]{:S(2)}) collective-permute-start(bf16[256,512]{1,0:T(8,128)(2,1)S(1)} %project_kv.1.refs_0_), channel_id=1, source_target_pairs={{0,4},{1,5},{2,6},{3,7},{4,0},{5,1},{6,2},{7,3},{8,12},{9,13},{10,... | collective-permute-start | bytes 786440 | tf_op jit(solution)/shard_map/ppermute | solution.py:626
  13.2 2.8 %collective-permute-done.2.refs_1_ = bf16[128,1024]{1,0:T(8,128)(2,1)S(1)} collective-permute-done((bf16[128,1024]{1,0:T(8,128)(2,1)S(1)}, bf16[128,1024]{1,0:T(8,128)(2,1)S(1)}, u32[]{:S(2)}, u32[]{:S(2)}) %collective-permute-start.2) | collective-permute-done | bytes 262176 | tf_op jit(solution)/shard_map/ppermute | solution.py:626
  16.0 2.5 %collective-permute-done.1.refs_3_ = bf16[128,1024]{1,0:T(8,128)(2,1)S(1)} collective-permute-done((bf16[128,1024]{1,0:T(8,128)(2,1)S(1)}, bf16[128,1024]{1,0:T(8,128)(2,1)S(1)}, u32[]{:S(2)}, u32[]{:S(2)}) %collective-permute-start.1) | collective-permute-done | bytes 262176 | tf_op jit(solution)/shard_map/ppermute | solution.py:626
  18.5 1.5 %collective-permute-start.5 = (bf16[256,512]{1,0:T(8,128)(2,1)S(1)}, bf16[256,512]{1,0:T(8,128)(2,1)S(1)}, u32[]{:S(2)}, u32[]{:S(2)}) collective-permute-start(bf16[256,512]{1,0:T(8,128)(2,1)S(1)} %collective-permute-done.refs_1_), channel_id=1, source_target_pairs={{0,4},{1,5},{2,6},{3,7},{4,0},{5,1},{6,2},{7,3},{8,12},{9,13},{10,... | collective-permute-start | bytes 786440 | tf_op jit(solution)/shard_map/ppermute | solution.py:626
  20.0 0.4 collective-permute-start.7
  20.5 2.6 %collective-permute-start.6 = (bf16[128,1024]{1,0:T(8,128)(2,1)S(1)}, bf16[128,1024]{1,0:T(8,128)(2,1)S(1)}, u32[]{:S(2)}, u32[]{:S(2)}) collective-permute-start(bf16[128,1024]{1,0:T(8,128)(2,1)S(1)} %get-tuple-element.305), channel_id=1, source_target_pairs={{0,16},{8,24},{16,0},{24,8},{1,17},{9,25},{17,1},{25,9},{2,18},{10... | collective-permute-start | bytes 786440 | tf_op jit(solution)/shard_map/ppermute | solution.py:626
  23.1 4.9 %project.1.q_ref = bf16[256,1024]{1,0:T(8,128)(2,1)S(1)} custom-call(bf16[256,4096]{1,0:T(8,128)(2,1)} %x_ref.1, bf16[4096,1024]{1,0:T(8,128)(2,1)} %refs_2_.1), custom_call_target="tpu_custom_call" | custom-call | bytes 1 | tf_op jit(solution)/shard_map/project/pallas_call | solution.py:135
  28.1 0.5 collective-permute-start.10
  28.7 1.2 %collective-permute-done.7.refs_2_ = bf16[128,1024]{1,0:T(8,128)(2,1)S(1)} collective-permute-done((bf16[128,1024]{1,0:T(8,128)(2,1)S(1)}, bf16[128,1024]{1,0:T(8,128)(2,1)S(1)}, u32[]{:S(2)}, u32[]{:S(2)}) %collective-permute-start.7) | collective-permute-done | bytes 262176 | tf_op jit(solution)/shard_map/ppermute | solution.py:626
  29.8 3.8 %collective-permute-done.6.refs_4_ = bf16[128,1024]{1,0:T(8,128)(2,1)S(1)} collective-permute-done((bf16[128,1024]{1,0:T(8,128)(2,1)S(1)}, bf16[128,1024]{1,0:T(8,128)(2,1)S(1)}, u32[]{:S(2)}, u32[]{:S(2)}) %collective-permute-start.6) | collective-permute-done | bytes 262176 | tf_op jit(solution)/shard_map/ppermute | solution.py:626
  33.7 2.0 %collective-permute-start.8 = (bf16[128,1024]{1,0:T(8,128)(2,1)S(1)}, bf16[128,1024]{1,0:T(8,128)(2,1)S(1)}, u32[]{:S(2)}, u32[]{:S(2)}) collective-permute-start(bf16[128,1024]{1,0:T(8,128)(2,1)S(1)} %collective-permute-done.6.refs_4_), channel_id=1, source_target_pairs={{0,8},{8,0},{16,24},{24,16},{1,9},{9,1},{17,25},{25,17},{2,10},{10... | collective-permute-start | bytes 786440 | tf_op jit(solution)/shard_map/ppermute | solution.py:626
  35.7 3.0 %upper_stats.1 = (f32[2,2,512]{2,1,0:T(2,128)S(1)}, f32[2,128,512]{2,1,0:T(8,128)S(1)}, bf16[2,1024,1024]{2,1,0:T(8,128)(2,1)S(1)}, bf16[2048,512]{1,0:T(8,128)(2,1)S(1)}) custom-call(s32[16]{0:T(128)S(1)} %copy-done.1, s32[8]{0:T(128)S(1)} %copy-done.2, bf16[256,1024]{1,0:T(8,128)(2,1)S(1)} %project.1.q_ref, bf16[256,512]{1,0:T(8,128)(2,1)S(1)} %project_kv.1.refs_0_, ...), custom_call_target="tpu_custom_call" | custom-call | bytes 1 | tf_op jit(solution)/shard_map/upper_stats/pallas_call | solution.py:479
  38.7 2.8 %lower_stats.1 = (f32[2,2,512]{2,1,0:T(2,128)S(1)}, f32[2,128,512]{2,1,0:T(8,128)S(1)}, bf16[2,1024,1024]{2,1,0:T(8,128)(2,1)S(1)}) custom-call(s32[16]{0:T(128)S(1)} %copy-done.1, s32[8]{0:T(128)S(1)} %copy-done.2, bf16[256,1024]{1,0:T(8,128)(2,1)S(1)} %project.1.q_ref, bf16[2048,512]{1,0:T(8,128)(2,1)S(1)} %get-tuple-element.226.refs_0_.refs_1_, ...), custom_call_target="tpu_custom_call" | custom-call | bytes 1 | tf_op jit(solution)/shard_map/lower_stats/pallas_call | solution.py:479
  41.5 1.8 %context_grad.2.refs_0_ = f32[256,1024]{1,0:T(8,128)S(1)} custom-call(bf16[256,1024]{1,0:T(8,128)(2,1)S(1)} %copy-done, bf16[128,1024]{1,0:T(8,128)(2,1)S(1)} %collective-permute-done.2.refs_1_, bf16[128,1024]{1,0:T(8,128)(2,1)S(1)} %collective-permute-done.7.refs_2_, bf16[128,1024]{1,0:T(8,128)(2,1)S(1)} %collective-permute-done.1.refs_3_, ...), custom_call_target="tpu_custom_call" | custom-call | bytes 1 | tf_op jit(solution)/shard_map/context_grad/pallas_call | solution.py:171
  43.4 1.4 %collective-permute-done.8.refs_2_ = bf16[128,1024]{1,0:T(8,128)(2,1)S(1)} collective-permute-done((bf16[128,1024]{1,0:T(8,128)(2,1)S(1)}, bf16[128,1024]{1,0:T(8,128)(2,1)S(1)}, u32[]{:S(2)}, u32[]{:S(2)}) %collective-permute-start.8) | collective-permute-done | bytes 262176 | tf_op jit(solution)/shard_map/ppermute | solution.py:626
  44.8 0.7 context_grad.3.g_ref
  45.6 5.2 %upper_grads.1 = (bf16[128,1024]{1,0:T(8,128)(2,1)S(1)}, bf16[4,128,512]{2,1,0:T(8,128)(2,1)S(1)}, bf16[2,128,512]{2,1,0:T(8,128)(2,1)S(1)}, bf16[2,128,512]{2,1...) custom-call(s32[16]{0:T(128)S(1)} %copy-done.1, ...), custom_call_target="tpu_custom_call" | custom-call | bytes 1 | tf_op jit(solution)/shard_map/upper_grads/pallas_call | solution.py:607
  50.8 0.5 collective-permute-start.14
  51.3 1.0 collective-permute-done.13.refs_0_
  52.3 0.4 collective-permute-done.14.refs_1_
  52.9 2.0 %collective-permute-start.16 = (bf16[128,512]{1,0:T(8,128)(2,1)S(1)}, bf16[128,512]{1,0:T(8,128)(2,1)S(1)}, u32[]{:S(2)}, u32[]{:S(2)}) collective-permute-start(bf16[128,512]{1,0:T(8,128)(2,1)S(1)} %get-tuple-element.239), channel_id=1, source_target_pairs={{0,4},{1,5},{2,6},{3,7},{4,0},{5,1},{6,2},{7,3},{8,12},{9,13},{10,... | collective-permute-start | bytes 393224 | tf_op jit(solution)/shard_map/ppermute | solution.py:626
  54.9 1.5 %collective-permute-start.17 = (bf16[128,512]{1,0:T(8,128)(2,1)S(1)}, bf16[128,512]{1,0:T(8,128)(2,1)S(1)}, u32[]{:S(2)}, u32[]{:S(2)}) collective-permute-start(bf16[128,512]{1,0:T(8,128)(2,1)S(1)} %get-tuple-element.240), channel_id=1, source_target_pairs={{0,6},{1,7},{2,4},{3,5},{4,2},{5,3},{6,0},{7,1},{8,14},{9,15},{10,... | collective-permute-start | bytes 393224 | tf_op jit(solution)/shard_map/ppermute | solution.py:626
  56.4 3.4 %lower_grads.1 = (bf16[128,1024]{1,0:T(8,128)(2,1)S(1)}, bf16[4,128,512]{2,1,0:T(8,128)(2,1)S(1)}, bf16[2,128,512]{2,1,0:T(8,128)(2,1)S(1)}, bf16[2,128,512]{2,1...) custom-call(s32[16]{0:T(128)S(1)} %copy-done.1, ...), custom_call_target="tpu_custom_call" | custom-call | bytes 1 | tf_op jit(solution)/shard_map/lower_grads/pallas_call | solution.py:607
  59.9 0.5 collective-permute-start.19
  60.4 1.3 %query_terms.2 = (f32[2,128,1024]{2,1,0:T(8,128)S(1)}, f32[2,128,1024]{2,1,0:T(8,128)S(1)}) custom-call(bf16[128,1024]{1,0:T(8,128)(2,1)S(1)} %get-tuple-element.256.upper_ref, bf16[128,1024]{1,0:T(8,128)(2,1)S(1)} %get-tuple-element.257.lower_ref, bf16[2,1024,1024]{2,1,0:T(8,128)(2,1)S(1)} %get-tuple-element.234.w_ref), custom_call_target="tpu_custom_call" | custom-call | bytes 1 | tf_op jit(solution)/shard_map/query_terms/pallas_call | solution.py:231
  61.7 0.8 all_terms.4
  62.7 1.4 %collective-permute-start.20 = (bf16[128,512]{1,0:T(8,128)(2,1)S(1)}, bf16[128,512]{1,0:T(8,128)(2,1)S(1)}, u32[]{:S(2)}, u32[]{:S(2)}) collective-permute-start(bf16[128,512]{1,0:T(8,128)(2,1)S(1)} %get-tuple-element.271), channel_id=1, source_target_pairs={{0,2},{1,3},{2,0},{3,1},{4,6},{5,7},{6,4},{7,5},{8,10},{9,11},{10,... | collective-permute-start | bytes 393224 | tf_op jit(solution)/shard_map/ppermute | solution.py:626
  64.1 0.7 collective-permute-start.21
  64.8 1.5 %collective-permute-start.22 = (bf16[128,512]{1,0:T(8,128)(2,1)S(1)}, bf16[128,512]{1,0:T(8,128)(2,1)S(1)}, u32[]{:S(2)}, u32[]{:S(2)}) collective-permute-start(bf16[128,512]{1,0:T(8,128)(2,1)S(1)} %get-tuple-element.273), channel_id=1, source_target_pairs={{0,6},{1,7},{2,4},{3,5},{4,2},{5,3},{6,0},{7,1},{8,14},{9,15},{10,... | collective-permute-start | bytes 393224 | tf_op jit(solution)/shard_map/ppermute | solution.py:626
  66.3 1.3 %query_terms.3 = (f32[2,128,1024]{2,1,0:T(8,128)S(1)}, f32[2,128,1024]{2,1,0:T(8,128)S(1)}) custom-call(bf16[128,1024]{1,0:T(8,128)(2,1)S(1)} %get-tuple-element.256.upper_ref, bf16[128,1024]{1,0:T(8,128)(2,1)S(1)} %get-tuple-element.257.lower_ref, bf16[2,1024,1024]{2,1,0:T(8,128)(2,1)S(1)} %get-tuple-element.258.w_ref), custom_call_target="tpu_custom_call" | custom-call | bytes 1 | tf_op jit(solution)/shard_map/query_terms/pallas_call | solution.py:231
  67.6 0.8 all_terms.5
  68.4 0.8 collective-permute-done.20.refs_1_
  69.2 2.7 %collective-permute-done.21.refs_2_ = bf16[128,512]{1,0:T(8,128)(2,1)S(1)} collective-permute-done((bf16[128,512]{1,0:T(8,128)(2,1)S(1)}, bf16[128,512]{1,0:T(8,128)(2,1)S(1)}, u32[]{:S(2)}, u32[]{:S(2)}) %collective-permute-start.21) | collective-permute-done | bytes 131104 | tf_op jit(solution)/shard_map/ppermute | solution.py:626
  71.9 0.8 all_terms.6
  72.7 1.9 %collective-permute-start.24 = (bf16[128,1024]{1,0:T(8,128)(2,1)S(1)}, bf16[128,1024]{1,0:T(8,128)(2,1)S(1)}, u32[]{:S(2)}, u32[]{:S(2)}) collective-permute-start(bf16[128,1024]{1,0:T(8,128)(2,1)S(1)} %get-tuple-element.281), channel_id=1, source_target_pairs={{0,8},{8,0},{16,24},{24,16},{1,9},{9,1},{17,25},{25,17},{2,10},{10... | collective-permute-start | bytes 786440 | tf_op jit(solution)/shard_map/ppermute | solution.py:626
  74.7 2.7 %collective-permute-done.23.b_ref = bf16[2,128,1024]{2,1,0:T(8,128)(2,1)S(1)} collective-permute-done((bf16[2,128,1024]{2,1,0:T(8,128)(2,1)S(1)}, bf16[2,128,1024]{2,1,0:T(8,128)(2,1)S(1)}, u32[]{:S(2)}, u32[]{:S(2)}) %collective-permute-start.23) | collective-permute-done | bytes 524320 | tf_op jit(solution)/shard_map/ppermute | solution.py:626
  77.5 0.8 all_terms.7
  78.3 6.6 %collective-permute-done.24.b_ref = bf16[128,1024]{1,0:T(8,128)(2,1)S(1)} collective-permute-done((bf16[128,1024]{1,0:T(8,128)(2,1)S(1)}, bf16[128,1024]{1,0:T(8,128)(2,1)S(1)}, u32[]{:S(2)}, u32[]{:S(2)}) %collective-permute-start.24) | collective-permute-done | bytes 262176 | tf_op jit(solution)/shard_map/ppermute | solution.py:626
  85.0 0.4 collective-permute-start.26
  85.4 2.5 %collective-permute-start.27 = (bf16[128,1024]{1,0:T(8,128)(2,1)S(1)}, bf16[128,1024]{1,0:T(8,128)(2,1)S(1)}, u32[]{:S(2)}, u32[]{:S(2)}) collective-permute-start(bf16[128,1024]{1,0:T(8,128)(2,1)S(1)} %get-tuple-element.304), channel_id=1, source_target_pairs={{0,8},{8,0},{16,24},{24,16},{1,9},{9,1},{17,25},{25,17},{2,10},{10... | collective-permute-start | bytes 786440 | tf_op jit(solution)/shard_map/ppermute | solution.py:626
  88.0 10.0 %collective-permute-done.25.b_ref = bf16[128,1024]{1,0:T(8,128)(2,1)S(1)} collective-permute-done((bf16[128,1024]{1,0:T(8,128)(2,1)S(1)}, bf16[128,1024]{1,0:T(8,128)(2,1)S(1)}, u32[]{:S(2)}, u32[]{:S(2)}) %collective-permute-start.25) | collective-permute-done | bytes 262176 | tf_op jit(solution)/shard_map/ppermute | solution.py:626
  98.0 3.8 %collective-permute-done.26.b_ref = bf16[128,1024]{1,0:T(8,128)(2,1)S(1)} collective-permute-done((bf16[128,1024]{1,0:T(8,128)(2,1)S(1)}, bf16[128,1024]{1,0:T(8,128)(2,1)S(1)}, u32[]{:S(2)}, u32[]{:S(2)}) %collective-permute-start.26) | collective-permute-done | bytes 262176 | tf_op jit(solution)/shard_map/ppermute | solution.py:626
  101.9 1.4 %join_rows.1 = bf16[256,1024]{1,0:T(8,128)(2,1)} custom-call(s32[16]{0:T(128)S(1)} %copy-done.1, f32[128,1024]{1,0:T(8,128)S(1)} %merge.4.refs_0_, f32[128,1024]{1,0:T(8,128)S(1)} %merge.5.refs_1_, bf16[128,1024]{1,0:T(8,128)(2,1)S(1)} %collective-permute-done.27.refs_2_), custom_call_target="tpu_custom_call" | custom-call | bytes 1 | tf_op jit(solution)/shard_map/join_rows/pallas_call | solution.py:347
  (37 shorter events, 1.1 us)
Async XLA Ops:
  1.1 14.9 %collective-permute-start.2 = (bf16[128,1024]{1,0:T(8,128)(2,1)S(1)}, bf16[128,1024]{1,0:T(8,128)(2,1)S(1)}, u32[]{:S(2)}, u32[]{:S(2)}) collective-permute-start(bf16[128,1024]{1,0:T(8,128)(2,1)S(1)} %get-tuple-element.306), channel_id=1, source_target_pairs={{0,8},{8,0},{16,24},{24,16},{1,9},{9,1},{17,25},{25,17},{2,10},{10... | collective-permute-start | bytes 786440 | tf_op jit(solution)/shard_map/ppermute | solution.py:626
  4.2 14.3 %collective-permute-start.1 = (bf16[128,1024]{1,0:T(8,128)(2,1)S(1)}, bf16[128,1024]{1,0:T(8,128)(2,1)S(1)}, u32[]{:S(2)}, u32[]{:S(2)}) collective-permute-start(bf16[128,1024]{1,0:T(8,128)(2,1)S(1)} %get-tuple-element.306), channel_id=1, source_target_pairs={{0,16},{8,24},{16,0},{24,8},{1,17},{9,25},{17,1},{25,9},{2,18},{10... | collective-permute-start | bytes 786440 | tf_op jit(solution)/shard_map/ppermute | solution.py:626
  10.1 8.4 %collective-permute-start = (bf16[256,512]{1,0:T(8,128)(2,1)S(1)}, bf16[256,512]{1,0:T(8,128)(2,1)S(1)}, u32[]{:S(2)}, u32[]{:S(2)}) collective-permute-start(bf16[256,512]{1,0:T(8,128)(2,1)S(1)} %project_kv.1.refs_0_), channel_id=1, source_target_pairs={{0,2},{1,3},{2,0},{3,1},{4,6},{5,7},{6,4},{7,5},{8,10},{9,11},{10,... | collective-permute-start | bytes 786440 | tf_op jit(solution)/shard_map/ppermute | solution.py:626
  11.6 16.4 %collective-permute-start.4 = (bf16[256,512]{1,0:T(8,128)(2,1)S(1)}, bf16[256,512]{1,0:T(8,128)(2,1)S(1)}, u32[]{:S(2)}, u32[]{:S(2)}) collective-permute-start(bf16[256,512]{1,0:T(8,128)(2,1)S(1)} %project_kv.1.refs_0_), channel_id=1, source_target_pairs={{0,4},{1,5},{2,6},{3,7},{4,0},{5,1},{6,2},{7,3},{8,12},{9,13},{10,... | collective-permute-start | bytes 786440 | tf_op jit(solution)/shard_map/ppermute | solution.py:626
  18.5 9.5 %collective-permute-start.5 = (bf16[256,512]{1,0:T(8,128)(2,1)S(1)}, bf16[256,512]{1,0:T(8,128)(2,1)S(1)}, u32[]{:S(2)}, u32[]{:S(2)}) collective-permute-start(bf16[256,512]{1,0:T(8,128)(2,1)S(1)} %collective-permute-done.refs_1_), channel_id=1, source_target_pairs={{0,4},{1,5},{2,6},{3,7},{4,0},{5,1},{6,2},{7,3},{8,12},{9,13},{10,... | collective-permute-start | bytes 786440 | tf_op jit(solution)/shard_map/ppermute | solution.py:626
  20.0 15.7 %copy-start.1 = (s32[16]{0:T(128)S(1)}, s32[16]{0:T(128)}, u32[]{:S(2)}) copy-start(s32[16]{0:T(128)} %order.9) | copy-start | bytes 196
  20.0 15.7 %copy-start.2 = (s32[8]{0:T(128)S(1)}, s32[8]{0:T(128)}, u32[]{:S(2)}) copy-start(s32[8]{0:T(128)} %lengths.7) | copy-start | bytes 100
  20.0 9.8 %collective-permute-start.7 = (bf16[128,1024]{1,0:T(8,128)(2,1)S(1)}, bf16[128,1024]{1,0:T(8,128)(2,1)S(1)}, u32[]{:S(2)}, u32[]{:S(2)}) collective-permute-start(bf16[128,1024]{1,0:T(8,128)(2,1)S(1)} %get-tuple-element.305), channel_id=1, source_target_pairs={{0,8},{8,0},{16,24},{24,16},{1,9},{9,1},{17,25},{25,17},{2,10},{10... | collective-permute-start | bytes 786440 | tf_op jit(solution)/shard_map/ppermute | solution.py:626
  20.5 13.2 %collective-permute-start.6 = (bf16[128,1024]{1,0:T(8,128)(2,1)S(1)}, bf16[128,1024]{1,0:T(8,128)(2,1)S(1)}, u32[]{:S(2)}, u32[]{:S(2)}) collective-permute-start(bf16[128,1024]{1,0:T(8,128)(2,1)S(1)} %get-tuple-element.305), channel_id=1, source_target_pairs={{0,16},{8,24},{16,0},{24,8},{1,17},{9,25},{17,1},{25,9},{2,18},{10... | collective-permute-start | bytes 786440 | tf_op jit(solution)/shard_map/ppermute | solution.py:626
  28.0 5.6 %collective-permute-start.9 = (bf16[256,512]{1,0:T(8,128)(2,1)S(1)}, bf16[256,512]{1,0:T(8,128)(2,1)S(1)}, u32[]{:S(2)}, u32[]{:S(2)}) collective-permute-start(bf16[256,512]{1,0:T(8,128)(2,1)S(1)} %project_kv.1.refs_0_), channel_id=1, source_target_pairs={{0,1},{1,0},{2,3},{3,2},{4,5},{5,4},{6,7},{7,6},{8,9},{9,8},{10,11... | collective-permute-start | bytes 786440 | tf_op jit(solution)/shard_map/ppermute | solution.py:626
  28.1 7.6 %collective-permute-start.10 = (bf16[256,512]{1,0:T(8,128)(2,1)S(1)}, bf16[256,512]{1,0:T(8,128)(2,1)S(1)}, u32[]{:S(2)}, u32[]{:S(2)}) collective-permute-start(bf16[256,512]{1,0:T(8,128)(2,1)S(1)} %collective-permute-done.refs_1_), channel_id=1, source_target_pairs={{0,1},{1,0},{2,3},{3,2},{4,5},{5,4},{6,7},{7,6},{8,9},{9,8},{10,11... | collective-permute-start | bytes 786440 | tf_op jit(solution)/shard_map/ppermute | solution.py:626
  28.6 7.1 %collective-permute-start.11 = (bf16[256,512]{1,0:T(8,128)(2,1)S(1)}, bf16[256,512]{1,0:T(8,128)(2,1)S(1)}, u32[]{:S(2)}, u32[]{:S(2)}) collective-permute-start(bf16[256,512]{1,0:T(8,128)(2,1)S(1)} %collective-permute-done.4.refs_2_), channel_id=1, source_target_pairs={{0,1},{1,0},{2,3},{3,2},{4,5},{5,4},{6,7},{7,6},{8,9},{9,8},{10,11... | collective-permute-start | bytes 786440 | tf_op jit(solution)/shard_map/ppermute | solution.py:626
  29.8 5.9 %collective-permute-start.12 = (bf16[256,512]{1,0:T(8,128)(2,1)S(1)}, bf16[256,512]{1,0:T(8,128)(2,1)S(1)}, u32[]{:S(2)}, u32[]{:S(2)}) collective-permute-start(bf16[256,512]{1,0:T(8,128)(2,1)S(1)} %collective-permute-done.5.refs_3_), channel_id=1, source_target_pairs={{0,1},{1,0},{2,3},{3,2},{4,5},{5,4},{6,7},{7,6},{8,9},{9,8},{10,11... | collective-permute-start | bytes 786440 | tf_op jit(solution)/shard_map/ppermute | solution.py:626
  33.7 9.7 %collective-permute-start.3 = (bf16[128,1024]{1,0:T(8,128)(2,1)S(1)}, bf16[128,1024]{1,0:T(8,128)(2,1)S(1)}, u32[]{:S(2)}, u32[]{:S(2)}) collective-permute-start(bf16[128,1024]{1,0:T(8,128)(2,1)S(1)} %collective-permute-done.1.refs_3_), channel_id=1, source_target_pairs={{0,8},{8,0},{16,24},{24,16},{1,9},{9,1},{17,25},{25,17},{2,10},{10... | collective-permute-start | bytes 786440 | tf_op jit(solution)/shard_map/ppermute | solution.py:626
  33.7 11.2 %collective-permute-start.8 = (bf16[128,1024]{1,0:T(8,128)(2,1)S(1)}, bf16[128,1024]{1,0:T(8,128)(2,1)S(1)}, u32[]{:S(2)}, u32[]{:S(2)}) collective-permute-start(bf16[128,1024]{1,0:T(8,128)(2,1)S(1)} %collective-permute-done.6.refs_4_), channel_id=1, source_target_pairs={{0,8},{8,0},{16,24},{24,16},{1,9},{9,1},{17,25},{25,17},{2,10},{10... | collective-permute-start | bytes 786440 | tf_op jit(solution)/shard_map/ppermute | solution.py:626
  38.7 2.9 %copy-start = (bf16[256,1024]{1,0:T(8,128)(2,1)S(1)}, bf16[256,1024]{1,0:T(8,128)(2,1)}, u32[]{:S(2)}) copy-start(bf16[256,1024]{1,0:T(8,128)(2,1)} %refs_0_) | copy-start | bytes 1572868
  50.7 1.6 %collective-permute-start.13 = (bf16[2,128,512]{2,1,0:T(8,128)(2,1)S(1)}, bf16[2,128,512]{2,1,0:T(8,128)(2,1)S(1)}, u32[]{:S(2)}, u32[]{:S(2)}) collective-permute-start(bf16[2,128,512]{2,1,0:T(8,128)(2,1)S(1)} %get-tuple-element.213), channel_id=1, source_target_pairs={{0,1},{1,0},{2,3},{3,2},{4,5},{5,4},{6,7},{7,6},{8,9},{9,8},{10,11... | collective-permute-start | bytes 786440 | tf_op jit(solution)/shard_map/ppermute | solution.py:626
  50.8 1.9 %collective-permute-start.14 = (bf16[2,128,512]{2,1,0:T(8,128)(2,1)S(1)}, bf16[2,128,512]{2,1,0:T(8,128)(2,1)S(1)}, u32[]{:S(2)}, u32[]{:S(2)}) collective-permute-start(bf16[2,128,512]{2,1,0:T(8,128)(2,1)S(1)} %get-tuple-element.214), channel_id=1, source_target_pairs={{0,1},{1,0},{2,3},{3,2},{4,5},{5,4},{6,7},{7,6},{8,9},{9,8},{10,11... | collective-permute-start | bytes 786440 | tf_op jit(solution)/shard_map/ppermute | solution.py:626
  52.8 8.8 %collective-permute-start.15 = (bf16[128,512]{1,0:T(8,128)(2,1)S(1)}, bf16[128,512]{1,0:T(8,128)(2,1)S(1)}, u32[]{:S(2)}, u32[]{:S(2)}) collective-permute-start(bf16[128,512]{1,0:T(8,128)(2,1)S(1)} %get-tuple-element.238), channel_id=1, source_target_pairs={{0,2},{1,3},{2,0},{3,1},{4,6},{5,7},{6,4},{7,5},{8,10},{9,11},{10,... | collective-permute-start | bytes 393224 | tf_op jit(solution)/shard_map/ppermute | solution.py:626
  52.9 8.7 %collective-permute-start.16 = (bf16[128,512]{1,0:T(8,128)(2,1)S(1)}, bf16[128,512]{1,0:T(8,128)(2,1)S(1)}, u32[]{:S(2)}, u32[]{:S(2)}) collective-permute-start(bf16[128,512]{1,0:T(8,128)(2,1)S(1)} %get-tuple-element.239), channel_id=1, source_target_pairs={{0,4},{1,5},{2,6},{3,7},{4,0},{5,1},{6,2},{7,3},{8,12},{9,13},{10,... | collective-permute-start | bytes 393224 | tf_op jit(solution)/shard_map/ppermute | solution.py:626
  54.9 6.8 %collective-permute-start.17 = (bf16[128,512]{1,0:T(8,128)(2,1)S(1)}, bf16[128,512]{1,0:T(8,128)(2,1)S(1)}, u32[]{:S(2)}, u32[]{:S(2)}) collective-permute-start(bf16[128,512]{1,0:T(8,128)(2,1)S(1)} %get-tuple-element.240), channel_id=1, source_target_pairs={{0,6},{1,7},{2,4},{3,5},{4,2},{5,3},{6,0},{7,1},{8,14},{9,15},{10,... | collective-permute-start | bytes 393224 | tf_op jit(solution)/shard_map/ppermute | solution.py:626
  59.8 2.8 %collective-permute-start.18 = (bf16[2,128,512]{2,1,0:T(8,128)(2,1)S(1)}, bf16[2,128,512]{2,1,0:T(8,128)(2,1)S(1)}, u32[]{:S(2)}, u32[]{:S(2)}) collective-permute-start(bf16[2,128,512]{2,1,0:T(8,128)(2,1)S(1)} %get-tuple-element.249), channel_id=1, source_target_pairs={{0,1},{1,0},{2,3},{3,2},{4,5},{5,4},{6,7},{7,6},{8,9},{9,8},{10,11... | collective-permute-start | bytes 786440 | tf_op jit(solution)/shard_map/ppermute | solution.py:626
  59.9 2.7 %collective-permute-start.19 = (bf16[2,128,512]{2,1,0:T(8,128)(2,1)S(1)}, bf16[2,128,512]{2,1,0:T(8,128)(2,1)S(1)}, u32[]{:S(2)}, u32[]{:S(2)}) collective-permute-start(bf16[2,128,512]{2,1,0:T(8,128)(2,1)S(1)} %get-tuple-element.250), channel_id=1, source_target_pairs={{0,1},{1,0},{2,3},{3,2},{4,5},{5,4},{6,7},{7,6},{8,9},{9,8},{10,11... | collective-permute-start | bytes 786440 | tf_op jit(solution)/shard_map/ppermute | solution.py:626
  62.5 14.8 %collective-permute-start.23 = (bf16[2,128,1024]{2,1,0:T(8,128)(2,1)S(1)}, bf16[2,128,1024]{2,1,0:T(8,128)(2,1)S(1)}, u32[]{:S(2)}, u32[]{:S(2)}) collective-permute-start(bf16[2,128,1024]{2,1,0:T(8,128)(2,1)S(1)} %all_terms.4), channel_id=1, source_target_pairs={{0,8},{8,0},{16,24},{24,16},{1,9},{9,1},{17,25},{25,17},{2,10},{10... | collective-permute-start | bytes 1572872 | tf_op jit(solution)/shard_map/ppermute | solution.py:626
  62.7 6.4 %collective-permute-start.20 = (bf16[128,512]{1,0:T(8,128)(2,1)S(1)}, bf16[128,512]{1,0:T(8,128)(2,1)S(1)}, u32[]{:S(2)}, u32[]{:S(2)}) collective-permute-start(bf16[128,512]{1,0:T(8,128)(2,1)S(1)} %get-tuple-element.271), channel_id=1, source_target_pairs={{0,2},{1,3},{2,0},{3,1},{4,6},{5,7},{6,4},{7,5},{8,10},{9,11},{10,... | collective-permute-start | bytes 393224 | tf_op jit(solution)/shard_map/ppermute | solution.py:626
  64.1 7.8 %collective-permute-start.21 = (bf16[128,512]{1,0:T(8,128)(2,1)S(1)}, bf16[128,512]{1,0:T(8,128)(2,1)S(1)}, u32[]{:S(2)}, u32[]{:S(2)}) collective-permute-start(bf16[128,512]{1,0:T(8,128)(2,1)S(1)} %get-tuple-element.272), channel_id=1, source_target_pairs={{0,4},{1,5},{2,6},{3,7},{4,0},{5,1},{6,2},{7,3},{8,12},{9,13},{10,... | collective-permute-start | bytes 393224 | tf_op jit(solution)/shard_map/ppermute | solution.py:626
  64.8 7.1 %collective-permute-start.22 = (bf16[128,512]{1,0:T(8,128)(2,1)S(1)}, bf16[128,512]{1,0:T(8,128)(2,1)S(1)}, u32[]{:S(2)}, u32[]{:S(2)}) collective-permute-start(bf16[128,512]{1,0:T(8,128)(2,1)S(1)} %get-tuple-element.273), channel_id=1, source_target_pairs={{0,6},{1,7},{2,4},{3,5},{4,2},{5,3},{6,0},{7,1},{8,14},{9,15},{10,... | collective-permute-start | bytes 393224 | tf_op jit(solution)/shard_map/ppermute | solution.py:626
  72.7 12.2 %collective-permute-start.24 = (bf16[128,1024]{1,0:T(8,128)(2,1)S(1)}, bf16[128,1024]{1,0:T(8,128)(2,1)S(1)}, u32[]{:S(2)}, u32[]{:S(2)}) collective-permute-start(bf16[128,1024]{1,0:T(8,128)(2,1)S(1)} %get-tuple-element.281), channel_id=1, source_target_pairs={{0,8},{8,0},{16,24},{24,16},{1,9},{9,1},{17,25},{25,17},{2,10},{10... | collective-permute-start | bytes 786440 | tf_op jit(solution)/shard_map/ppermute | solution.py:626
  77.4 20.6 %collective-permute-start.25 = (bf16[128,1024]{1,0:T(8,128)(2,1)S(1)}, bf16[128,1024]{1,0:T(8,128)(2,1)S(1)}, u32[]{:S(2)}, u32[]{:S(2)}) collective-permute-start(bf16[128,1024]{1,0:T(8,128)(2,1)S(1)} %add.2), channel_id=1, source_target_pairs={{0,16},{8,24},{16,0},{24,8},{1,17},{9,25},{17,1},{25,9},{2,18},{10... | collective-permute-start | bytes 786440 | tf_op jit(solution)/shard_map/ppermute | solution.py:626
  85.0 16.8 %collective-permute-start.26 = (bf16[128,1024]{1,0:T(8,128)(2,1)S(1)}, bf16[128,1024]{1,0:T(8,128)(2,1)S(1)}, u32[]{:S(2)}, u32[]{:S(2)}) collective-permute-start(bf16[128,1024]{1,0:T(8,128)(2,1)S(1)} %add.3), channel_id=1, source_target_pairs={{0,16},{8,24},{16,0},{24,8},{1,17},{9,25},{17,1},{25,9},{2,18},{10... | collective-permute-start | bytes 786440 | tf_op jit(solution)/shard_map/ppermute | solution.py:626
  85.4 16.5 %collective-permute-start.27 = (bf16[128,1024]{1,0:T(8,128)(2,1)S(1)}, bf16[128,1024]{1,0:T(8,128)(2,1)S(1)}, u32[]{:S(2)}, u32[]{:S(2)}) collective-permute-start(bf16[128,1024]{1,0:T(8,128)(2,1)S(1)} %get-tuple-element.304), channel_id=1, source_target_pairs={{0,8},{8,0},{16,24},{24,16},{1,9},{9,1},{17,25},{25,17},{2,10},{10... | collective-permute-start | bytes 786440 | tf_op jit(solution)/shard_map/ppermute | solution.py:626

commit v6 on v4

--- a/solution.py
+++ b/solution.py
@@ -720,13 +720,17 @@
             bit *= 2
         return ends
 
-    far = [{0: out_grad[:half]}, {0: out_grad[half:]}]
-    bit = heads // 2
-    while bit > 1:
-        far = [got | {k ^ bit: swap(x, bit, "head") for k, x in got.items()} for got in far]
-        bit //= 2
-    near = [swap(out_grad[:half], 1, "head"), swap(out_grad[half:], 1, "head")]
+    def spread(x):
+        got, bit = {0: x}, heads // 2
+        while bit > 1:
+            got |= {k ^ bit: swap(x, bit, "head") for k, x in got.items()}
+            bit //= 2
+        return got, swap(x, 1, "head")
+
+    first_half = spread(out_grad[:half])
     own = turn(project_kv, inputs, w_key, value_projection)
+    own, rest_rows = lax.optimization_barrier((own, out_grad))
+    far, near = (list(x) for x in zip(first_half, spread(rest_rows[half:])))
     near_blocks, (far[0], near[0]) = gather_even(own, "ctx", (far[0], near[0]))
     query = turn(project, inputs, w_query)
     query, near_blocks = lax.optimization_barrier((query, near_blocks))

time: 103 us -> 104 us (level)
  Pallas kernels: 37.5 us -> 38.8 us
    pallas_call x2, Pallas kernels: 8.39 us -> 9.53 us  [grads(): pl.pallas_call(functools.partial(grads_body, sizes, upper, spare), in_spe...]
where the time goes in v6:
time: 104 us
  Pallas kernels  38.8 us (37%)
  waiting for transfers between devices  34.7 us (33%)
  starting transfers between devices  29.4 us (28%)
  local copies, waits for them, and re-layouts  1.07 us (1%)
    ppermute x28, waiting for transfers between devices, swap(): lax.ppermute(x, axis, [(i, i ^ k) for i in range(lax.axis_size(axis))])  34.7 us
    ppermute x28, starting transfers between devices, swap(): lax.ppermute(x, axis, [(i, i ^ k) for i in range(lax.axis_size(axis))])  29.4 us
    pallas_call x2, Pallas kernels, grads(): pl.pallas_call(functools.partial(grads_body, sizes, upper, spare), in_spe...  9.53 us
    pallas_call x4, Pallas kernels, all_terms(): pl.pallas_call(functools.partial(all_terms_body, places, len(terms)), in_...  6.35 us
    pallas_call x2, Pallas kernels, stats(): pl.pallas_call(functools.partial(stats_body, sizes, upper, spare), in_spe...  5.86 us
    pallas_call x1, Pallas kernels, project(): pl.pallas_call(functools.partial(project_body, parts), in_specs=[pl.Block...  4.87 us
    pallas_call x2, Pallas kernels, query_terms(): pl.pallas_call(functools.partial(query_terms_body, places), in_specs=[pl....  4.38 us
    pallas_call x1, Pallas kernels, project_kv(): pl.pallas_call(functools.partial(kv_body, parts), in_specs=[pl.BlockSpec(...  3.32 us
  transfers between devices with their start and end apart: 28, of which 11 were waited for; matrix products, arithmetic and copies ran while one was open for 0% of the time, Pallas kernels for 30%

profile of v6, /device:TPU:0, one launch (start us, length us, event | category | flops | bytes accessed | tf_op | source)
XLA Modules:
  0.0 104.4 jit_solution(7968220960803745022)
XLA Ops:
  0.0 1.0 slice.6
  1.0 3.1 %collective-permute-start.2 = (bf16[128,1024]{1,0:T(8,128)(2,1)S(1)}, bf16[128,1024]{1,0:T(8,128)(2,1)S(1)}, u32[]{:S(2)}, u32[]{:S(2)}) collective-permute-start(bf16[128,1024]{1,0:T(8,128)(2,1)S(1)} %slice.6), channel_id=1, source_target_pairs={{0,8},{8,0},{16,24},{24,16},{1,9},{9,1},{17,25},{25,17},{2,10},{10... | collective-permute-start | bytes 786440 | tf_op jit(solution)/shard_map/ppermute | solution.py:629
  4.1 2.6 %collective-permute-start.1 = (bf16[128,1024]{1,0:T(8,128)(2,1)S(1)}, bf16[128,1024]{1,0:T(8,128)(2,1)S(1)}, u32[]{:S(2)}, u32[]{:S(2)}) collective-permute-start(bf16[128,1024]{1,0:T(8,128)(2,1)S(1)} %slice.6), channel_id=1, source_target_pairs={{0,16},{8,24},{16,0},{24,8},{1,17},{9,25},{17,1},{25,9},{2,18},{10... | collective-permute-start | bytes 786440 | tf_op jit(solution)/shard_map/ppermute | solution.py:629
  6.7 3.3 %project_kv.1.refs_0_ = bf16[256,512]{1,0:T(8,128)(2,1)S(1)} custom-call(bf16[256,4096]{1,0:T(8,128)(2,1)} %x_ref.1, bf16[4096,256]{1,0:T(8,128)(2,1)} %refs_4_.2, bf16[4096,256]{1,0:T(8,128)(2,1)} %refs_5_.1), custom_call_target="tpu_custom_call" | custom-call | bytes 1 | tf_op jit(solution)/shard_map/project_kv/pallas_call | solution.py:89
  10.1 1.6 %collective-permute-start = (bf16[256,512]{1,0:T(8,128)(2,1)S(1)}, bf16[256,512]{1,0:T(8,128)(2,1)S(1)}, u32[]{:S(2)}, u32[]{:S(2)}) collective-permute-start(bf16[256,512]{1,0:T(8,128)(2,1)S(1)} %project_kv.1.refs_0_), channel_id=1, source_target_pairs={{0,2},{1,3},{2,0},{3,1},{4,6},{5,7},{6,4},{7,5},{8,10},{9,11},{10,... | collective-permute-start | bytes 786440 | tf_op jit(solution)/shard_map/ppermute | solution.py:629
  11.6 1.5 %collective-permute-start.4 = (bf16[256,512]{1,0:T(8,128)(2,1)S(1)}, bf16[256,512]{1,0:T(8,128)(2,1)S(1)}, u32[]{:S(2)}, u32[]{:S(2)}) collective-permute-start(bf16[256,512]{1,0:T(8,128)(2,1)S(1)} %project_kv.1.refs_0_), channel_id=1, source_target_pairs={{0,4},{1,5},{2,6},{3,7},{4,0},{5,1},{6,2},{7,3},{8,12},{9,13},{10,... | collective-permute-start | bytes 786440 | tf_op jit(solution)/shard_map/ppermute | solution.py:629
  13.1 2.8 %collective-permute-done.2.refs_1_ = bf16[128,1024]{1,0:T(8,128)(2,1)S(1)} collective-permute-done((bf16[128,1024]{1,0:T(8,128)(2,1)S(1)}, bf16[128,1024]{1,0:T(8,128)(2,1)S(1)}, u32[]{:S(2)}, u32[]{:S(2)}) %collective-permute-start.2) | collective-permute-done | bytes 262176 | tf_op jit(solution)/shard_map/ppermute | solution.py:629
  15.9 2.5 %collective-permute-done.1.refs_3_ = bf16[128,1024]{1,0:T(8,128)(2,1)S(1)} collective-permute-done((bf16[128,1024]{1,0:T(8,128)(2,1)S(1)}, bf16[128,1024]{1,0:T(8,128)(2,1)S(1)}, u32[]{:S(2)}, u32[]{:S(2)}) %collective-permute-start.1) | collective-permute-done | bytes 262176 | tf_op jit(solution)/shard_map/ppermute | solution.py:629
  18.5 1.5 %collective-permute-start.5 = (bf16[256,512]{1,0:T(8,128)(2,1)S(1)}, bf16[256,512]{1,0:T(8,128)(2,1)S(1)}, u32[]{:S(2)}, u32[]{:S(2)}) collective-permute-start(bf16[256,512]{1,0:T(8,128)(2,1)S(1)} %collective-permute-done.refs_1_), channel_id=1, source_target_pairs={{0,4},{1,5},{2,6},{3,7},{4,0},{5,1},{6,2},{7,3},{8,12},{9,13},{10,... | collective-permute-start | bytes 786440 | tf_op jit(solution)/shard_map/ppermute | solution.py:629
  20.0 0.5 collective-permute-start.7
  20.6 2.6 %collective-permute-start.6 = (bf16[128,1024]{1,0:T(8,128)(2,1)S(1)}, bf16[128,1024]{1,0:T(8,128)(2,1)S(1)}, u32[]{:S(2)}, u32[]{:S(2)}) collective-permute-start(bf16[128,1024]{1,0:T(8,128)(2,1)S(1)} %slice.7), channel_id=1, source_target_pairs={{0,16},{8,24},{16,0},{24,8},{1,17},{9,25},{17,1},{25,9},{2,18},{10... | collective-permute-start | bytes 786440 | tf_op jit(solution)/shard_map/ppermute | solution.py:629
  23.2 4.9 %project.1.q_ref = bf16[256,1024]{1,0:T(8,128)(2,1)S(1)} custom-call(bf16[256,4096]{1,0:T(8,128)(2,1)} %x_ref.1, bf16[4096,1024]{1,0:T(8,128)(2,1)} %w_ref.1), custom_call_target="tpu_custom_call" | custom-call | bytes 1 | tf_op jit(solution)/shard_map/project/pallas_call | solution.py:135
  28.2 0.5 collective-permute-start.10
  28.7 1.2 %collective-permute-done.7.refs_2_ = bf16[128,1024]{1,0:T(8,128)(2,1)S(1)} collective-permute-done((bf16[128,1024]{1,0:T(8,128)(2,1)S(1)}, bf16[128,1024]{1,0:T(8,128)(2,1)S(1)}, u32[]{:S(2)}, u32[]{:S(2)}) %collective-permute-start.7) | collective-permute-done | bytes 262176 | tf_op jit(solution)/shard_map/ppermute | solution.py:629
  29.9 3.8 %collective-permute-done.6.refs_4_ = bf16[128,1024]{1,0:T(8,128)(2,1)S(1)} collective-permute-done((bf16[128,1024]{1,0:T(8,128)(2,1)S(1)}, bf16[128,1024]{1,0:T(8,128)(2,1)S(1)}, u32[]{:S(2)}, u32[]{:S(2)}) %collective-permute-start.6) | collective-permute-done | bytes 262176 | tf_op jit(solution)/shard_map/ppermute | solution.py:629
  33.7 2.0 %collective-permute-start.8 = (bf16[128,1024]{1,0:T(8,128)(2,1)S(1)}, bf16[128,1024]{1,0:T(8,128)(2,1)S(1)}, u32[]{:S(2)}, u32[]{:S(2)}) collective-permute-start(bf16[128,1024]{1,0:T(8,128)(2,1)S(1)} %collective-permute-done.6.refs_4_), channel_id=1, source_target_pairs={{0,8},{8,0},{16,24},{24,16},{1,9},{9,1},{17,25},{25,17},{2,10},{10... | collective-permute-start | bytes 786440 | tf_op jit(solution)/shard_map/ppermute | solution.py:629
  35.8 3.0 %upper_stats.1 = (f32[2,2,512]{2,1,0:T(2,128)S(1)}, f32[2,128,512]{2,1,0:T(8,128)S(1)}, bf16[2,1024,1024]{2,1,0:T(8,128)(2,1)S(1)}, bf16[2048,512]{1,0:T(8,128)(2,1)S(1)}) custom-call(s32[16]{0:T(128)S(1)} %copy-done.1, s32[8]{0:T(128)S(1)} %copy-done.2, bf16[256,1024]{1,0:T(8,128)(2,1)S(1)} %project.1.q_ref, bf16[256,512]{1,0:T(8,128)(2,1)S(1)} %project_kv.1.refs_0_, ...), custom_call_target="tpu_custom_call" | custom-call | bytes 1 | tf_op jit(solution)/shard_map/upper_stats/pallas_call | solution.py:479
  38.8 2.9 %lower_stats.1 = (f32[2,2,512]{2,1,0:T(2,128)S(1)}, f32[2,128,512]{2,1,0:T(8,128)S(1)}, bf16[2,1024,1024]{2,1,0:T(8,128)(2,1)S(1)}) custom-call(s32[16]{0:T(128)S(1)} %copy-done.1, s32[8]{0:T(128)S(1)} %copy-done.2, bf16[256,1024]{1,0:T(8,128)(2,1)S(1)} %project.1.q_ref, bf16[2048,512]{1,0:T(8,128)(2,1)S(1)} %get-tuple-element.221.refs_0_.refs_1_, ...), custom_call_target="tpu_custom_call" | custom-call | bytes 1 | tf_op jit(solution)/shard_map/lower_stats/pallas_call | solution.py:479
  41.7 1.8 %context_grad.2.refs_0_ = f32[256,1024]{1,0:T(8,128)S(1)} custom-call(bf16[256,1024]{1,0:T(8,128)(2,1)S(1)} %copy-done, bf16[128,1024]{1,0:T(8,128)(2,1)S(1)} %collective-permute-done.2.refs_1_, bf16[128,1024]{1,0:T(8,128)(2,1)S(1)} %collective-permute-done.7.refs_2_, bf16[128,1024]{1,0:T(8,128)(2,1)S(1)} %collective-permute-done.1.refs_3_, ...), custom_call_target="tpu_custom_call" | custom-call | bytes 1 | tf_op jit(solution)/shard_map/context_grad/pallas_call | solution.py:171
  43.5 1.4 %collective-permute-done.8.refs_2_ = bf16[128,1024]{1,0:T(8,128)(2,1)S(1)} collective-permute-done((bf16[128,1024]{1,0:T(8,128)(2,1)S(1)}, bf16[128,1024]{1,0:T(8,128)(2,1)S(1)}, u32[]{:S(2)}, u32[]{:S(2)}) %collective-permute-start.8) | collective-permute-done | bytes 262176 | tf_op jit(solution)/shard_map/ppermute | solution.py:629
  44.9 0.7 context_grad.3.g_ref
  45.7 5.1 %upper_grads.1 = (bf16[128,1024]{1,0:T(8,128)(2,1)S(1)}, bf16[4,128,512]{2,1,0:T(8,128)(2,1)S(1)}, bf16[2,128,512]{2,1,0:T(8,128)(2,1)S(1)}, bf16[2,128,512]{2,1,0:T(8,128)(2,1)S(1)}, f32[2048,512]{1,0:T(8,128)S(1)}) custom-call(s32[16]{0:T(128)S(1)} %copy-done.1, s32[8]{0:T(128)S(1)} %copy-done.2, bf16[256,1024]{1,0:T(8,128)(2,1)S(1)} %project.1.q_ref, ...), custom_call_target="tpu_custom_call" | custom-call | bytes 1 | tf_op jit(solution)/shard_map/upper_grads/pallas_call | solution.py:610
  50.8 0.5 collective-permute-start.14
  51.3 1.0 collective-permute-done.13.refs_0_
  52.3 0.4 collective-permute-done.14.refs_1_
  52.8 0.4 collective-permute-start.15
  53.2 0.3 collective-permute-start.16
  53.5 2.9 %collective-permute-start.17 = (bf16[128,512]{1,0:T(8,128)(2,1)S(1)}, bf16[128,512]{1,0:T(8,128)(2,1)S(1)}, u32[]{:S(2)}, u32[]{:S(2)}) collective-permute-start(bf16[128,512]{1,0:T(8,128)(2,1)S(1)} %get-tuple-element.235), channel_id=1, source_target_pairs={{0,6},{1,7},{2,4},{3,5},{4,2},{5,3},{6,0},{7,1},{8,14},{9,15},{10,... | collective-permute-start | bytes 393224 | tf_op jit(solution)/shard_map/ppermute | solution.py:629
  56.4 4.5 %lower_grads.1 = (bf16[128,1024]{1,0:T(8,128)(2,1)S(1)}, bf16[4,128,512]{2,1,0:T(8,128)(2,1)S(1)}, bf16[2,128,512]{2,1,0:T(8,128)(2,1)S(1)}, bf16[2,128,512]{2,1...) custom-call(s32[16]{0:T(128)S(1)} %copy-done.1, ...), custom_call_target="tpu_custom_call" | custom-call | bytes 1 | tf_op jit(solution)/shard_map/lower_grads/pallas_call | solution.py:610
  60.9 0.5 collective-permute-start.19
  61.4 1.3 %query_terms.2 = (f32[2,128,1024]{2,1,0:T(8,128)S(1)}, f32[2,128,1024]{2,1,0:T(8,128)S(1)}) custom-call(bf16[128,1024]{1,0:T(8,128)(2,1)S(1)} %get-tuple-element.250.upper_ref, bf16[128,1024]{1,0:T(8,128)(2,1)S(1)} %get-tuple-element.251.lower_ref, bf16[2,1024,1024]{2,1,0:T(8,128)(2,1)S(1)} %get-tuple-element.229.w_ref), custom_call_target="tpu_custom_call" | custom-call | bytes 1 | tf_op jit(solution)/shard_map/query_terms/pallas_call | solution.py:231
  62.8 0.8 all_terms.4
  63.8 0.3 collective-permute-start.20
  64.1 0.5 collective-permute-start.21
  64.6 2.7 %collective-permute-start.22 = (bf16[128,512]{1,0:T(8,128)(2,1)S(1)}, bf16[128,512]{1,0:T(8,128)(2,1)S(1)}, u32[]{:S(2)}, u32[]{:S(2)}) collective-permute-start(bf16[128,512]{1,0:T(8,128)(2,1)S(1)} %get-tuple-element.265), channel_id=1, source_target_pairs={{0,6},{1,7},{2,4},{3,5},{4,2},{5,3},{6,0},{7,1},{8,14},{9,15},{10,... | collective-permute-start | bytes 393224 | tf_op jit(solution)/shard_map/ppermute | solution.py:629
  67.4 3.1 %query_terms.3 = (f32[2,128,1024]{2,1,0:T(8,128)S(1)}, f32[2,128,1024]{2,1,0:T(8,128)S(1)}) custom-call(bf16[128,1024]{1,0:T(8,128)(2,1)S(1)} %get-tuple-element.250.upper_ref, bf16[128,1024]{1,0:T(8,128)(2,1)S(1)} %get-tuple-element.251.lower_ref, bf16[4096,1024]{1,0:T(8,128)(2,1)} %w_ref.1), custom_call_target="tpu_custom_call" | custom-call | bytes 1 | tf_op jit(solution)/shard_map/query_terms/pallas_call | solution.py:231
  70.5 2.4 %all_terms.5 = (bf16[128,1024]{1,0:T(8,128)(2,1)S(1)}, bf16[128,1024]{1,0:T(8,128)(2,1)S(1)}) custom-call(f32[2,128,1024]{2,1,0:T(8,128)S(1)} %get-tuple-element.254.first_ref, bf16[128,512]{1,0:T(8,128)(2,1)S(1)} %get-tuple-element.255.refs_0_, bf16[128,512]{1,0:T(8,128)(2,1)S(1)} %collective-permute-done.15.refs_1_, ...), custom_call_target="tpu_custom_call" | custom-call | bytes 1 | tf_op jit(solution)/shard_map/all_terms/pallas_call | solution.py:280
  72.9 0.8 all_terms.6
  73.7 2.1 %collective-permute-start.24 = (bf16[128,1024]{1,0:T(8,128)(2,1)S(1)}, bf16[128,1024]{1,0:T(8,128)(2,1)S(1)}, u32[]{:S(2)}, u32[]{:S(2)}) collective-permute-start(bf16[128,1024]{1,0:T(8,128)(2,1)S(1)} %get-tuple-element.273), channel_id=1, source_target_pairs={{0,8},{8,0},{16,24},{24,16},{1,9},{9,1},{17,25},{25,17},{2,10},{10... | collective-permute-start | bytes 786440 | tf_op jit(solution)/shard_map/ppermute | solution.py:629
  75.8 2.7 %collective-permute-done.23.b_ref = bf16[2,128,1024]{2,1,0:T(8,128)(2,1)S(1)} collective-permute-done((bf16[2,128,1024]{2,1,0:T(8,128)(2,1)S(1)}, bf16[2,128,1024]{2,1,0:T(8,128)(2,1)S(1)}, u32[]{:S(2)}, u32[]{:S(2)}) %collective-permute-start.23) | collective-permute-done | bytes 524320 | tf_op jit(solution)/shard_map/ppermute | solution.py:629
  78.5 0.2 collective-permute-start.25
  78.7 2.4 %all_terms.7 = (bf16[128,1024]{1,0:T(8,128)(2,1)S(1)}, bf16[128,1024]{1,0:T(8,128)(2,1)S(1)}) custom-call(f32[2,128,1024]{2,1,0:T(8,128)S(1)} %get-tuple-element.277.first_ref, bf16[128,512]{1,0:T(8,128)(2,1)S(1)} %get-tuple-element.278.refs_0_, bf16[128,512]{1,0:T(8,128)(2,1)S(1)} %collective-permute-done.20.refs_1_, ...), custom_call_target="tpu_custom_call" | custom-call | bytes 1 | tf_op jit(solution)/shard_map/all_terms/pallas_call | solution.py:280
  81.1 4.9 %collective-permute-done.24.b_ref = bf16[128,1024]{1,0:T(8,128)(2,1)S(1)} collective-permute-done((bf16[128,1024]{1,0:T(8,128)(2,1)S(1)}, bf16[128,1024]{1,0:T(8,128)(2,1)S(1)}, u32[]{:S(2)}, u32[]{:S(2)}) %collective-permute-start.24) | collective-permute-done | bytes 262176 | tf_op jit(solution)/shard_map/ppermute | solution.py:629
  86.0 0.2 collective-permute-start.26
  86.3 2.5 %collective-permute-start.27 = (bf16[128,1024]{1,0:T(8,128)(2,1)S(1)}, bf16[128,1024]{1,0:T(8,128)(2,1)S(1)}, u32[]{:S(2)}, u32[]{:S(2)}) collective-permute-start(bf16[128,1024]{1,0:T(8,128)(2,1)S(1)} %get-tuple-element.296), channel_id=1, source_target_pairs={{0,8},{8,0},{16,24},{24,16},{1,9},{9,1},{17,25},{25,17},{2,10},{10... | collective-permute-start | bytes 786440 | tf_op jit(solution)/shard_map/ppermute | solution.py:629
  88.9 10.4 %collective-permute-done.25.b_ref = bf16[128,1024]{1,0:T(8,128)(2,1)S(1)} collective-permute-done((bf16[128,1024]{1,0:T(8,128)(2,1)S(1)}, bf16[128,1024]{1,0:T(8,128)(2,1)S(1)}, u32[]{:S(2)}, u32[]{:S(2)}) %collective-permute-start.25) | collective-permute-done | bytes 262176 | tf_op jit(solution)/shard_map/ppermute | solution.py:629
  99.3 3.6 %collective-permute-done.26.b_ref = bf16[128,1024]{1,0:T(8,128)(2,1)S(1)} collective-permute-done((bf16[128,1024]{1,0:T(8,128)(2,1)S(1)}, bf16[128,1024]{1,0:T(8,128)(2,1)S(1)}, u32[]{:S(2)}, u32[]{:S(2)}) %collective-permute-start.26) | collective-permute-done | bytes 262176 | tf_op jit(solution)/shard_map/ppermute | solution.py:629
  103.0 1.4 %join_rows.1 = bf16[256,1024]{1,0:T(8,128)(2,1)} custom-call(s32[16]{0:T(128)S(1)} %copy-done.1, f32[128,1024]{1,0:T(8,128)S(1)} %merge.4.refs_0_, f32[128,1024]{1,0:T(8,128)S(1)} %merge.5.refs_1_, bf16[128,1024]{1,0:T(8,128)(2,1)S(1)} %collective-permute-done.27.refs_2_), custom_call_target="tpu_custom_call" | custom-call | bytes 1 | tf_op jit(solution)/shard_map/join_rows/pallas_call | solution.py:347
  (38 shorter events, 1.0 us)
Async XLA Ops:
  0.0 20.0 %copy-start = (bf16[256,1024]{1,0:T(8,128)(2,1)S(1)}, bf16[256,1024]{1,0:T(8,128)(2,1)}, u32[]{:S(2)}) copy-start(bf16[256,1024]{1,0:T(8,128)(2,1)} %refs_0_) | copy-start | bytes 1572868
  1.0 14.9 %collective-permute-start.2 = (bf16[128,1024]{1,0:T(8,128)(2,1)S(1)}, bf16[128,1024]{1,0:T(8,128)(2,1)S(1)}, u32[]{:S(2)}, u32[]{:S(2)}) collective-permute-start(bf16[128,1024]{1,0:T(8,128)(2,1)S(1)} %slice.6), channel_id=1, source_target_pairs={{0,8},{8,0},{16,24},{24,16},{1,9},{9,1},{17,25},{25,17},{2,10},{10... | collective-permute-start | bytes 786440 | tf_op jit(solution)/shard_map/ppermute | solution.py:629
  4.1 14.3 %collective-permute-start.1 = (bf16[128,1024]{1,0:T(8,128)(2,1)S(1)}, bf16[128,1024]{1,0:T(8,128)(2,1)S(1)}, u32[]{:S(2)}, u32[]{:S(2)}) collective-permute-start(bf16[128,1024]{1,0:T(8,128)(2,1)S(1)} %slice.6), channel_id=1, source_target_pairs={{0,16},{8,24},{16,0},{24,8},{1,17},{9,25},{17,1},{25,9},{2,18},{10... | collective-permute-start | bytes 786440 | tf_op jit(solution)/shard_map/ppermute | solution.py:629
  10.1 8.4 %collective-permute-start = (bf16[256,512]{1,0:T(8,128)(2,1)S(1)}, bf16[256,512]{1,0:T(8,128)(2,1)S(1)}, u32[]{:S(2)}, u32[]{:S(2)}) collective-permute-start(bf16[256,512]{1,0:T(8,128)(2,1)S(1)} %project_kv.1.refs_0_), channel_id=1, source_target_pairs={{0,2},{1,3},{2,0},{3,1},{4,6},{5,7},{6,4},{7,5},{8,10},{9,11},{10,... | collective-permute-start | bytes 786440 | tf_op jit(solution)/shard_map/ppermute | solution.py:629
  11.6 16.5 %collective-permute-start.4 = (bf16[256,512]{1,0:T(8,128)(2,1)S(1)}, bf16[256,512]{1,0:T(8,128)(2,1)S(1)}, u32[]{:S(2)}, u32[]{:S(2)}) collective-permute-start(bf16[256,512]{1,0:T(8,128)(2,1)S(1)} %project_kv.1.refs_0_), channel_id=1, source_target_pairs={{0,4},{1,5},{2,6},{3,7},{4,0},{5,1},{6,2},{7,3},{8,12},{9,13},{10,... | collective-permute-start | bytes 786440 | tf_op jit(solution)/shard_map/ppermute | solution.py:629
  18.5 9.6 %collective-permute-start.5 = (bf16[256,512]{1,0:T(8,128)(2,1)S(1)}, bf16[256,512]{1,0:T(8,128)(2,1)S(1)}, u32[]{:S(2)}, u32[]{:S(2)}) collective-permute-start(bf16[256,512]{1,0:T(8,128)(2,1)S(1)} %collective-permute-done.refs_1_), channel_id=1, source_target_pairs={{0,4},{1,5},{2,6},{3,7},{4,0},{5,1},{6,2},{7,3},{8,12},{9,13},{10,... | collective-permute-start | bytes 786440 | tf_op jit(solution)/shard_map/ppermute | solution.py:629
  20.0 15.8 %copy-start.1 = (s32[16]{0:T(128)S(1)}, s32[16]{0:T(128)}, u32[]{:S(2)}) copy-start(s32[16]{0:T(128)} %order.9) | copy-start | bytes 196
  20.0 15.8 %copy-start.2 = (s32[8]{0:T(128)S(1)}, s32[8]{0:T(128)}, u32[]{:S(2)}) copy-start(s32[8]{0:T(128)} %lengths.7) | copy-start | bytes 100
  20.0 9.9 %collective-permute-start.7 = (bf16[128,1024]{1,0:T(8,128)(2,1)S(1)}, bf16[128,1024]{1,0:T(8,128)(2,1)S(1)}, u32[]{:S(2)}, u32[]{:S(2)}) collective-permute-start(bf16[128,1024]{1,0:T(8,128)(2,1)S(1)} %slice.7), channel_id=1, source_target_pairs={{0,8},{8,0},{16,24},{24,16},{1,9},{9,1},{17,25},{25,17},{2,10},{10... | collective-permute-start | bytes 786440 | tf_op jit(solution)/shard_map/ppermute | solution.py:629
  20.6 13.2 %collective-permute-start.6 = (bf16[128,1024]{1,0:T(8,128)(2,1)S(1)}, bf16[128,1024]{1,0:T(8,128)(2,1)S(1)}, u32[]{:S(2)}, u32[]{:S(2)}) collective-permute-start(bf16[128,1024]{1,0:T(8,128)(2,1)S(1)} %slice.7), channel_id=1, source_target_pairs={{0,16},{8,24},{16,0},{24,8},{1,17},{9,25},{17,1},{25,9},{2,18},{10... | collective-permute-start | bytes 786440 | tf_op jit(solution)/shard_map/ppermute | solution.py:629
  28.1 5.7 %collective-permute-start.9 = (bf16[256,512]{1,0:T(8,128)(2,1)S(1)}, bf16[256,512]{1,0:T(8,128)(2,1)S(1)}, u32[]{:S(2)}, u32[]{:S(2)}) collective-permute-start(bf16[256,512]{1,0:T(8,128)(2,1)S(1)} %project_kv.1.refs_0_), channel_id=1, source_target_pairs={{0,1},{1,0},{2,3},{3,2},{4,5},{5,4},{6,7},{7,6},{8,9},{9,8},{10,11... | collective-permute-start | bytes 786440 | tf_op jit(solution)/shard_map/ppermute | solution.py:629
  28.2 7.6 %collective-permute-start.10 = (bf16[256,512]{1,0:T(8,128)(2,1)S(1)}, bf16[256,512]{1,0:T(8,128)(2,1)S(1)}, u32[]{:S(2)}, u32[]{:S(2)}) collective-permute-start(bf16[256,512]{1,0:T(8,128)(2,1)S(1)} %collective-permute-done.refs_1_), channel_id=1, source_target_pairs={{0,1},{1,0},{2,3},{3,2},{4,5},{5,4},{6,7},{7,6},{8,9},{9,8},{10,11... | collective-permute-start | bytes 786440 | tf_op jit(solution)/shard_map/ppermute | solution.py:629
  28.7 7.1 %collective-permute-start.11 = (bf16[256,512]{1,0:T(8,128)(2,1)S(1)}, bf16[256,512]{1,0:T(8,128)(2,1)S(1)}, u32[]{:S(2)}, u32[]{:S(2)}) collective-permute-start(bf16[256,512]{1,0:T(8,128)(2,1)S(1)} %collective-permute-done.4.refs_2_), channel_id=1, source_target_pairs={{0,1},{1,0},{2,3},{3,2},{4,5},{5,4},{6,7},{7,6},{8,9},{9,8},{10,11... | collective-permute-start | bytes 786440 | tf_op jit(solution)/shard_map/ppermute | solution.py:629
  29.9 5.9 %collective-permute-start.12 = (bf16[256,512]{1,0:T(8,128)(2,1)S(1)}, bf16[256,512]{1,0:T(8,128)(2,1)S(1)}, u32[]{:S(2)}, u32[]{:S(2)}) collective-permute-start(bf16[256,512]{1,0:T(8,128)(2,1)S(1)} %collective-permute-done.5.refs_3_), channel_id=1, source_target_pairs={{0,1},{1,0},{2,3},{3,2},{4,5},{5,4},{6,7},{7,6},{8,9},{9,8},{10,11... | collective-permute-start | bytes 786440 | tf_op jit(solution)/shard_map/ppermute | solution.py:629
  33.7 9.8 %collective-permute-start.3 = (bf16[128,1024]{1,0:T(8,128)(2,1)S(1)}, bf16[128,1024]{1,0:T(8,128)(2,1)S(1)}, u32[]{:S(2)}, u32[]{:S(2)}) collective-permute-start(bf16[128,1024]{1,0:T(8,128)(2,1)S(1)} %collective-permute-done.1.refs_3_), channel_id=1, source_target_pairs={{0,8},{8,0},{16,24},{24,16},{1,9},{9,1},{17,25},{25,17},{2,10},{10... | collective-permute-start | bytes 786440 | tf_op jit(solution)/shard_map/ppermute | solution.py:629
  33.7 11.2 %collective-permute-start.8 = (bf16[128,1024]{1,0:T(8,128)(2,1)S(1)}, bf16[128,1024]{1,0:T(8,128)(2,1)S(1)}, u32[]{:S(2)}, u32[]{:S(2)}) collective-permute-start(bf16[128,1024]{1,0:T(8,128)(2,1)S(1)} %collective-permute-done.6.refs_4_), channel_id=1, source_target_pairs={{0,8},{8,0},{16,24},{24,16},{1,9},{9,1},{17,25},{25,17},{2,10},{10... | collective-permute-start | bytes 786440 | tf_op jit(solution)/shard_map/ppermute | solution.py:629
  50.7 1.6 %collective-permute-start.13 = (bf16[2,128,512]{2,1,0:T(8,128)(2,1)S(1)}, bf16[2,128,512]{2,1,0:T(8,128)(2,1)S(1)}, u32[]{:S(2)}, u32[]{:S(2)}) collective-permute-start(bf16[2,128,512]{2,1,0:T(8,128)(2,1)S(1)} %get-tuple-element.208), channel_id=1, source_target_pairs={{0,1},{1,0},{2,3},{3,2},{4,5},{5,4},{6,7},{7,6},{8,9},{9,8},{10,11... | collective-permute-start | bytes 786440 | tf_op jit(solution)/shard_map/ppermute | solution.py:629
  50.8 1.9 %collective-permute-start.14 = (bf16[2,128,512]{2,1,0:T(8,128)(2,1)S(1)}, bf16[2,128,512]{2,1,0:T(8,128)(2,1)S(1)}, u32[]{:S(2)}, u32[]{:S(2)}) collective-permute-start(bf16[2,128,512]{2,1,0:T(8,128)(2,1)S(1)} %get-tuple-element.209), channel_id=1, source_target_pairs={{0,1},{1,0},{2,3},{3,2},{4,5},{5,4},{6,7},{7,6},{8,9},{9,8},{10,11... | collective-permute-start | bytes 786440 | tf_op jit(solution)/shard_map/ppermute | solution.py:629
  52.8 9.9 %collective-permute-start.15 = (bf16[128,512]{1,0:T(8,128)(2,1)S(1)}, bf16[128,512]{1,0:T(8,128)(2,1)S(1)}, u32[]{:S(2)}, u32[]{:S(2)}) collective-permute-start(bf16[128,512]{1,0:T(8,128)(2,1)S(1)} %get-tuple-element.233), channel_id=1, source_target_pairs={{0,2},{1,3},{2,0},{3,1},{4,6},{5,7},{6,4},{7,5},{8,10},{9,11},{10,... | collective-permute-start | bytes 393224 | tf_op jit(solution)/shard_map/ppermute | solution.py:629
  53.2 9.5 %collective-permute-start.16 = (bf16[128,512]{1,0:T(8,128)(2,1)S(1)}, bf16[128,512]{1,0:T(8,128)(2,1)S(1)}, u32[]{:S(2)}, u32[]{:S(2)}) collective-permute-start(bf16[128,512]{1,0:T(8,128)(2,1)S(1)} %get-tuple-element.234), channel_id=1, source_target_pairs={{0,4},{1,5},{2,6},{3,7},{4,0},{5,1},{6,2},{7,3},{8,12},{9,13},{10,... | collective-permute-start | bytes 393224 | tf_op jit(solution)/shard_map/ppermute | solution.py:629
  53.5 9.3 %collective-permute-start.17 = (bf16[128,512]{1,0:T(8,128)(2,1)S(1)}, bf16[128,512]{1,0:T(8,128)(2,1)S(1)}, u32[]{:S(2)}, u32[]{:S(2)}) collective-permute-start(bf16[128,512]{1,0:T(8,128)(2,1)S(1)} %get-tuple-element.235), channel_id=1, source_target_pairs={{0,6},{1,7},{2,4},{3,5},{4,2},{5,3},{6,0},{7,1},{8,14},{9,15},{10,... | collective-permute-start | bytes 393224 | tf_op jit(solution)/shard_map/ppermute | solution.py:629
  60.9 2.8 %collective-permute-start.18 = (bf16[2,128,512]{2,1,0:T(8,128)(2,1)S(1)}, bf16[2,128,512]{2,1,0:T(8,128)(2,1)S(1)}, u32[]{:S(2)}, u32[]{:S(2)}) collective-permute-start(bf16[2,128,512]{2,1,0:T(8,128)(2,1)S(1)} %get-tuple-element.244), channel_id=1, source_target_pairs={{0,1},{1,0},{2,3},{3,2},{4,5},{5,4},{6,7},{7,6},{8,9},{9,8},{10,11... | collective-permute-start | bytes 786440 | tf_op jit(solution)/shard_map/ppermute | solution.py:629
  60.9 2.7 %collective-permute-start.19 = (bf16[2,128,512]{2,1,0:T(8,128)(2,1)S(1)}, bf16[2,128,512]{2,1,0:T(8,128)(2,1)S(1)}, u32[]{:S(2)}, u32[]{:S(2)}) collective-permute-start(bf16[2,128,512]{2,1,0:T(8,128)(2,1)S(1)} %get-tuple-element.245), channel_id=1, source_target_pairs={{0,1},{1,0},{2,3},{3,2},{4,5},{5,4},{6,7},{7,6},{8,9},{9,8},{10,11... | collective-permute-start | bytes 786440 | tf_op jit(solution)/shard_map/ppermute | solution.py:629
  63.6 14.8 %collective-permute-start.23 = (bf16[2,128,1024]{2,1,0:T(8,128)(2,1)S(1)}, bf16[2,128,1024]{2,1,0:T(8,128)(2,1)S(1)}, u32[]{:S(2)}, u32[]{:S(2)}) collective-permute-start(bf16[2,128,1024]{2,1,0:T(8,128)(2,1)S(1)} %all_terms.4), channel_id=1, source_target_pairs={{0,8},{8,0},{16,24},{24,16},{1,9},{9,1},{17,25},{25,17},{2,10},{10... | collective-permute-start | bytes 1572872 | tf_op jit(solution)/shard_map/ppermute | solution.py:629
  63.8 9.0 %collective-permute-start.20 = (bf16[128,512]{1,0:T(8,128)(2,1)S(1)}, bf16[128,512]{1,0:T(8,128)(2,1)S(1)}, u32[]{:S(2)}, u32[]{:S(2)}) collective-permute-start(bf16[128,512]{1,0:T(8,128)(2,1)S(1)} %get-tuple-element.263), channel_id=1, source_target_pairs={{0,2},{1,3},{2,0},{3,1},{4,6},{5,7},{6,4},{7,5},{8,10},{9,11},{10,... | collective-permute-start | bytes 393224 | tf_op jit(solution)/shard_map/ppermute | solution.py:629
  64.1 8.7 %collective-permute-start.21 = (bf16[128,512]{1,0:T(8,128)(2,1)S(1)}, bf16[128,512]{1,0:T(8,128)(2,1)S(1)}, u32[]{:S(2)}, u32[]{:S(2)}) collective-permute-start(bf16[128,512]{1,0:T(8,128)(2,1)S(1)} %get-tuple-element.264), channel_id=1, source_target_pairs={{0,4},{1,5},{2,6},{3,7},{4,0},{5,1},{6,2},{7,3},{8,12},{9,13},{10,... | collective-permute-start | bytes 393224 | tf_op jit(solution)/shard_map/ppermute | solution.py:629
  64.6 8.2 %collective-permute-start.22 = (bf16[128,512]{1,0:T(8,128)(2,1)S(1)}, bf16[128,512]{1,0:T(8,128)(2,1)S(1)}, u32[]{:S(2)}, u32[]{:S(2)}) collective-permute-start(bf16[128,512]{1,0:T(8,128)(2,1)S(1)} %get-tuple-element.265), channel_id=1, source_target_pairs={{0,6},{1,7},{2,4},{3,5},{4,2},{5,3},{6,0},{7,1},{8,14},{9,15},{10,... | collective-permute-start | bytes 393224 | tf_op jit(solution)/shard_map/ppermute | solution.py:629
  73.7 12.3 %collective-permute-start.24 = (bf16[128,1024]{1,0:T(8,128)(2,1)S(1)}, bf16[128,1024]{1,0:T(8,128)(2,1)S(1)}, u32[]{:S(2)}, u32[]{:S(2)}) collective-permute-start(bf16[128,1024]{1,0:T(8,128)(2,1)S(1)} %get-tuple-element.273), channel_id=1, source_target_pairs={{0,8},{8,0},{16,24},{24,16},{1,9},{9,1},{17,25},{25,17},{2,10},{10... | collective-permute-start | bytes 786440 | tf_op jit(solution)/shard_map/ppermute | solution.py:629
  78.5 20.7 %collective-permute-start.25 = (bf16[128,1024]{1,0:T(8,128)(2,1)S(1)}, bf16[128,1024]{1,0:T(8,128)(2,1)S(1)}, u32[]{:S(2)}, u32[]{:S(2)}) collective-permute-start(bf16[128,1024]{1,0:T(8,128)(2,1)S(1)} %add.2), channel_id=1, source_target_pairs={{0,16},{8,24},{16,0},{24,8},{1,17},{9,25},{17,1},{25,9},{2,18},{10... | collective-permute-start | bytes 786440 | tf_op jit(solution)/shard_map/ppermute | solution.py:629
  86.0 16.9 %collective-permute-start.26 = (bf16[128,1024]{1,0:T(8,128)(2,1)S(1)}, bf16[128,1024]{1,0:T(8,128)(2,1)S(1)}, u32[]{:S(2)}, u32[]{:S(2)}) collective-permute-start(bf16[128,1024]{1,0:T(8,128)(2,1)S(1)} %add.3), channel_id=1, source_target_pairs={{0,16},{8,24},{16,0},{24,8},{1,17},{9,25},{17,1},{25,9},{2,18},{10... | collective-permute-start | bytes 786440 | tf_op jit(solution)/shard_map/ppermute | solution.py:629
  86.3 16.6 %collective-permute-start.27 = (bf16[128,1024]{1,0:T(8,128)(2,1)S(1)}, bf16[128,1024]{1,0:T(8,128)(2,1)S(1)}, u32[]{:S(2)}, u32[]{:S(2)}) collective-permute-start(bf16[128,1024]{1,0:T(8,128)(2,1)S(1)} %get-tuple-element.296), channel_id=1, source_target_pairs={{0,8},{8,0},{16,24},{24,16},{1,9},{9,1},{17,25},{25,17},{2,10},{10... | collective-permute-start | bytes 786440 | tf_op jit(solution)/shard_map/ppermute | solution.py:629
